TPU v7x, 256 devices: a whole 4x4x8 slice. The times are simulated.
256 devices in a mesh: section: 2 (over core), stream: 16 (over x, y), slab: 8 (over z).
Axes of the slice: x: 4, y: 4, z: 8, core: 2. Of those that a mesh axis runs over, the one named last changes fastest.
Arguments:
- state: float32 [2, 4, 256, 128, 128], P('section', None, 'stream', 'slab'), may hold values from -6 to 6
- source_mask: int32 [16, 8], P(None, 'slab'), may hold values 0 or 1
- deriv_x: float32 [256, 256], replicated, may hold values from -0.28125 to 0.28125
- deriv_z: float32 [128, 128], replicated, may hold values from -0.397747564 to 0.397747564
- filter_x: float32 [256, 256], replicated, may hold values from -0.375 to 0.375
- filter_z: float32 [128, 128], replicated, may hold values from -0.5 to 0.5
Outputs:
- advanced: float32 [2, 4, 256, 128, 128], P('section', None, 'stream', 'slab')
All inputs are finite; a program needn't handle non-finite values. No bound on the sum of `source_mask` on one device may be relied on, other than what follows from the above.
Results may differ from a plain program's by a relative error of at most 0.0001.
Values sent between devices are 32-bit elements; how exact they have to be, the bound alone decides.
No kernel may reach another device: no remote copies, remote signals or barrier semaphores. Data moves between devices by JAX's collectives and lax.ppermute only.
A program may use at most 64 MiB of HBM per device.

v0:
```python
import jax
import jax.numpy as jnp
from jax import lax
from jax.sharding import PartitionSpec as P

SEGMENTS = 8
MBLK = 16


mach_number = 0.5
time_step = 0.05
filter_weight = 0.25


def shifted_2(value, axis, steps):
    count = lax.axis_size(axis)
    leading, last = (max(0, -steps), min(count, count - steps))
    return lax.ppermute(value, axis, [(source, source + steps) for source in range(leading, last)])


def with_halo(cells, sides, width):
    for axis, dim in sides:
        count = lax.axis_size(axis)
        ends = count - 1
        head = lax.slice_in_dim(cells, 0, width, axis=dim)
        tail = lax.slice_in_dim(cells, cells.shape[dim] - width, cells.shape[dim], axis=dim)
        cells = jnp.concatenate(
            [
                lax.ppermute(tail, axis, [(i, (i + 1) % count) for i in range(ends)]),
                cells,
                lax.ppermute(head, axis, [((i + 1) % count, i) for i in range(ends)]),
            ],
            axis=dim,
        )
    return cells


def along_x(matrix, fields):
    return jnp.einsum("ij,fjyz->fiyz", matrix, fields, precision=lax.Precision.HIGHEST)


def along_z(matrix, fields):
    return jnp.einsum("fxyz,kz->fxyk", fields, matrix, precision=lax.Precision.HIGHEST)


def padded_slope(padded_one, which_dim):
    upper_cut = [slice(1, -1), slice(1, -1), slice(1, -1)]
    lower_cut = [slice(1, -1), slice(1, -1), slice(1, -1)]
    upper_cut[which_dim] = slice(2, None)
    lower_cut[which_dim] = slice(None, -2)
    return 0.5 * (padded_one[tuple(upper_cut)] - padded_one[tuple(lower_cut)])


def lamb_padded(padded, order):
    dim_x, dim_y, dim_z = order
    speed_x, speed_y, speed_z = (padded[0], padded[1], padded[2])
    center_x = speed_x[1:-1, 1:-1, 1:-1]
    center_y = speed_y[1:-1, 1:-1, 1:-1]
    center_z = speed_z[1:-1, 1:-1, 1:-1]
    vortex_x = padded_slope(speed_z, dim_y) - padded_slope(speed_y, dim_z)
    vortex_y = padded_slope(speed_x, dim_z) - padded_slope(speed_z, dim_x)
    vortex_z = padded_slope(speed_y, dim_x) - padded_slope(speed_x, dim_y)
    return jnp.stack(
        [
            vortex_y * center_z - vortex_z * center_y,
            vortex_z * center_x - vortex_x * center_z,
            vortex_x * center_y - vortex_y * center_x,
        ]
    )


def exchange_source(region_cells, padded, order):
    own_source = -region_cells * lamb_padded(padded, order)
    return shifted_2(own_source, "section", 1)


def slope_in_y(fields):
    padded = with_halo(fields, (("slab", 2),), 2)
    length = fields.shape[2]

    def shifted(offset):
        return lax.slice_in_dim(padded, 2 + offset, 2 + offset + length, axis=2)

    return (8.0 * (shifted(1) - shifted(-1)) - (shifted(2) - shifted(-2))) / 12.0


def tendency(slope_x, slope_y, slope_z, forcing):
    press_rate = -mach_number * slope_x[0] - slope_x[1] - slope_y[1] - slope_z[1]
    axial_rate = -mach_number * slope_x[1] - slope_x[0] + forcing[0]
    normal_rate = -mach_number * slope_x[2] - slope_y[0] + forcing[1]
    third_rate = -mach_number * slope_x[3] - slope_z[0] + forcing[2]
    return jnp.stack([press_rate, axial_rate, normal_rate, third_rate])


def block_x(matrix, fields):
    return lax.all_to_all(
        along_x(matrix, lax.all_to_all(fields, "stream", split_axis=2, concat_axis=1, tiled=True)),
        "stream",
        split_axis=1,
        concat_axis=2,
        tiled=True,
    )


def shards(state, source_mask, deriv_x, deriv_z, filter_x, filter_z):
    fields = state[0]
    blocks = source_mask.astype(jnp.float32)
    block_rows = blocks.shape[0]
    block_cols = blocks.shape[1]
    region = jnp.broadcast_to(blocks[:, None, :, None], (block_rows, MBLK, block_cols, MBLK))
    region = region.reshape(block_rows * MBLK, block_cols * MBLK)
    forcing = None
    width_x = fields.shape[1]
    region = lax.dynamic_slice_in_dim(region, lax.axis_index("stream") * width_x, width_x, 0)
    region_cells = region[None, :, :, None]
    for segment_index in range(SEGMENTS):
        if segment_index % 2 == 0:
            padded = with_halo(fields[1:4], (("stream", 1), ("slab", 2)), 1)
            padded = jnp.pad(padded, ((0, 0), (0, 0), (0, 0), (1, 1)))
            forcing = exchange_source(region_cells, padded, (0, 1, 2))
        slope_x = block_x(deriv_x, fields)
        slope_y = slope_in_y(jnp.stack([fields[0], fields[2]]))
        slope_z = along_z(deriv_z, jnp.stack([fields[0], fields[3]]))
        fields = fields + time_step * tendency(slope_x, slope_y, slope_z, forcing)
    result = (
        fields
        + filter_weight * block_x(filter_x, fields)
        + filter_weight * along_z(filter_z, fields)
    )
    return result[None]


def solution(mesh):
    placed = (P("section", None, "stream", "slab", None), P(None, "slab"), P(), P(), P(), P())
    return jax.shard_map(
        shards,
        mesh=mesh,
        in_specs=placed,
        out_specs=P("section", None, "stream", "slab", None),
        check_vma=False,
    )
```

profile of v0, /device:TPU:96, one launch (start us, length us, event | category | flops | bytes accessed | tf_op | source)
XLA Modules:
  0.0 402.9 jit_solution(13201326228273239943)
XLA Ops:
  15.1 8.1 %all-to-all-start = ((f32[4,16,16,128]{3,1,0,2:T(8,128)}), f32[4,16,16,128]{3,1,0,2:T(8,128)S(1)}, u32[]{:S(2)}, u32[]{:S(2)}) async-start(f32[4,16,16,128]{3,1,0,2:T(8,128)} %copy.45), calls=%async_computation | async-start | bytes 1048576 | tf_op jit(solution)/shard_map/all_to_all | solution.py:97
  39.3 7.2 %all-to-all-start.1 = ((f32[4,256,1,128]{3,0,2,1:T(4,128)}), f32[4,256,1,128]{3,0,2,1:T(4,128)S(1)}, u32[]{:S(2)}, u32[]{:S(2)}) async-start(f32[4,256,1,128]{3,0,2,1:T(4,128)} %copy.48), calls=%async_computation.1 | async-start | bytes 1048576 | tf_op jit(solution)/shard_map/all_to_all | solution.py:96
  47.1 9.5 %all-to-all-done.1 = f32[4,256,1,128]{3,0,2,1:T(4,128)S(1)} async-done(((f32[4,256,1,128]{3,0,2,1:T(4,128)}), f32[4,256,1,128]{3,0,2,1:T(4,128)S(1)}, u32[]{:S(2)}, u32[]{:S(2)}) %all-to-all-start.1) | async-done | bytes 524320 | tf_op jit(solution)/shard_map/all_to_all | solution.py:96
  78.6 9.5 %all-to-all-done.3 = f32[4,256,1,128]{3,0,2,1:T(4,128)S(1)} async-done(((f32[4,256,1,128]{3,0,2,1:T(4,128)}), f32[4,256,1,128]{3,0,2,1:T(4,128)S(1)}, u32[]{:S(2)}, u32[]{:S(2)}) %all-to-all-start.3) | async-done | bytes 524320 | tf_op jit(solution)/shard_map/all_to_all | solution.py:96
  93.4 6.7 %all-to-all-start.4 = ((f32[4,16,16,128]{3,1,0,2:T(8,128)}), f32[4,16,16,128]{3,1,0,2:T(8,128)S(1)}, u32[]{:S(2)}, u32[]{:S(2)}) async-start(f32[4,16,16,128]{3,1,0,2:T(8,128)} %copy.57), calls=%async_computation.4 | async-start | bytes 1048576 | tf_op jit(solution)/shard_map/all_to_all | solution.py:97
  119.8 7.2 %all-to-all-start.5 = ((f32[4,256,1,128]{3,0,2,1:T(4,128)}), f32[4,256,1,128]{3,0,2,1:T(4,128)S(1)}, u32[]{:S(2)}, u32[]{:S(2)}) async-start(f32[4,256,1,128]{3,0,2,1:T(4,128)} %copy.60), calls=%async_computation.5 | async-start | bytes 1048576 | tf_op jit(solution)/shard_map/all_to_all | solution.py:96
  127.6 9.5 %all-to-all-done.5 = f32[4,256,1,128]{3,0,2,1:T(4,128)S(1)} async-done(((f32[4,256,1,128]{3,0,2,1:T(4,128)}), f32[4,256,1,128]{3,0,2,1:T(4,128)S(1)}, u32[]{:S(2)}, u32[]{:S(2)}) %all-to-all-start.5) | async-done | bytes 524320 | tf_op jit(solution)/shard_map/all_to_all | solution.py:96
  155.1 5.6 %all-to-all-start.7 = ((f32[4,256,1,128]{3,0,2,1:T(4,128)}), f32[4,256,1,128]{3,0,2,1:T(4,128)S(1)}, u32[]{:S(2)}, u32[]{:S(2)}) async-start(f32[4,256,1,128]{3,0,2,1:T(4,128)} %copy.66), calls=%async_computation.7 | async-start | bytes 1048576 | tf_op jit(solution)/shard_map/all_to_all | solution.py:96
  163.6 7.1 %all-to-all-done.7 = f32[4,256,1,128]{3,0,2,1:T(4,128)S(1)} async-done(((f32[4,256,1,128]{3,0,2,1:T(4,128)}), f32[4,256,1,128]{3,0,2,1:T(4,128)S(1)}, u32[]{:S(2)}, u32[]{:S(2)}) %all-to-all-start.7) | async-done | bytes 524320 | tf_op jit(solution)/shard_map/all_to_all | solution.py:96
  178.6 6.7 %all-to-all-start.8 = ((f32[4,16,16,128]{3,1,0,2:T(8,128)}), f32[4,16,16,128]{3,1,0,2:T(8,128)}, u32[]{:S(2)}, u32[]{:S(2)}) async-start(f32[4,16,16,128]{3,1,0,2:T(8,128)} %copy.69), calls=%async_computation.8 | async-start | bytes 1048576 | tf_op jit(solution)/shard_map/all_to_all | solution.py:97
  194.7 5.1 %collective-permute-start.19 = (f32[2,16,2,128]{3,2,1,0:T(2,128)}, f32[2,16,2,128]{3,2,1,0:T(2,128)}, u32[]{:S(2)}, u32[]{:S(2)}) collective-permute-start(f32[2,16,2,128]{3,2,1,0:T(2,128)} %get-tuple-element.124), channel_id=1, source_target_pairs={{0,1},{1,2},{2,3},{3,4},{4,5},{5,6},{6,7},{8,9},{9,10},{10,11},{11... | collective-permute-start | bytes 98312 | tf_op jit(solution)/shard_map/ppermute | solution.py:29
  207.6 7.2 %all-to-all-start.9 = ((f32[4,256,1,128]{3,0,2,1:T(4,128)}), f32[4,256,1,128]{3,0,2,1:T(4,128)S(1)}, u32[]{:S(2)}, u32[]{:S(2)}) async-start(f32[4,256,1,128]{3,0,2,1:T(4,128)} %copy.72), calls=%async_computation.9 | async-start | bytes 1048576 | tf_op jit(solution)/shard_map/all_to_all | solution.py:96
  218.9 8.8 %all-to-all-done.9 = f32[4,256,1,128]{3,0,2,1:T(4,128)S(1)} async-done(((f32[4,256,1,128]{3,0,2,1:T(4,128)}), f32[4,256,1,128]{3,0,2,1:T(4,128)S(1)}, u32[]{:S(2)}, u32[]{:S(2)}) %all-to-all-start.9) | async-done | bytes 524320 | tf_op jit(solution)/shard_map/all_to_all | solution.py:96
  239.3 15.3 %collective-permute-start.26 = (f32[2,16,2,128]{3,2,1,0:T(2,128)}, f32[2,16,2,128]{3,2,1,0:T(2,128)S(1)}, u32[]{:S(2)}, u32[]{:S(2)}) collective-permute-start(f32[2,16,2,128]{3,2,1,0:T(2,128)} %get-tuple-element.120), channel_id=1, source_target_pairs={{0,1},{1,2},{2,3},{3,4},{4,5},{5,6},{6,7},{8,9},{9,10},{10,11},{11... | collective-permute-start | bytes 98312 | tf_op jit(solution)/shard_map/ppermute | solution.py:29
  257.7 7.1 %all-to-all-start.11 = ((f32[4,256,1,128]{3,0,2,1:T(4,128)}), f32[4,256,1,128]{3,0,2,1:T(4,128)S(1)}, u32[]{:S(2)}, u32[]{:S(2)}) async-start(f32[4,256,1,128]{3,0,2,1:T(4,128)} %copy.78), calls=%async_computation.11 | async-start | bytes 1048576 | tf_op jit(solution)/shard_map/all_to_all | solution.py:96
  268.9 6.1 %all-to-all-done.11 = f32[4,256,1,128]{3,0,2,1:T(4,128)S(1)} async-done(((f32[4,256,1,128]{3,0,2,1:T(4,128)}), f32[4,256,1,128]{3,0,2,1:T(4,128)S(1)}, u32[]{:S(2)}, u32[]{:S(2)}) %all-to-all-start.11) | async-done | bytes 524320 | tf_op jit(solution)/shard_map/all_to_all | solution.py:96
  283.6 7.4 %all-to-all-start.12 = ((f32[4,16,16,128]{3,1,0,2:T(8,128)}), f32[4,16,16,128]{3,1,0,2:T(8,128)}, u32[]{:S(2)}, u32[]{:S(2)}) async-start(f32[4,16,16,128]{3,1,0,2:T(8,128)} %copy.81), calls=%async_computation.12 | async-start | bytes 1048576 | tf_op jit(solution)/shard_map/all_to_all | solution.py:97
  300.4 5.1 %collective-permute-start.28 = (f32[2,16,2,128]{3,2,1,0:T(2,128)}, f32[2,16,2,128]{3,2,1,0:T(2,128)}, u32[]{:S(2)}, u32[]{:S(2)}) collective-permute-start(f32[2,16,2,128]{3,2,1,0:T(2,128)} %get-tuple-element.116), channel_id=1, source_target_pairs={{0,1},{1,2},{2,3},{3,4},{4,5},{5,6},{6,7},{8,9},{9,10},{10,11},{11... | collective-permute-start | bytes 98312 | tf_op jit(solution)/shard_map/ppermute | solution.py:29
  313.3 7.2 %all-to-all-start.13 = ((f32[4,256,1,128]{3,0,2,1:T(4,128)}), f32[4,256,1,128]{3,0,2,1:T(4,128)S(1)}, u32[]{:S(2)}, u32[]{:S(2)}) async-start(f32[4,256,1,128]{3,0,2,1:T(4,128)} %copy.84), calls=%async_computation.13 | async-start | bytes 1048576 | tf_op jit(solution)/shard_map/all_to_all | solution.py:96
  324.5 8.8 %all-to-all-done.13 = f32[4,256,1,128]{3,0,2,1:T(4,128)S(1)} async-done(((f32[4,256,1,128]{3,0,2,1:T(4,128)}), f32[4,256,1,128]{3,0,2,1:T(4,128)S(1)}, u32[]{:S(2)}, u32[]{:S(2)}) %all-to-all-start.13) | async-done | bytes 524320 | tf_op jit(solution)/shard_map/all_to_all | solution.py:96
  355.2 5.1 %all-to-all-start.15 = ((f32[4,256,1,128]{3,0,2,1:T(4,128)}), f32[4,256,1,128]{3,0,2,1:T(4,128)S(1)}, u32[]{:S(2)}, u32[]{:S(2)}) async-start(f32[4,256,1,128]{3,0,2,1:T(4,128)} %copy.90), calls=%async_computation.15 | async-start | bytes 1048576 | tf_op jit(solution)/shard_map/all_to_all | solution.py:96
  364.5 6.0 %all-to-all-done.15 = f32[4,256,1,128]{3,0,2,1:T(4,128)S(1)} async-done(((f32[4,256,1,128]{3,0,2,1:T(4,128)}), f32[4,256,1,128]{3,0,2,1:T(4,128)S(1)}, u32[]{:S(2)}, u32[]{:S(2)}) %all-to-all-start.15) | async-done | bytes 524320 | tf_op jit(solution)/shard_map/all_to_all | solution.py:96
  373.2 13.3 %all_to_all.264 = f32[4,16,16,128]{3,1,0,2:T(8,128)S(1)} all-to-all(f32[4,16,16,128]{3,1,0,2:T(8,128)S(1)} %copy.93), channel_id=1, replica_groups=mesh['section'=2,'stream'=16,'slab'=8] {'stream'}, dimensions={2} | all-to-all | bytes 1048576 | tf_op jit(solution)/shard_map/all_to_all | solution.py:97
  387.9 13.3 %all_to_all.265 = f32[4,256,1,128]{3,0,2,1:T(4,128)S(1)} all-to-all(f32[4,256,1,128]{3,0,2,1:T(4,128)S(1)} %copy.96), channel_id=1, replica_groups=mesh['section'=2,'stream'=16,'slab'=8] {'stream'}, dimensions={1} | all-to-all | bytes 1048576 | tf_op jit(solution)/shard_map/all_to_all | solution.py:96
  (338 shorter events, 207.7 us)
Async XLA Ops:
  1.1 22.2 %collective-permute-start.2 = (f32[3,1,16,128]{3,2,1,0:T(8,128)S(1)}, f32[3,1,16,128]{3,2,1,0:T(8,128)S(1)}, u32[]{:S(2)}, u32[]{:S(2)}) collective-permute-start(f32[3,1,16,128]{3,2,1,0:T(8,128)S(1)} %get-tuple-element.107), channel_id=1, source_target_pairs={{0,8},{8,16},{16,24},{24,32},{32,40},{40,48},{48,56},{56,64},{64,7... | collective-permute-start | bytes 73736 | tf_op jit(solution)/shard_map/ppermute | solution.py:29
  4.6 18.7 %collective-permute-start.3 = (f32[3,1,16,128]{3,2,1,0:T(8,128)S(1)}, f32[3,1,16,128]{3,2,1,0:T(8,128)S(1)}, u32[]{:S(2)}, u32[]{:S(2)}) collective-permute-start(f32[3,1,16,128]{3,2,1,0:T(8,128)S(1)} %get-tuple-element.108), channel_id=1, source_target_pairs={{8,0},{16,8},{24,16},{32,24},{40,32},{48,40},{56,48},{64,56},{72,6... | collective-permute-start | bytes 73736 | tf_op jit(solution)/shard_map/ppermute | solution.py:31
  7.0 39.9 %collective-permute-start = (f32[2,16,2,128]{3,2,1,0:T(2,128)S(1)}, f32[2,16,2,128]{3,2,1,0:T(2,128)S(1)}, u32[]{:S(2)}, u32[]{:S(2)}) collective-permute-start(f32[2,16,2,128]{3,2,1,0:T(2,128)S(1)} %get-tuple-element.139), channel_id=1, source_target_pairs={{1,0},{2,1},{3,2},{4,3},{5,4},{6,5},{7,6},{9,8},{10,9},{11,10},{12... | collective-permute-start | bytes 98312 | tf_op jit(solution)/shard_map/ppermute | solution.py:31
  9.0 37.9 %collective-permute-start.1 = (f32[2,16,2,128]{3,2,1,0:T(2,128)S(1)}, f32[2,16,2,128]{3,2,1,0:T(2,128)S(1)}, u32[]{:S(2)}, u32[]{:S(2)}) collective-permute-start(f32[2,16,2,128]{3,2,1,0:T(2,128)S(1)} %get-tuple-element.140), channel_id=1, source_target_pairs={{0,1},{1,2},{2,3},{3,4},{4,5},{5,6},{6,7},{8,9},{9,10},{10,11},{11... | collective-permute-start | bytes 98312 | tf_op jit(solution)/shard_map/ppermute | solution.py:29
  15.1 22.1 %all-to-all-start = ((f32[4,16,16,128]{3,1,0,2:T(8,128)}), f32[4,16,16,128]{3,1,0,2:T(8,128)S(1)}, u32[]{:S(2)}, u32[]{:S(2)}) async-start(f32[4,16,16,128]{3,1,0,2:T(8,128)} %copy.45), calls=%async_computation | async-start | bytes 1048576 | tf_op jit(solution)/shard_map/all_to_all | solution.py:97
  35.9 21.0 %collective-permute-start.6 = (f32[3,16,16,128]{3,2,1,0:T(8,128)S(1)}, f32[3,16,16,128]{3,2,1,0:T(8,128)S(1)}, u32[]{:S(2)}, u32[]{:S(2)}) collective-permute-start(f32[3,16,16,128]{3,2,1,0:T(8,128)S(1)} %maximum_multiply_fusion.8), channel_id=1, source_target_pairs={{0,128},{1,129},{2,130},{3,131},{4,132},{5,133},{6,134},{7,135},{8... | collective-permute-start | bytes 1179656 | tf_op jit(solution)/shard_map/ppermute | solution.py:18
  93.4 24.3 %all-to-all-start.4 = ((f32[4,16,16,128]{3,1,0,2:T(8,128)}), f32[4,16,16,128]{3,1,0,2:T(8,128)S(1)}, u32[]{:S(2)}, u32[]{:S(2)}) async-start(f32[4,16,16,128]{3,1,0,2:T(8,128)} %copy.57), calls=%async_computation.4 | async-start | bytes 1048576 | tf_op jit(solution)/shard_map/all_to_all | solution.py:97
  106.7 20.7 %collective-permute-start.9 = (f32[2,16,2,128]{3,2,1,0:T(2,128)}, f32[2,16,2,128]{3,2,1,0:T(2,128)S(1)}, u32[]{:S(2)}, u32[]{:S(2)}) collective-permute-start(f32[2,16,2,128]{3,2,1,0:T(2,128)} %get-tuple-element.131), channel_id=1, source_target_pairs={{1,0},{2,1},{3,2},{4,3},{5,4},{6,5},{7,6},{9,8},{10,9},{11,10},{12... | collective-permute-start | bytes 98312 | tf_op jit(solution)/shard_map/ppermute | solution.py:31
  108.6 18.8 %collective-permute-start.10 = (f32[2,16,2,128]{3,2,1,0:T(2,128)}, f32[2,16,2,128]{3,2,1,0:T(2,128)S(1)}, u32[]{:S(2)}, u32[]{:S(2)}) collective-permute-start(f32[2,16,2,128]{3,2,1,0:T(2,128)} %get-tuple-element.132), channel_id=1, source_target_pairs={{0,1},{1,2},{2,3},{3,4},{4,5},{5,6},{6,7},{8,9},{9,10},{10,11},{11... | collective-permute-start | bytes 98312 | tf_op jit(solution)/shard_map/ppermute | solution.py:29
  116.1 21.3 %collective-permute-start.15 = (f32[3,16,16,128]{3,2,1,0:T(8,128)}, f32[3,16,16,128]{3,2,1,0:T(8,128)S(1)}, u32[]{:S(2)}, u32[]{:S(2)}) collective-permute-start(f32[3,16,16,128]{3,2,1,0:T(8,128)} %maximum_multiply_fusion.9), channel_id=1, source_target_pairs={{0,128},{1,129},{2,130},{3,131},{4,132},{5,133},{6,134},{7,135},{8... | collective-permute-start | bytes 1179656 | tf_op jit(solution)/shard_map/ppermute | solution.py:18
  178.6 26.0 %all-to-all-start.8 = ((f32[4,16,16,128]{3,1,0,2:T(8,128)}), f32[4,16,16,128]{3,1,0,2:T(8,128)}, u32[]{:S(2)}, u32[]{:S(2)}) async-start(f32[4,16,16,128]{3,1,0,2:T(8,128)} %copy.69), calls=%async_computation.8 | async-start | bytes 1048576 | tf_op jit(solution)/shard_map/all_to_all | solution.py:97
  192.8 24.1 %collective-permute-start.18 = (f32[2,16,2,128]{3,2,1,0:T(2,128)}, f32[2,16,2,128]{3,2,1,0:T(2,128)S(1)}, u32[]{:S(2)}, u32[]{:S(2)}) collective-permute-start(f32[2,16,2,128]{3,2,1,0:T(2,128)} %get-tuple-element.123), channel_id=1, source_target_pairs={{1,0},{2,1},{3,2},{4,3},{5,4},{6,5},{7,6},{9,8},{10,9},{11,10},{12... | collective-permute-start | bytes 98312 | tf_op jit(solution)/shard_map/ppermute | solution.py:31
  194.7 22.2 %collective-permute-start.19 = (f32[2,16,2,128]{3,2,1,0:T(2,128)}, f32[2,16,2,128]{3,2,1,0:T(2,128)}, u32[]{:S(2)}, u32[]{:S(2)}) collective-permute-start(f32[2,16,2,128]{3,2,1,0:T(2,128)} %get-tuple-element.124), channel_id=1, source_target_pairs={{0,1},{1,2},{2,3},{3,4},{4,5},{5,6},{6,7},{8,9},{9,10},{10,11},{11... | collective-permute-start | bytes 98312 | tf_op jit(solution)/shard_map/ppermute | solution.py:29
  202.5 25.5 %collective-permute-start.24 = (f32[3,16,16,128]{3,2,1,0:T(8,128)}, f32[3,16,16,128]{3,2,1,0:T(8,128)}, u32[]{:S(2)}, u32[]{:S(2)}) collective-permute-start(f32[3,16,16,128]{3,2,1,0:T(8,128)} %maximum_multiply_fusion.10), channel_id=1, source_target_pairs={{0,128},{1,129},{2,130},{3,131},{4,132},{5,133},{6,134},{7,135},{8... | collective-permute-start | bytes 1179656 | tf_op jit(solution)/shard_map/ppermute | solution.py:18
  207.6 20.0 %all-to-all-start.9 = ((f32[4,256,1,128]{3,0,2,1:T(4,128)}), f32[4,256,1,128]{3,0,2,1:T(4,128)S(1)}, u32[]{:S(2)}, u32[]{:S(2)}) async-start(f32[4,256,1,128]{3,0,2,1:T(4,128)} %copy.72), calls=%async_computation.9 | async-start | bytes 1048576 | tf_op jit(solution)/shard_map/all_to_all | solution.py:96
  231.1 23.5 %all-to-all-start.10 = ((f32[4,16,16,128]{3,1,0,2:T(8,128)}), f32[4,16,16,128]{3,1,0,2:T(8,128)}, u32[]{:S(2)}, u32[]{:S(2)}) async-start(f32[4,16,16,128]{3,1,0,2:T(8,128)} %copy.75), calls=%async_computation.10 | async-start | bytes 1048576 | tf_op jit(solution)/shard_map/all_to_all | solution.py:97
  237.3 29.5 %collective-permute-start.25 = (f32[2,16,2,128]{3,2,1,0:T(2,128)}, f32[2,16,2,128]{3,2,1,0:T(2,128)S(1)}, u32[]{:S(2)}, u32[]{:S(2)}) collective-permute-start(f32[2,16,2,128]{3,2,1,0:T(2,128)} %get-tuple-element.119), channel_id=1, source_target_pairs={{1,0},{2,1},{3,2},{4,3},{5,4},{6,5},{7,6},{9,8},{10,9},{11,10},{12... | collective-permute-start | bytes 98312 | tf_op jit(solution)/shard_map/ppermute | solution.py:31
  239.3 27.6 %collective-permute-start.26 = (f32[2,16,2,128]{3,2,1,0:T(2,128)}, f32[2,16,2,128]{3,2,1,0:T(2,128)S(1)}, u32[]{:S(2)}, u32[]{:S(2)}) collective-permute-start(f32[2,16,2,128]{3,2,1,0:T(2,128)} %get-tuple-element.120), channel_id=1, source_target_pairs={{0,1},{1,2},{2,3},{3,4},{4,5},{5,6},{6,7},{8,9},{9,10},{10,11},{11... | collective-permute-start | bytes 98312 | tf_op jit(solution)/shard_map/ppermute | solution.py:29
  283.6 26.7 %all-to-all-start.12 = ((f32[4,16,16,128]{3,1,0,2:T(8,128)}), f32[4,16,16,128]{3,1,0,2:T(8,128)}, u32[]{:S(2)}, u32[]{:S(2)}) async-start(f32[4,16,16,128]{3,1,0,2:T(8,128)} %copy.81), calls=%async_computation.12 | async-start | bytes 1048576 | tf_op jit(solution)/shard_map/all_to_all | solution.py:97
  298.5 24.1 %collective-permute-start.27 = (f32[2,16,2,128]{3,2,1,0:T(2,128)}, f32[2,16,2,128]{3,2,1,0:T(2,128)S(1)}, u32[]{:S(2)}, u32[]{:S(2)}) collective-permute-start(f32[2,16,2,128]{3,2,1,0:T(2,128)} %get-tuple-element.115), channel_id=1, source_target_pairs={{1,0},{2,1},{3,2},{4,3},{5,4},{6,5},{7,6},{9,8},{10,9},{11,10},{12... | collective-permute-start | bytes 98312 | tf_op jit(solution)/shard_map/ppermute | solution.py:31
  300.4 22.2 %collective-permute-start.28 = (f32[2,16,2,128]{3,2,1,0:T(2,128)}, f32[2,16,2,128]{3,2,1,0:T(2,128)}, u32[]{:S(2)}, u32[]{:S(2)}) collective-permute-start(f32[2,16,2,128]{3,2,1,0:T(2,128)} %get-tuple-element.116), channel_id=1, source_target_pairs={{0,1},{1,2},{2,3},{3,4},{4,5},{5,6},{6,7},{8,9},{9,10},{10,11},{11... | collective-permute-start | bytes 98312 | tf_op jit(solution)/shard_map/ppermute | solution.py:29
  308.2 25.6 %collective-permute-start.33 = (f32[3,16,16,128]{3,2,1,0:T(8,128)}, f32[3,16,16,128]{3,2,1,0:T(8,128)}, u32[]{:S(2)}, u32[]{:S(2)}) collective-permute-start(f32[3,16,16,128]{3,2,1,0:T(8,128)} %maximum_multiply_fusion.11), channel_id=1, source_target_pairs={{0,128},{1,129},{2,130},{3,131},{4,132},{5,133},{6,134},{7,135},{8... | collective-permute-start | bytes 1179656 | tf_op jit(solution)/shard_map/ppermute | solution.py:18
  313.3 20.0 %all-to-all-start.13 = ((f32[4,256,1,128]{3,0,2,1:T(4,128)}), f32[4,256,1,128]{3,0,2,1:T(4,128)S(1)}, u32[]{:S(2)}, u32[]{:S(2)}) async-start(f32[4,256,1,128]{3,0,2,1:T(4,128)} %copy.84), calls=%async_computation.13 | async-start | bytes 1048576 | tf_op jit(solution)/shard_map/all_to_all | solution.py:96
  343.1 19.4 %collective-permute-start.34 = (f32[2,16,2,128]{3,2,1,0:T(2,128)}, f32[2,16,2,128]{3,2,1,0:T(2,128)S(1)}, u32[]{:S(2)}, u32[]{:S(2)}) collective-permute-start(f32[2,16,2,128]{3,2,1,0:T(2,128)} %get-tuple-element.111), channel_id=1, source_target_pairs={{1,0},{2,1},{3,2},{4,3},{5,4},{6,5},{7,6},{9,8},{10,9},{11,10},{12... | collective-permute-start | bytes 98312 | tf_op jit(solution)/shard_map/ppermute | solution.py:31
  (85 other events, 686.6 us)
where the time goes:
time: 409 us; the launch traced here: 403 us
  starting transfers between devices  208 us (51%)
  waiting for transfers between devices  76.9 us (19%)
  local copies, waits for them, and re-layouts  34.5 us (8%)
  other arithmetic  32.5 us (8%)
  blocking collectives  26.7 us (7%)
  matrix products  22 us (5%)
    ppermute x16, starting transfers between devices, with_halo(): lax.ppermute(tail, axis, [(i, (i + 1) % count) for i in range(ends)])  71.6 us
    all_to_all x8, waiting for transfers between devices, block_x(): lax.all_to_all(along_x(matrix, lax.all_to_all(fields, 'stream', split_axi...  65.4 us
    all_to_all x8, starting transfers between devices, block_x(): lax.all_to_all(along_x(matrix, lax.all_to_all(fields, 'stream', split_axi...  50.8 us
    all_to_all x8, starting transfers between devices, block_x(): lax.all_to_all(fields, 'stream', split_axis=2, concat_axis=1, tiled=True)  44.6 us
    ppermute x16, starting transfers between devices, with_halo(): lax.ppermute(head, axis, [((i + 1) % count, i) for i in range(ends)])  34.3 us
    all_to_all x1, blocking collectives, block_x(): lax.all_to_all(fields, 'stream', split_axis=2, concat_axis=1, tiled=True)  13.3 us
    all_to_all x1, blocking collectives, block_x(): lax.all_to_all(along_x(matrix, lax.all_to_all(fields, 'stream', split_axi...  13.3 us
    dot_general x9, matrix products, along_z(): jnp.einsum('fxyz,kz->fxyk', fields, matrix, precision=lax.Precision.HIGHEST)  12.9 us
  transfers between devices with their start and end apart: 52, of which 12 were waited for; matrix products, arithmetic and copies ran while one was open for 16% of the time, Pallas kernels for 0%

commit v1 on v0

v1 whole, which is shorter than its diff:
```python
import functools

import jax
import jax.numpy as jnp
from jax import lax
from jax.experimental import pallas as pl
from jax.experimental.pallas import tpu as pltpu
from jax.sharding import PartitionSpec as P

mach_number = 0.5
tau = 0.05
filter_weight = 0.25
REACH = 10
OUT_P, OUT_U, OUT_V, OUT_W = 14, 10, 12, 10
AXES = ("section", "stream", "slab")
LEFT = ("e1", "ta", "m1", "m2", "e2", "a", "e4", "e6", "e8", "fx")
RIGHT = ("c", "cc", "fz")
f32, bf16 = jnp.float32, jnp.bfloat16


def call(body, out_shape, *args, flops=0, scratch=()):
    moved = sum(a.size * a.dtype.itemsize for a in args)
    return pl.pallas_call(
        body,
        out_shape=out_shape,
        scratch_shapes=scratch,
        compiler_params=pltpu.CompilerParams(vmem_limit_bytes=40 * 2**20),
        cost_estimate=pl.CostEstimate(flops=flops, bytes_accessed=moved, transcendentals=0),
    )(*args)


def halves(value):
    high = value.astype(bf16)
    return high, (value - high.astype(f32)).astype(bf16)


def left_form(matrix):
    high, low = halves(matrix)
    return jnp.concatenate([high, high, low], axis=1)


def right_form(matrix):
    high, low = halves(matrix)
    return jnp.concatenate([high, high, low], axis=0)


def times_left(form, planes):
    high, low = halves(jnp.concatenate(planes, axis=1))
    out = jnp.dot(form, jnp.concatenate([high, low, high], axis=0), preferred_element_type=f32)
    width = planes[0].shape[1]
    return [out[:, i * width : (i + 1) * width] for i in range(len(planes))]


def times_right(planes, form):
    high, low = halves(jnp.concatenate(planes, axis=0))
    out = jnp.dot(jnp.concatenate([high, low, high], axis=1), form, preferred_element_type=f32)
    length = planes[0].shape[0]
    return [out[i * length : (i + 1) * length] for i in range(len(planes))]


def prepare_kernel(dx_ref, dzt_ref, fx_ref, fzt_ref, left_ref, right_ref):
    def dot(one, two):
        return jnp.dot(one, two, precision=lax.Precision.HIGHEST, preferred_element_type=f32)

    dx, dzt = dx_ref[...], dzt_ref[...]
    square = dot(dx, dx)
    e1 = -tau * mach_number * dx
    e2 = 2.0 * e1 + (tau * mach_number) ** 2 * square
    e4 = 2.0 * e2 + dot(e2, e2)
    values = {
        "e1": e1,
        "ta": -tau * dx,
        "m1": 2.0 * e1,
        "m2": tau**2 * square - e2,
        "e2": e2,
        "a": dx,
        "e4": e4,
        "e6": e2 + e4 + dot(e2, e4),
        "e8": 2.0 * e4 + dot(e4, e4),
        "fx": filter_weight * fx_ref[...],
    }
    for i, name in enumerate(LEFT):
        left_ref[i] = left_form(values[name])
    others = {"c": dzt, "cc": tau**2 * dot(dzt, dzt), "fz": filter_weight * fzt_ref[...]}
    for i, name in enumerate(RIGHT):
        right_ref[i] = right_form(others[name])


class Products:
    def __init__(self, left_ref, right_ref):
        self.left_ref, self.right_ref = left_ref, right_ref

    def left(self, name, planes):
        return times_left(self.left_ref[LEFT.index(name)], planes)

    def right(self, planes, name):
        return times_right(planes, self.right_ref[RIGHT.index(name)])


def inside(value, reach, low_ok, high_ok):
    rows = value.shape[0]
    return jnp.concatenate(
        [value[:reach] * low_ok, value[reach : rows - reach], value[rows - reach :] * high_ok], axis=0
    )


def shift_rows(value, steps):
    zeros = jnp.zeros((abs(steps),) + value.shape[1:], f32)
    if steps > 0:
        return jnp.concatenate([value[steps:], zeros], axis=0)
    return jnp.concatenate([zeros, value[:steps]], axis=0)


def slope4(value):
    near = shift_rows(value, 1) - shift_rows(value, -1)
    far = shift_rows(value, 2) - shift_rows(value, -2)
    return (2.0 / 3.0) * near - (1.0 / 12.0) * far


def spread_kernel(edge_ref, ext_ref, right_ref, out_ref):
    low_ok, high_ok = edge_ref[0], edge_ref[1]
    own = ext_ref.shape[1] - 2 * REACH
    rows, xs, nz = ext_ref.shape[1:]

    def twice(value):
        once = inside(slope4(value), REACH, low_ok, high_ok)
        return inside(slope4(once), REACH, low_ok, high_ok)

    def put(place, value):
        out_ref[:, place] = value[REACH : REACH + own]

    def slope2(ref_index):
        return 0.5 * (
            ext_ref[ref_index, REACH + 1 : REACH + 1 + own] - ext_ref[ref_index, REACH - 1 : REACH - 1 + own]
        )

    through = times_right([ext_ref[3].reshape(rows * xs, nz)], right_ref[RIGHT.index("c")])[0]
    rate = through.reshape(rows, xs, nz) + slope4(ext_ref[2])
    rate = inside(rate, REACH, low_ok, high_ok)
    for place, value in ((0, ext_ref[0]), (3, ext_ref[1]), (6, rate)):
        put(place, value)
        value = twice(value)
        put(place + 1, value)
        put(place + 2, twice(value))
    put(9, ext_ref[2])
    put(10, ext_ref[3])
    out_ref[:, 11] = slope2(1)
    out_ref[:, 12] = slope2(3)


def gather_kernel(edge_ref, back_ref, own_ref, high_ref, low_ref):
    low_ok, high_ok = edge_ref[0], edge_ref[1]
    own = back_ref.shape[0]
    lead = 0
    place = 0
    for output, (count, reach) in enumerate(((8, OUT_P), (6, OUT_U), (7, OUT_V), (6, OUT_W))):
        total = back_ref[:, lead + count - 1]
        for k in range(count - 2, -1, -1):
            edge = 2 * (count - 1 - k)
            zeros = jnp.zeros((2,) + total.shape[1:], f32)
            total = slope4(jnp.concatenate([zeros, total, zeros], axis=0))
            total = jnp.concatenate(
                [
                    total[:edge] * low_ok,
                    total[edge : edge + own] + back_ref[:, lead + k],
                    total[edge + own :] * high_ok,
                ],
                axis=0,
            )
        own_ref[output] = total[reach : reach + own]
        low_ref[place : place + reach] = total[:reach]
        high_ref[place : place + reach] = total[reach + own :]
        place += reach
        lead += count


def plane(ref, index):
    blocks, _, xs, nz = ref.shape
    return ref[:, index].reshape(blocks * xs, nz)


def waves_kernel(in_ref, left_ref, right_ref, out_ref):
    do = Products(left_ref, right_ref)
    p0 = [plane(in_ref, i) for i in range(3)]
    u0 = [plane(in_ref, 3 + i) for i in range(3)]

    def advance(now, before):
        count = len(before) - 1
        one = do.left("m1", now[:count])
        two = do.left("m2", before[:count])
        three = do.right(before[:count], "cc")
        return [
            2.0 * now[i] - before[i] + (one[i] + two[i] + three[i] + tau**2 * before[i + 1])
            for i in range(count)
        ]

    moved = do.left("e1", p0)
    driven = do.left("ta", u0)
    p1 = [p0[i] + (moved[i] + driven[i] - tau * plane(in_ref, 6 + i)) for i in range(3)]
    h2 = p0[0] + moved[0] + p1[0]
    out_ref[2] = h2
    p2 = advance(p1, p0)
    p3 = advance(p2, p1)
    h4 = h2 + do.left("e2", [h2])[0] + p2[0] + do.left("e1", p2[:1])[0] + p3[0]
    out_ref[3] = h4
    p4 = advance(p3, p2)
    p5 = advance(p4, p3)
    h6 = h4 + do.left("e2", [h4])[0] + p4[0] + do.left("e1", p4)[0] + p5[0]
    out_ref[0] = p4[0]
    out_ref[1] = p5[0]
    out_ref[4] = h6


def held_kernel(in_ref, waves_ref, left_ref, right_ref, out_ref):
    do = Products(left_ref, right_ref)
    start = [plane(in_ref, i) for i in (3, 10, 11, 12, 9)]
    h = [waves_ref[2 + n] for n in range(3)]
    pull_x = do.left("a", h)
    pull_z = do.right(h, "c")
    for n, growth in enumerate(("e2", "e4", "e6")):
        change = do.left(growth, start)
        out_ref[n, 0] = start[0] + change[0] - tau * pull_x[n]
        out_ref[n, 1] = start[1] + change[1] - tau * pull_z[n]
        for k in (2, 3, 4):
            out_ref[n, k] = start[k] + change[k]


def source_kernel(region_ref, in_ref, held_ref, up1_ref, down1_ref, up2_ref, down2_ref, left_ref, right_ref, out_ref):
    do = Products(left_ref, right_ref)
    nx, nz = up1_ref.shape[1:]
    row = lax.broadcasted_iota(jnp.int32, (nx, nz), 0)
    lane = lax.broadcasted_iota(jnp.int32, (nx, nz), 1)
    region = region_ref[...]

    def slope_x(value):
        ahead = jnp.where(row == nx - 1, 0.0, pltpu.roll(value, nx - 1, 0))
        behind = jnp.where(row == 0, 0.0, pltpu.roll(value, 1, 0))
        return 0.5 * (ahead - behind)

    def slope_z(value):
        ahead = jnp.where(lane == nz - 1, 0.0, pltpu.roll(value, nz - 1, 1))
        behind = jnp.where(lane == 0, 0.0, pltpu.roll(value, 1, 1))
        return 0.5 * (ahead - behind)

    near = [up1_ref[n] - down1_ref[n] for n in range(3)]
    half = [0.5 * value for value in near]
    pull_x = do.left("a", half)
    pull_z = do.right(half, "c")
    for n in range(4):
        if n == 0:
            u, w, slope_u, slope_w, v = [plane(in_ref, i) for i in (3, 10, 11, 12, 9)]
        else:
            u, w = held_ref[n - 1, 0], held_ref[n - 1, 1]
            slope_u = held_ref[n - 1, 2] - tau * pull_x[n - 1]
            slope_w = held_ref[n - 1, 3] - tau * pull_z[n - 1]
            far = up2_ref[n - 1] - down2_ref[n - 1]
            v = held_ref[n - 1, 4] - tau * ((2.0 / 3.0) * near[n - 1] - (1.0 / 12.0) * far)
        o_x = slope_w - slope_z(v)
        o_y = slope_z(u) - slope_x(w)
        o_z = slope_x(v) - slope_u
        out_ref[n, 0] = region * (o_z * v - o_y * w)
        out_ref[n, 1] = region * (o_x * w - o_z * u)
        out_ref[n, 2] = region * (o_y * u - o_x * v)


class Chain:
    def __init__(self, left_ref, right_ref):
        self.do = Products(left_ref, right_ref)

    def advance(self, now, before, drive, count):
        m_now = self.do.left("m1", now)
        m_before = self.do.left("m2", before)
        c_before = self.do.right(before, "cc")
        out = []
        for k in range(count):
            terms = []
            if k < len(now):
                terms.append(2.0 * now[k] + m_now[k])
            if k < len(before):
                terms.append(m_before[k] + c_before[k] - before[k])
            if 0 <= k - 2 < len(before):
                terms.append(tau**2 * before[k - 2])
            if k < len(drive):
                terms.append(drive[k])
            out.append(functools.reduce(lambda one, two: one + two, terms))
        return out

    def grow(self, sums, before, now):
        moved = self.do.left("e1", before)
        kept = self.do.left("e2", sums) if sums else []
        out = [before[k] + moved[k] + now[k] for k in range(len(now))]
        return [out[k] + (sums[k] + kept[k]) if k < len(sums) else out[k] for k in range(len(now))]


def drives(do, source_ref, first, last):
    one = do.left("a", [source_ref[n, 0] for n in range(first, last)])
    two = do.right([source_ref[n, 2] for n in range(first, last)], "c")
    return [
        (-(tau**2) * (one[n - first] + two[n - first]), -(tau**2) * source_ref[n, 1])
        for n in range(first, last)
    ]


def driven_kernel(waves_ref, source_ref, left_ref, right_ref, out_ref):
    chain = Chain(left_ref, right_ref)
    drive = drives(chain.do, source_ref, 0, 2)
    q2 = list(drive[0])
    moved = chain.do.left("m1", q2)
    q3 = [2.0 * q2[k] + moved[k] + drive[0][k] for k in range(2)]
    g4 = chain.grow([], q2, q3)
    q4 = chain.advance(q3, q2, drive[1], 4)
    q5 = chain.advance(q4, q3, drive[1], 4)
    g6 = chain.grow(g4, q4, q5)
    for first, values, wave in ((0, q4, 0), (4, q5, 1), (8, g6, 4)):
        out_ref[first] = values[0] + waves_ref[wave]
        for k in range(1, 4):
            out_ref[first + k] = values[k]


def finish_kernel(in_ref, driven_ref, source_ref, left_ref, right_ref, out_ref):
    chain = Chain(left_ref, right_ref)
    do = chain.do
    drive = drives(do, source_ref, 2, 4)
    q4, q5, g6 = [[driven_ref[first + k] for k in range(4)] for first in (0, 4, 8)]
    q6 = chain.advance(q5, q4, drive[0], 6)
    q7 = chain.advance(q6, q5, drive[0], 6)
    for k, value in enumerate(chain.grow(g6, q6, q7)):
        out_ref[8 + k] = value
    for k, value in enumerate(chain.advance(q7, q6, drive[1], 8)):
        out_ref[k] = value
    total = [source_ref[0, k] for k in range(3)]
    for n in (1, 2, 3):
        kept = do.left("e2", total)
        total = [total[k] + kept[k] + source_ref[n, k] for k in range(3)]
    moved = do.left("e1", total)
    begin = [plane(in_ref, i) for i in (3, 9, 10)]
    kept = do.left("e8", begin)
    for i in range(3):
        out_ref[14 + i] = begin[i] + kept[i] + tau * (2.0 * total[i] + moved[i])


def filter_kernel(last_ref, left_ref, right_ref, out_ref):
    do = Products(left_ref, right_ref)
    blocks, _, xs, nz = out_ref.shape

    def emit(place, values):
        fx, fz = do.left("fx", values), do.right(values, "fz")
        for i, value in enumerate(values):
            out_ref[:, place + i] = (value + fx[i] + fz[i]).reshape(blocks, xs, nz)

    emit(0, [last_ref[k] for k in range(8)])
    g8 = [last_ref[8 + k] for k in range(6)]
    axial = do.left("ta", g8)
    axial[0] = last_ref[14] + axial[0]
    emit(8, axial)
    emit(14, [last_ref[15]] + [-tau * value for value in g8])
    third = [-tau * value for value in do.right(g8, "c")]
    third[0] = last_ref[16] + third[0]
    emit(21, third)


def along_y(steps):
    streams, slabs = lax.axis_size("stream"), lax.axis_size("slab")
    count = streams * slabs

    def device(y):
        return (y % streams) * slabs + y // streams

    return [(device(y), device(y + steps)) for y in range(max(0, -steps), min(count, count - steps))]


def shards(state, source_mask, deriv_x, deriv_z, filter_x, filter_z):
    _, _, xs, own, nz = state.shape
    slabs, streams = lax.axis_size("slab"), lax.axis_size("stream")
    slab = lax.axis_index("slab")
    nx = xs * streams
    upward = [(i, i + 1) for i in range(slabs - 1)]
    downward = [(i + 1, i) for i in range(slabs - 1)]
    edges = jnp.stack([(slab > 0).astype(f32), (slab < slabs - 1).astype(f32)])
    region = jnp.repeat(source_mask[:, 0].astype(f32), nx // source_mask.shape[0])
    region = jnp.broadcast_to(region[:, None], (nx, nz))

    raw = jnp.swapaxes(state[0], 1, 2)
    from_low = lax.ppermute(raw[:, own - REACH :], "slab", upward)
    from_high = lax.ppermute(raw[:, :REACH], "slab", downward)
    left, right = call(
        prepare_kernel,
        (
            jax.ShapeDtypeStruct((len(LEFT), nx, 3 * nx), bf16),
            jax.ShapeDtypeStruct((len(RIGHT), 3 * nz, nz), bf16),
        ),
        deriv_x,
        deriv_z.T,
        filter_x,
        filter_z.T,
        flops=10**9,
    )
    ext = jnp.concatenate([from_low, raw, from_high], axis=1)

    def shape(*dims):
        return jax.ShapeDtypeStruct(dims, f32)

    def with_edges(body, out_shape, *args):
        return pl.pallas_call(
            body,
            out_shape=out_shape,
            in_specs=[pl.BlockSpec(memory_space=pltpu.SMEM)]
            + [pl.BlockSpec(memory_space=pltpu.VMEM)] * len(args),
            compiler_params=pltpu.CompilerParams(vmem_limit_bytes=40 * 2**20),
        )(edges, *args)

    spread = with_edges(spread_kernel, shape(own, 13, xs, nz), ext, right)
    planes = lax.all_to_all(spread, "stream", split_axis=0, concat_axis=0, tiled=True)
    waves = call(waves_kernel, shape(5, nx, nz), planes, left, right, flops=2 * 10**9)
    sums = waves[2:5]
    near = [lax.ppermute(sums, AXES, along_y(steps)) for steps in (-1, 1, -2, 2)]
    held = call(held_kernel, shape(3, 5, nx, nz), planes, waves, left, right, flops=10**9)
    source = call(
        source_kernel, shape(4, 3, nx, nz), region, planes, held, *near, left, right, flops=10**9
    )
    source = lax.ppermute(source, "section", [(0, 1)])
    driven = call(driven_kernel, shape(12, nx, nz), waves, source, left, right, flops=2 * 10**9)
    last = call(finish_kernel, shape(17, nx, nz), planes, driven, source, left, right, flops=3 * 10**9)
    done = call(filter_kernel, shape(streams, 27, xs, nz), last, left, right, flops=10**9)
    back = lax.all_to_all(done, "stream", split_axis=0, concat_axis=0, tiled=True)
    border = OUT_P + OUT_U + OUT_V + OUT_W
    mine, high, low = with_edges(
        gather_kernel, (shape(4, own, xs, nz), shape(border, xs, nz), shape(border, xs, nz)), back
    )
    from_low = lax.ppermute(high, "slab", upward)
    from_high = lax.ppermute(low, "slab", downward)
    place = 0
    outs = []
    for i, reach in enumerate((OUT_P, OUT_U, OUT_V, OUT_W)):
        rest = ((0, own - reach), (0, 0), (0, 0))
        from_below = jnp.pad(from_low[place : place + reach], rest)
        from_above = jnp.pad(from_high[place : place + reach], ((own - reach, 0), (0, 0), (0, 0)))
        outs.append(mine[i] + from_below + from_above)
        place += reach
    return jnp.swapaxes(jnp.stack(outs), 1, 2)[None]


def solution(mesh):
    placed = (P("section", None, "stream", "slab", None), P(None, "slab"), P(), P(), P(), P())
    return jax.shard_map(
        shards,
        mesh=mesh,
        in_specs=placed,
        out_specs=P("section", None, "stream", "slab", None),
        check_vma=False,
    )
```

time: 409 us -> 167 us (0.41); the launches traced: 403 us -> 166 us
  starting transfers between devices: 208 us -> 34.8 us
  blocking collectives: 26.7 us -> 82.5 us
  waiting for transfers between devices: 76.9 us -> 21.2 us
  other arithmetic: 32.5 us -> 0.29 us
  local copies, waits for them, and re-layouts: 34.5 us -> 5.67 us
  matrix products: 22 us -> 0 us
  Pallas kernels: 0 us -> 21.7 us
    all_to_all x16 -> x0, starting transfers between devices: 95.4 us -> none  [the longest x8 50.8 us: block_x(): lax.all_to_all(along_x(matrix, lax.all_to_all(fields, 'stream', split_axi...]
    ppermute x36 -> x9, starting transfers between devices: 113 us -> 34.8 us  [the longest x4 20.4 us: shards(): lax.ppermute(sums, AXES, along_y(steps))]
    all_to_all x16 -> x0, waiting for transfers between devices: 72 us -> none  [the longest x8 65.4 us: block_x(): lax.all_to_all(along_x(matrix, lax.all_to_all(fields, 'stream', split_axi...]
    all_to_all x2, blocking collectives: 26.7 us -> 82.5 us  [the longest x1 52.7 us: shards(): lax.all_to_all(done, 'stream', split_axis=0, concat_axis=0, tiled=True)]
    dot_general x18 -> x0, matrix products: 22 us -> none  [the longest x9 12.9 us: along_z(): jnp.einsum('fxyz,kz->fxyk', fields, matrix, precision=lax.Precision.HIGHEST)]
    pallas_call x0 -> x9, Pallas kernels: none -> 21.7 us  [the longest x7 18.8 us: call(): pl.pallas_call(body, out_shape=out_shape, scratch_shapes=scratch, compile...]
    ppermute x36 -> x9, waiting for transfers between devices: 4.95 us -> 21.2 us  [the longest x1 5.43 us: shards(): from_low = lax.ppermute(high, 'slab', upward)]
    add x16 -> x0, other arithmetic: 8.84 us -> none  [the longest x8 7.01 us: tendency(): axial_rate = -mach_number * slope_x[1] - slope_x[0] + forcing[0]]
  transfers between devices with their start and end apart: 52 -> 9, of which waited for: 12 -> 7; matrix products, arithmetic and copies ran while one was open for 16% -> 0% of each run, Pallas kernels for 0% -> 2%
where the time goes in v1:
time: 167 us; the launch traced here: 166 us
  blocking collectives  82.5 us (49%)
  starting transfers between devices  34.8 us (21%)
  Pallas kernels  21.7 us (13%)
  waiting for transfers between devices  21.2 us (13%)
  local copies, waits for them, and re-layouts  5.67 us (3%)
    all_to_all x1, blocking collectives, shards(): lax.all_to_all(done, 'stream', split_axis=0, concat_axis=0, tiled=True)  52.7 us
    all_to_all x1, blocking collectives, shards(): lax.all_to_all(spread, 'stream', split_axis=0, concat_axis=0, tiled=True)  29.8 us
    ppermute x4, starting transfers between devices, shards(): lax.ppermute(sums, AXES, along_y(steps))  20.4 us
    pallas_call x7, Pallas kernels, call(): pl.pallas_call(body, out_shape=out_shape, scratch_shapes=scratch, compile...  18.8 us
    ppermute x1, waiting for transfers between devices, shards(): from_low = lax.ppermute(high, 'slab', upward)  5.43 us
    ppermute x1, waiting for transfers between devices, shards(): from_high = lax.ppermute(raw[:, :REACH], 'slab', downward)  5.33 us
    ppermute x1, starting transfers between devices, shards(): from_low = lax.ppermute(raw[:, own - REACH:], 'slab', upward)  5.04 us
    ppermute x1, starting transfers between devices, shards(): from_high = lax.ppermute(low, 'slab', downward)  3.92 us
  transfers between devices with their start and end apart: 9, of which 7 were waited for; matrix products, arithmetic and copies ran while one was open for 0% of the time, Pallas kernels for 2%

profile of v1, /device:TPU:96, one launch (start us, length us, event | category | flops | bytes accessed | tf_op | source)
XLA Modules:
  0.0 166.4 jit_solution(8509972351989930572)
XLA Ops:
  1.4 5.0 %collective-permute-start = (f32[4,10,16,128]{3,2,1,0:T(8,128)S(1)}, f32[4,10,16,128]{3,2,1,0:T(8,128)S(1)}, u32[]{:S(2)}, u32[]{:S(2)}) collective-permute-start(f32[4,10,16,128]{3,2,1,0:T(8,128)S(1)} %get-tuple-element.19), channel_id=1, source_target_pairs={{0,1},{1,2},{2,3},{3,4},{4,5},{5,6},{6,7},{8,9},{9,10},{10,11},{11... | collective-permute-start | bytes 983048 | tf_op jit(solution)/shard_map/ppermute | solution.py:384
  6.4 1.9 %collective-permute-start.1 = (f32[4,10,16,128]{3,2,1,0:T(8,128)S(1)}, f32[4,10,16,128]{3,2,1,0:T(8,128)S(1)}, u32[]{:S(2)}, u32[]{:S(2)}) collective-permute-start(f32[4,10,16,128]{3,2,1,0:T(8,128)S(1)} %get-tuple-element.20), channel_id=1, source_target_pairs={{1,0},{2,1},{3,2},{4,3},{5,4},{6,5},{7,6},{9,8},{10,9},{11,10},{12... | collective-permute-start | bytes 983048 | tf_op jit(solution)/shard_map/ppermute | solution.py:385
  8.6 1.9 %shard_map.64 = (bf16[10,256,768]{2,1,0:T(8,128)(2,1)S(1)}, bf16[3,384,128]{2,1,0:T(8,128)(2,1)S(1)}) custom-call(f32[256,256]{1,0:T(8,128)S(1)} %copy-done.2, f32[128,128]{1,0:T(8,128)S(1)} %bitcast.43, f32[256,256]{1,0:T(8,128)S(1)} %copy-done.3, f32[128,128]{1,0:T(8,128)S(1)} %bitcast.44), custom_call_target="tpu_custom_call" | custom-call | flops 1000000000 | bytes 655360 | tf_op jit(solution)/shard_map/pallas_call | solution.py:23
  10.5 2.8 %collective-permute-done = f32[4,10,16,128]{3,2,1,0:T(8,128)S(1)} collective-permute-done((f32[4,10,16,128]{3,2,1,0:T(8,128)S(1)}, f32[4,10,16,128]{3,2,1,0:T(8,128)S(1)}, u32[]{:S(2)}, u32[]{:S(2)}) %collective-permute-start) | collective-permute-done | bytes 327712 | tf_op jit(solution)/shard_map/ppermute | solution.py:384
  13.3 5.3 %collective-permute-done.1 = f32[4,10,16,128]{3,2,1,0:T(8,128)S(1)} collective-permute-done((f32[4,10,16,128]{3,2,1,0:T(8,128)S(1)}, f32[4,10,16,128]{3,2,1,0:T(8,128)S(1)}, u32[]{:S(2)}, u32[]{:S(2)}) %collective-permute-start.1) | collective-permute-done | bytes 327712 | tf_op jit(solution)/shard_map/ppermute | solution.py:385
  20.1 29.8 %all_to_all.10.in_ref = f32[16,13,16,128]{3,2,1,0:T(8,128)S(1)} all-to-all(f32[16,13,16,128]{3,2,1,0:T(8,128)S(1)} %shard_map.65), channel_id=1, replica_groups=mesh['section'=2,'stream'=16,'slab'=8] {'stream'}, dimensions={0} | all-to-all | bytes 3407872 | tf_op jit(solution)/shard_map/all_to_all | solution.py:413
  49.8 2.5 %shard_map.66.waves_ref = f32[5,256,128]{2,1,0:T(8,128)S(1)} custom-call(f32[16,13,16,128]{3,2,1,0:T(8,128)S(1)} %all_to_all.10.in_ref, bf16[10,256,768]{2,1,0:T(8,128)(2,1)S(1)} %get-tuple-element.11.left_ref, bf16[3,384,128]{2,1,0:T(8,128)(2,1)S(1)} %get-tuple-element.10.right_ref), custom_call_target="tpu_custom_call" | custom-call | flops 2000000000 | bytes 5931008 | tf_op jit(solution)/shard_map/pallas_call | solution.py:23
  53.1 3.4 %collective-permute-start.5 = (f32[3,256,128]{2,1,0:T(8,128)}, f32[3,256,128]{2,1,0:T(8,128)S(1)}, u32[]{:S(2)}, u32[]{:S(2)}) collective-permute-start(f32[3,256,128]{2,1,0:T(8,128)} %slice.63), channel_id=1, source_target_pairs={{0,16},{8,24},{16,32},{24,40},{32,48},{40,56},{48,64},{56,72},{64,... | collective-permute-start | bytes 1179656 | tf_op jit(solution)/shard_map/ppermute | solution.py:416
  56.6 6.9 %collective-permute-start.4 = (f32[3,256,128]{2,1,0:T(8,128)}, f32[3,256,128]{2,1,0:T(8,128)S(1)}, u32[]{:S(2)}, u32[]{:S(2)}) collective-permute-start(f32[3,256,128]{2,1,0:T(8,128)} %slice.63), channel_id=1, source_target_pairs={{16,0},{24,8},{32,16},{40,24},{48,32},{56,40},{64,48},{72,56},{80,... | collective-permute-start | bytes 1179656 | tf_op jit(solution)/shard_map/ppermute | solution.py:416
  63.5 2.4 %collective-permute-start.3 = (f32[3,256,128]{2,1,0:T(8,128)}, f32[3,256,128]{2,1,0:T(8,128)}, u32[]{:S(2)}, u32[]{:S(2)}) collective-permute-start(f32[3,256,128]{2,1,0:T(8,128)} %slice.63), channel_id=1, source_target_pairs={{0,8},{8,16},{16,24},{24,32},{32,40},{40,48},{48,56},{56,64},{64,7... | collective-permute-start | bytes 1179656 | tf_op jit(solution)/shard_map/ppermute | solution.py:416
  65.9 7.7 %collective-permute-start.2 = (f32[3,256,128]{2,1,0:T(8,128)}, f32[3,256,128]{2,1,0:T(8,128)}, u32[]{:S(2)}, u32[]{:S(2)}) collective-permute-start(f32[3,256,128]{2,1,0:T(8,128)} %slice.63), channel_id=1, source_target_pairs={{8,0},{16,8},{24,16},{32,24},{40,32},{48,40},{56,48},{64,56},{72,6... | collective-permute-start | bytes 1179656 | tf_op jit(solution)/shard_map/ppermute | solution.py:416
  73.8 2.1 %copy-done.1 = bf16[10,256,768]{2,1,0:T(8,128)(2,1)S(1)} copy-done((bf16[10,256,768]{2,1,0:T(8,128)(2,1)S(1)}, bf16[10,256,768]{2,1,0:T(8,128)(2,1)}, u32[]{:S(2)}) %copy-start.1) | copy-done | bytes 3932184
  79.3 2.1 %shard_map.68 = f32[4,3,256,128]{3,2,1,0:T(8,128)S(1)} custom-call(f32[256,128]{1,0:T(8,128)S(1)} %broadcast_in_dim.15.region_ref, f32[16,13,16,128]{3,2,1,0:T(8,128)S(1)} %all_to_all.10.in_ref, f32[3,5,256,128]{3,2,1,0:T(8,128)S(1)} %shard_map.67.held_ref, f32[3,256,128]{2,1,0:T(8,128)} %collective-permute-done.2.up1_ref, ...), custom_call_target="tpu_custom_call" | custom-call | flops 1000000000 | bytes 9601024 | tf_op jit(solution)/shard_map/pallas_call | solution.py:23
  81.4 1.6 collective-permute-start.6
  83.0 2.7 %collective-permute-done.6.source_ref = f32[4,3,256,128]{3,2,1,0:T(8,128)S(1)} collective-permute-done((f32[4,3,256,128]{3,2,1,0:T(8,128)S(1)}, f32[4,3,256,128]{3,2,1,0:T(8,128)S(1)}, u32[]{:S(2)}, u32[]{:S(2)}) %collective-permute-start.6) | collective-permute-done | bytes 1572896 | tf_op jit(solution)/shard_map/ppermute | solution.py:421
  85.7 2.2 %shard_map.69.driven_ref = f32[12,256,128]{2,1,0:T(8,128)S(1)} custom-call(f32[5,256,128]{2,1,0:T(8,128)S(1)} %shard_map.66.waves_ref, f32[4,3,256,128]{3,2,1,0:T(8,128)S(1)} %collective-permute-done.6.source_ref, bf16[10,256,768]{2,1,0:T(8,128)(2,1)S(1)} %copy-done.1, bf16[3,384,128]{2,1,0:T(8,128)(2,1)S(1)} %get-tuple-element.10.right_ref), custom_call_target="tpu_custom_call" | custom-call | flops 2000000000 | bytes 6455296 | tf_op jit(solution)/shard_map/pallas_call | solution.py:23
  88.0 4.8 %shard_map.70.last_ref = f32[17,256,128]{2,1,0:T(8,128)S(1)} custom-call(f32[16,13,16,128]{3,2,1,0:T(8,128)S(1)} %all_to_all.10.in_ref, f32[12,256,128]{2,1,0:T(8,128)S(1)} %shard_map.69.driven_ref, f32[4,3,256,128]{3,2,1,0:T(8,128)S(1)} %collective-permute-done.6.source_ref, bf16[10,256,768]{2,1,0:T(8,128)(2,1)S(1)} %copy-done.1, ...), custom_call_target="tpu_custom_call" | custom-call | flops 3000000000 | bytes 9076736 | tf_op jit(solution)/shard_map/pallas_call | solution.py:23
  92.8 3.7 %shard_map.71 = f32[16,27,16,128]{3,2,1,0:T(8,128)S(1)} custom-call(f32[17,256,128]{2,1,0:T(8,128)S(1)} %shard_map.70.last_ref, bf16[10,256,768]{2,1,0:T(8,128)(2,1)S(1)} %copy-done.1, bf16[3,384,128]{2,1,0:T(8,128)(2,1)S(1)} %get-tuple-element.10.right_ref), custom_call_target="tpu_custom_call" | custom-call | flops 1000000000 | bytes 6455296 | tf_op jit(solution)/shard_map/pallas_call | solution.py:23
  96.5 52.7 %all_to_all.11.back_ref = f32[16,27,16,128]{3,2,1,0:T(8,128)S(1)} all-to-all(f32[16,27,16,128]{3,2,1,0:T(8,128)S(1)} %shard_map.71), channel_id=1, replica_groups=mesh['section'=2,'stream'=16,'slab'=8] {'stream'}, dimensions={0} | all-to-all | bytes 7077888 | tf_op jit(solution)/shard_map/all_to_all | solution.py:425
  149.2 1.6 shard_map.72
  150.8 1.9 %collective-permute-start.7 = (f32[46,16,128]{2,1,0:T(8,128)S(1)}, f32[46,16,128]{2,1,0:T(8,128)S(1)}, u32[]{:S(2)}, u32[]{:S(2)}) collective-permute-start(f32[46,16,128]{2,1,0:T(8,128)S(1)} %get-tuple-element.13), channel_id=1, source_target_pairs={{0,1},{1,2},{2,3},{3,4},{4,5},{5,6},{6,7},{8,9},{9,10},{10,11},{11... | collective-permute-start | bytes 1130504 | tf_op jit(solution)/shard_map/ppermute | solution.py:430
  152.8 3.9 %collective-permute-start.8 = (f32[46,16,128]{2,1,0:T(8,128)S(1)}, f32[46,16,128]{2,1,0:T(8,128)S(1)}, u32[]{:S(2)}, u32[]{:S(2)}) collective-permute-start(f32[46,16,128]{2,1,0:T(8,128)S(1)} %get-tuple-element.14), channel_id=1, source_target_pairs={{1,0},{2,1},{3,2},{4,3},{5,4},{6,5},{7,6},{9,8},{10,9},{11,10},{12... | collective-permute-start | bytes 1130504 | tf_op jit(solution)/shard_map/ppermute | solution.py:431
  156.7 5.4 %collective-permute-done.7 = f32[46,16,128]{2,1,0:T(8,128)S(1)} collective-permute-done((f32[46,16,128]{2,1,0:T(8,128)S(1)}, f32[46,16,128]{2,1,0:T(8,128)S(1)}, u32[]{:S(2)}, u32[]{:S(2)}) %collective-permute-start.7) | collective-permute-done | bytes 376864 | tf_op jit(solution)/shard_map/ppermute | solution.py:430
  162.2 3.1 %collective-permute-done.8 = f32[46,16,128]{2,1,0:T(8,128)S(1)} collective-permute-done((f32[46,16,128]{2,1,0:T(8,128)S(1)}, f32[46,16,128]{2,1,0:T(8,128)S(1)}, u32[]{:S(2)}, u32[]{:S(2)}) %collective-permute-start.8) | collective-permute-done | bytes 376864 | tf_op jit(solution)/shard_map/ppermute | solution.py:431
  (40 shorter events, 8.4 us)
Async XLA Ops:
  0.0 8.3 %copy-start.4 = (f32[128,128]{1,0:T(8,128)S(1)}, f32[128,128]{1,0:T(8,128)}, u32[]{:S(2)}) copy-start(f32[128,128]{1,0:T(8,128)} %param.9) | copy-start | bytes 196612
  0.0 8.4 %copy-start.5 = (f32[128,128]{1,0:T(8,128)S(1)}, f32[128,128]{1,0:T(8,128)}, u32[]{:S(2)}) copy-start(f32[128,128]{1,0:T(8,128)} %param.11) | copy-start | bytes 196612
  0.0 8.5 %copy-start.3 = (f32[256,256]{1,0:T(8,128)S(1)}, f32[256,256]{1,0:T(8,128)}, u32[]{:S(2)}) copy-start(f32[256,256]{1,0:T(8,128)} %fx_ref.1) | copy-start | bytes 786436
  0.0 8.5 %copy-start.2 = (f32[256,256]{1,0:T(8,128)S(1)}, f32[256,256]{1,0:T(8,128)}, u32[]{:S(2)}) copy-start(f32[256,256]{1,0:T(8,128)} %dx_ref.1) | copy-start | bytes 786436
  1.4 12.0 %collective-permute-start = (f32[4,10,16,128]{3,2,1,0:T(8,128)S(1)}, f32[4,10,16,128]{3,2,1,0:T(8,128)S(1)}, u32[]{:S(2)}, u32[]{:S(2)}) collective-permute-start(f32[4,10,16,128]{3,2,1,0:T(8,128)S(1)} %get-tuple-element.19), channel_id=1, source_target_pairs={{0,1},{1,2},{2,3},{3,4},{4,5},{5,6},{6,7},{8,9},{9,10},{10,11},{11... | collective-permute-start | bytes 983048 | tf_op jit(solution)/shard_map/ppermute | solution.py:384
  6.4 12.3 %collective-permute-start.1 = (f32[4,10,16,128]{3,2,1,0:T(8,128)S(1)}, f32[4,10,16,128]{3,2,1,0:T(8,128)S(1)}, u32[]{:S(2)}, u32[]{:S(2)}) collective-permute-start(f32[4,10,16,128]{3,2,1,0:T(8,128)S(1)} %get-tuple-element.20), channel_id=1, source_target_pairs={{1,0},{2,1},{3,2},{4,3},{5,4},{6,5},{7,6},{9,8},{10,9},{11,10},{12... | collective-permute-start | bytes 983048 | tf_op jit(solution)/shard_map/ppermute | solution.py:385
  10.4 39.4 %copy-start = (bf16[10,256,768]{2,1,0:T(8,128)(2,1)}, bf16[10,256,768]{2,1,0:T(8,128)(2,1)S(1)}, u32[]{:S(2)}) copy-start(bf16[10,256,768]{2,1,0:T(8,128)(2,1)S(1)} %get-tuple-element.11.left_ref) | copy-start | bytes 11796484
  49.8 23.8 %copy-start.7 = (s32[16,1]{0,1:T(1,128)S(1)}, s32[16,1]{0,1:T(1,128)}, u32[]{:S(2)}) copy-start(s32[16,1]{0,1:T(1,128)} %param.7) | copy-start | bytes 196
  53.1 24.2 %collective-permute-start.5 = (f32[3,256,128]{2,1,0:T(8,128)}, f32[3,256,128]{2,1,0:T(8,128)S(1)}, u32[]{:S(2)}, u32[]{:S(2)}) collective-permute-start(f32[3,256,128]{2,1,0:T(8,128)} %slice.63), channel_id=1, source_target_pairs={{0,16},{8,24},{16,32},{24,40},{32,48},{40,56},{48,64},{56,72},{64,... | collective-permute-start | bytes 1179656 | tf_op jit(solution)/shard_map/ppermute | solution.py:416
  56.6 20.8 %collective-permute-start.4 = (f32[3,256,128]{2,1,0:T(8,128)}, f32[3,256,128]{2,1,0:T(8,128)S(1)}, u32[]{:S(2)}, u32[]{:S(2)}) collective-permute-start(f32[3,256,128]{2,1,0:T(8,128)} %slice.63), channel_id=1, source_target_pairs={{16,0},{24,8},{32,16},{40,24},{48,32},{56,40},{64,48},{72,56},{80,... | collective-permute-start | bytes 1179656 | tf_op jit(solution)/shard_map/ppermute | solution.py:416
  63.5 14.2 %collective-permute-start.3 = (f32[3,256,128]{2,1,0:T(8,128)}, f32[3,256,128]{2,1,0:T(8,128)}, u32[]{:S(2)}, u32[]{:S(2)}) collective-permute-start(f32[3,256,128]{2,1,0:T(8,128)} %slice.63), channel_id=1, source_target_pairs={{0,8},{8,16},{16,24},{24,32},{32,40},{40,48},{48,56},{56,64},{64,7... | collective-permute-start | bytes 1179656 | tf_op jit(solution)/shard_map/ppermute | solution.py:416
  65.9 13.3 %collective-permute-start.2 = (f32[3,256,128]{2,1,0:T(8,128)}, f32[3,256,128]{2,1,0:T(8,128)}, u32[]{:S(2)}, u32[]{:S(2)}) collective-permute-start(f32[3,256,128]{2,1,0:T(8,128)} %slice.63), channel_id=1, source_target_pairs={{8,0},{16,8},{24,16},{32,24},{40,32},{48,40},{56,48},{64,56},{72,6... | collective-permute-start | bytes 1179656 | tf_op jit(solution)/shard_map/ppermute | solution.py:416
  73.8 2.1 %copy-start.1 = (bf16[10,256,768]{2,1,0:T(8,128)(2,1)S(1)}, bf16[10,256,768]{2,1,0:T(8,128)(2,1)}, u32[]{:S(2)}) copy-start(bf16[10,256,768]{2,1,0:T(8,128)(2,1)} %copy-done) | copy-start | bytes 11796484
  81.4 4.3 %collective-permute-start.6 = (f32[4,3,256,128]{3,2,1,0:T(8,128)S(1)}, f32[4,3,256,128]{3,2,1,0:T(8,128)S(1)}, u32[]{:S(2)}, u32[]{:S(2)}) collective-permute-start(f32[4,3,256,128]{3,2,1,0:T(8,128)S(1)} %shard_map.68), channel_id=1, source_target_pairs={{0,128},{1,129},{2,130},{3,131},{4,132},{5,133},{6,134},{7,135},{8... | collective-permute-start | bytes 4718600 | tf_op jit(solution)/shard_map/ppermute | solution.py:421
  149.2 16.1 %copy-start.6 = (pred[16]{0:T(512)(128)(4,1)S(1)}, pred[16]{0:T(512)(128)(4,1)}, u32[]{:S(2)}) copy-start(pred[16]{0:T(512)(128)(4,1)} %constant.10.clone.1) | copy-start | bytes 52
  150.8 11.3 %collective-permute-start.7 = (f32[46,16,128]{2,1,0:T(8,128)S(1)}, f32[46,16,128]{2,1,0:T(8,128)S(1)}, u32[]{:S(2)}, u32[]{:S(2)}) collective-permute-start(f32[46,16,128]{2,1,0:T(8,128)S(1)} %get-tuple-element.13), channel_id=1, source_target_pairs={{0,1},{1,2},{2,3},{3,4},{4,5},{5,6},{6,7},{8,9},{9,10},{10,11},{11... | collective-permute-start | bytes 1130504 | tf_op jit(solution)/shard_map/ppermute | solution.py:430
  152.8 12.5 %collective-permute-start.8 = (f32[46,16,128]{2,1,0:T(8,128)S(1)}, f32[46,16,128]{2,1,0:T(8,128)S(1)}, u32[]{:S(2)}, u32[]{:S(2)}) collective-permute-start(f32[46,16,128]{2,1,0:T(8,128)S(1)} %get-tuple-element.14), channel_id=1, source_target_pairs={{1,0},{2,1},{3,2},{4,3},{5,4},{6,5},{7,6},{9,8},{10,9},{11,10},{12... | collective-permute-start | bytes 1130504 | tf_op jit(solution)/shard_map/ppermute | solution.py:431

commit v2 on v1

--- a/solution.py
+++ b/solution.py
@@ -10,7 +10,8 @@
 mach_number = 0.5
 tau = 0.05
 filter_weight = 0.25
-REACH = 10
+IN_P, IN_U, IN_V, IN_W = 8, 8, 10, 8
+SLOTS = 19
 OUT_P, OUT_U, OUT_V, OUT_W = 14, 10, 12, 10
 AXES = ("section", "stream", "slab")
 LEFT = ("e1", "ta", "m1", "m2", "e2", "a", "e4", "e6", "e8", "fx")
@@ -27,6 +28,15 @@
         compiler_params=pltpu.CompilerParams(vmem_limit_bytes=40 * 2**20),
         cost_estimate=pl.CostEstimate(flops=flops, bytes_accessed=moved, transcendentals=0),
     )(*args)
+
+
+def order_of(count):
+    places = []
+    for j in range(count):
+        step, rung = j // 2, j % 2
+        x, y = (rung, step) if step < 4 else (3 - rung, 7 - step)
+        places.append(4 * x + y)
+    return places
 
 
 def halves(value):
@@ -117,61 +127,110 @@
     return (2.0 / 3.0) * near - (1.0 / 12.0) * far
 
 
-def spread_kernel(edge_ref, ext_ref, right_ref, out_ref):
+def spread_kernel(edge_ref, raw_ref, low_ref, high_ref, right_ref, out_ref):
     low_ok, high_ok = edge_ref[0], edge_ref[1]
-    own = ext_ref.shape[1] - 2 * REACH
-    rows, xs, nz = ext_ref.shape[1:]
+    own, xs, nz = raw_ref.shape[1:]
+    order = order_of(own)
+    ext = []
+    lead = 0
+    for i, reach in enumerate((IN_P, IN_U, IN_V, IN_W)):
+        ext.append(
+            jnp.concatenate([low_ref[lead : lead + reach], raw_ref[i], high_ref[lead : lead + reach]], axis=0)
+        )
+        lead += reach
 
     def twice(value):
-        once = inside(slope4(value), REACH, low_ok, high_ok)
-        return inside(slope4(once), REACH, low_ok, high_ok)
+        once = inside(slope4(value), IN_P, low_ok, high_ok)
+        return inside(slope4(once), IN_P, low_ok, high_ok)
 
     def put(place, value):
-        out_ref[:, place] = value[REACH : REACH + own]
-
-    def slope2(ref_index):
-        return 0.5 * (
-            ext_ref[ref_index, REACH + 1 : REACH + 1 + own] - ext_ref[ref_index, REACH - 1 : REACH - 1 + own]
-        )
-
-    through = times_right([ext_ref[3].reshape(rows * xs, nz)], right_ref[RIGHT.index("c")])[0]
-    rate = through.reshape(rows, xs, nz) + slope4(ext_ref[2])
-    rate = inside(rate, REACH, low_ok, high_ok)
-    for place, value in ((0, ext_ref[0]), (3, ext_ref[1]), (6, rate)):
+        reach = (value.shape[0] - own) // 2
+        for j in range(own):
+            out_ref[order[j], place] = value[reach + j]
+
+    def slope2(value):
+        return 0.5 * (value[IN_P + 1 : IN_P + 1 + own] - value[IN_P - 1 : IN_P - 1 + own])
+
+    rows = ext[3].shape[0]
+    through = times_right([ext[3].reshape(rows * xs, nz)], right_ref[RIGHT.index("c")])[0]
+    cut = IN_V - IN_W
+    rate = through.reshape(rows, xs, nz) + slope4(ext[2])[cut : cut + rows]
+    rate = inside(rate, IN_W, low_ok, high_ok)
+    for place, value in ((0, ext[0]), (3, ext[1]), (6, rate)):
         put(place, value)
         value = twice(value)
         put(place + 1, value)
         put(place + 2, twice(value))
-    put(9, ext_ref[2])
-    put(10, ext_ref[3])
-    out_ref[:, 11] = slope2(1)
-    out_ref[:, 12] = slope2(3)
-
-
-def gather_kernel(edge_ref, back_ref, own_ref, high_ref, low_ref):
-    low_ok, high_ok = edge_ref[0], edge_ref[1]
-    own = back_ref.shape[0]
-    lead = 0
-    place = 0
-    for output, (count, reach) in enumerate(((8, OUT_P), (6, OUT_U), (7, OUT_V), (6, OUT_W))):
-        total = back_ref[:, lead + count - 1]
-        for k in range(count - 2, -1, -1):
-            edge = 2 * (count - 1 - k)
+    put(9, raw_ref[2])
+    put(10, raw_ref[3])
+    put(11, slope2(ext[1]))
+    put(12, slope2(ext[3]))
+
+
+class Raiser:
+    def __init__(self, edge_ref, back_ref):
+        self.low_ok, self.high_ok = edge_ref[0], edge_ref[1]
+        self.back_ref = back_ref
+        self.own = back_ref.shape[0]
+        self.order = order_of(self.own)
+
+    def load(self, slot):
+        return jnp.stack([self.back_ref[self.order[j], slot] for j in range(self.own)])
+
+    def total(self, fields):
+        total = fields[-1]
+        for value in fields[-2::-1]:
+            edge = (total.shape[0] - self.own) // 2 + 2
             zeros = jnp.zeros((2,) + total.shape[1:], f32)
             total = slope4(jnp.concatenate([zeros, total, zeros], axis=0))
+            centre = total[edge : edge + self.own]
+            if value is not None:
+                centre = centre + value
             total = jnp.concatenate(
-                [
-                    total[:edge] * low_ok,
-                    total[edge : edge + own] + back_ref[:, lead + k],
-                    total[edge + own :] * high_ok,
-                ],
-                axis=0,
+                [total[:edge] * self.low_ok, centre, total[edge + self.own :] * self.high_ok], axis=0
             )
+        return total
+
+
+def gather_odd_kernel(edge_ref, back_ref, out_ref):
+    @pl.when(edge_ref[2] > 0)
+    def _():
+        raiser = Raiser(edge_ref, back_ref)
+        p = [raiser.load(10 + i) for i in range(4)]
+        u = [raiser.load(14 + i) for i in range(3)]
+        lead = 0
+        for value in (
+            raiser.total([None, p[0], None, p[1], None, p[2], None, p[3]]),
+            raiser.total([None, u[0], None, u[1], None, u[2]]),
+            raiser.total([None, raiser.load(17)]),
+        ):
+            out_ref[lead : lead + value.shape[0]] = value
+            lead += value.shape[0]
+
+
+def gather_kernel(edge_ref, back_ref, own_ref, high_ref, low_ref):
+    raiser = Raiser(edge_ref, back_ref)
+    own = raiser.own
+    sound = 1.0 - edge_ref[2]
+
+    def extra(i):
+        return sound * raiser.load(10 + i)
+
+    p = [raiser.load(0), None, raiser.load(1), None, raiser.load(2), None, extra(0)]
+    u = [raiser.load(3), None, raiser.load(4), None, extra(1)]
+    w = [raiser.load(5), None, raiser.load(6), extra(4), extra(2), extra(5)]
+    v = [raiser.load(7), raiser.load(8), extra(6), raiser.load(9), extra(7), extra(3), extra(8)]
+    place = 0
+    for output, (fields, room) in enumerate(((p, OUT_P), (u, OUT_U), (v, OUT_V), (w, OUT_W))):
+        total = raiser.total(fields)
+        reach = 2 * (len(fields) - 1)
         own_ref[output] = total[reach : reach + own]
-        low_ref[place : place + reach] = total[:reach]
+        if room > reach:
+            low_ref[place : place + room - reach] = jnp.zeros((room - reach,) + total.shape[1:], f32)
+            high_ref[place + reach : place + room] = jnp.zeros((room - reach,) + total.shape[1:], f32)
+        low_ref[place + room - reach : place + room] = total[:reach]
         high_ref[place : place + reach] = total[reach + own :]
-        place += reach
-        lead += count
+        place += room
 
 
 def plane(ref, index):
@@ -292,18 +351,22 @@
         return [out[k] + (sums[k] + kept[k]) if k < len(sums) else out[k] for k in range(len(now))]
 
 
-def drives(do, source_ref, first, last):
+def drives(do, flag_ref, own_ref, source_ref, first, last):
+    flow = flag_ref[2] > 0
     one = do.left("a", [source_ref[n, 0] for n in range(first, last)])
     two = do.right([source_ref[n, 2] for n in range(first, last)], "c")
     return [
-        (-(tau**2) * (one[n - first] + two[n - first]), -(tau**2) * source_ref[n, 1])
+        (
+            -(tau**2) * (one[n - first] + two[n - first]),
+            -(tau**2) * jnp.where(flow, own_ref[n, 1], source_ref[n, 1]),
+        )
         for n in range(first, last)
     ]
 
 
-def driven_kernel(waves_ref, source_ref, left_ref, right_ref, out_ref):
+def driven_kernel(flag_ref, waves_ref, own_ref, source_ref, left_ref, right_ref, out_ref):
     chain = Chain(left_ref, right_ref)
-    drive = drives(chain.do, source_ref, 0, 2)
+    drive = drives(chain.do, flag_ref, own_ref, source_ref, 0, 2)
     q2 = list(drive[0])
     moved = chain.do.left("m1", q2)
     q3 = [2.0 * q2[k] + moved[k] + drive[0][k] for k in range(2)]
@@ -317,10 +380,10 @@
             out_ref[first + k] = values[k]
 
 
-def finish_kernel(in_ref, driven_ref, source_ref, left_ref, right_ref, out_ref):
+def finish_kernel(flag_ref, in_ref, driven_ref, own_ref, source_ref, left_ref, right_ref, out_ref):
     chain = Chain(left_ref, right_ref)
     do = chain.do
-    drive = drives(do, source_ref, 2, 4)
+    drive = drives(do, flag_ref, own_ref, source_ref, 2, 4)
     q4, q5, g6 = [[driven_ref[first + k] for k in range(4)] for first in (0, 4, 8)]
     q6 = chain.advance(q5, q4, drive[0], 6)
     q7 = chain.advance(q6, q5, drive[0], 6)
@@ -339,7 +402,7 @@
         out_ref[14 + i] = begin[i] + kept[i] + tau * (2.0 * total[i] + moved[i])
 
 
-def filter_kernel(last_ref, left_ref, right_ref, out_ref):
+def filter_kernel(flag_ref, last_ref, left_ref, right_ref, out_ref):
     do = Products(left_ref, right_ref)
     blocks, _, xs, nz = out_ref.shape
 
@@ -348,23 +411,41 @@
         for i, value in enumerate(values):
             out_ref[:, place + i] = (value + fx[i] + fz[i]).reshape(blocks, xs, nz)
 
-    emit(0, [last_ref[k] for k in range(8)])
-    g8 = [last_ref[8 + k] for k in range(6)]
-    axial = do.left("ta", g8)
-    axial[0] = last_ref[14] + axial[0]
-    emit(8, axial)
-    emit(14, [last_ref[15]] + [-tau * value for value in g8])
-    third = [-tau * value for value in do.right(g8, "c")]
-    third[0] = last_ref[16] + third[0]
-    emit(21, third)
+    def p(k):
+        return last_ref[k]
+
+    def h(k):
+        return last_ref[8 + k]
+
+    def third(*which):
+        return [-tau * value for value in do.right([h(k) for k in which], "c")]
+
+    axial = do.left("ta", [h(0), h(2)])
+    depth = third(0, 2)
+    emit(0, [p(0), p(2), p(4), last_ref[14] + axial[0], axial[1], last_ref[16] + depth[0], depth[1]])
+    emit(7, [last_ref[15], -tau * h(0), -tau * h(2)])
+
+    @pl.when(flag_ref[2] > 0)
+    def _():
+        axial = do.left("ta", [h(1), h(3), h(5)])
+        emit(10, [p(1), p(3), p(5), p(7)] + axial + third(1))
+        out_ref[:, 18] = jnp.zeros((blocks, xs, nz), f32)
+
+    @pl.when(flag_ref[2] <= 0)
+    def _():
+        axial = do.left("ta", [h(4)])
+        depth = third(4, 3, 5)
+        emit(10, [p(6), axial[0], depth[0], -tau * h(4), depth[1], depth[2]])
+        emit(16, [-tau * h(1), -tau * h(3), -tau * h(5)])
 
 
 def along_y(steps):
     streams, slabs = lax.axis_size("stream"), lax.axis_size("slab")
     count = streams * slabs
+    order = order_of(streams)
 
     def device(y):
-        return (y % streams) * slabs + y // streams
+        return order[y % streams] * slabs + y // streams
 
     return [(device(y), device(y + steps)) for y in range(max(0, -steps), min(count, count - steps))]
 
@@ -376,13 +457,20 @@
     nx = xs * streams
     upward = [(i, i + 1) for i in range(slabs - 1)]
     downward = [(i + 1, i) for i in range(slabs - 1)]
-    edges = jnp.stack([(slab > 0).astype(f32), (slab < slabs - 1).astype(f32)])
+    edges = jnp.stack(
+        [slab > 0, slab < slabs - 1, lax.axis_index("section") == 0]
+    ).astype(f32)
     region = jnp.repeat(source_mask[:, 0].astype(f32), nx // source_mask.shape[0])
     region = jnp.broadcast_to(region[:, None], (nx, nz))
 
     raw = jnp.swapaxes(state[0], 1, 2)
-    from_low = lax.ppermute(raw[:, own - REACH :], "slab", upward)
-    from_high = lax.ppermute(raw[:, :REACH], "slab", downward)
+    reaches = (IN_P, IN_U, IN_V, IN_W)
+    from_low = lax.ppermute(
+        jnp.concatenate([raw[i, own - reach :] for i, reach in enumerate(reaches)]), "slab", upward
+    )
+    from_high = lax.ppermute(
+        jnp.concatenate([raw[i, :reach] for i, reach in enumerate(reaches)]), "slab", downward
+    )
     left, right = call(
         prepare_kernel,
         (
@@ -395,7 +483,6 @@
         filter_z.T,
         flops=10**9,
     )
-    ext = jnp.concatenate([from_low, raw, from_high], axis=1)
 
     def shape(*dims):
         return jax.ShapeDtypeStruct(dims, f32)
@@ -409,7 +496,7 @@
             compiler_params=pltpu.CompilerParams(vmem_limit_bytes=40 * 2**20),
         )(edges, *args)
 
-    spread = with_edges(spread_kernel, shape(own, 13, xs, nz), ext, right)
+    spread = with_edges(spread_kernel, shape(own, 13, xs, nz), raw, from_low, from_high, right)
     planes = lax.all_to_all(spread, "stream", split_axis=0, concat_axis=0, tiled=True)
     waves = call(waves_kernel, shape(5, nx, nz), planes, left, right, flops=2 * 10**9)
     sums = waves[2:5]
@@ -418,25 +505,36 @@
     source = call(
         source_kernel, shape(4, 3, nx, nz), region, planes, held, *near, left, right, flops=10**9
     )
-    source = lax.ppermute(source, "section", [(0, 1)])
-    driven = call(driven_kernel, shape(12, nx, nz), waves, source, left, right, flops=2 * 10**9)
-    last = call(finish_kernel, shape(17, nx, nz), planes, driven, source, left, right, flops=3 * 10**9)
-    done = call(filter_kernel, shape(streams, 27, xs, nz), last, left, right, flops=10**9)
+    moved = lax.ppermute(source, "section", [(0, 1)])
+    driven = with_edges(driven_kernel, shape(12, nx, nz), waves, source, moved, left, right)
+    last = with_edges(finish_kernel, shape(17, nx, nz), planes, driven, source, moved, left, right)
+    done = with_edges(filter_kernel, shape(streams, SLOTS, xs, nz), last, left, right)
     back = lax.all_to_all(done, "stream", split_axis=0, concat_axis=0, tiled=True)
     border = OUT_P + OUT_U + OUT_V + OUT_W
+    rows = ((OUT_P, 0), (OUT_U, 1), (2, 3))
+    odd = with_edges(gather_odd_kernel, shape(sum(own + 2 * reach for reach, _ in rows), xs, nz), back)
+    odd = lax.ppermute(odd, "section", [(0, 1)])
     mine, high, low = with_edges(
         gather_kernel, (shape(4, own, xs, nz), shape(border, xs, nz), shape(border, xs, nz)), back
     )
-    from_low = lax.ppermute(high, "slab", upward)
-    from_high = lax.ppermute(low, "slab", downward)
-    place = 0
+    starts = (0, OUT_P, OUT_P + OUT_U, OUT_P + OUT_U + OUT_V)
+    reaches = (OUT_P, OUT_U, OUT_V, OUT_W)
+    lead = 0
+    more_high, more_low, more_own = [], [], [jnp.zeros((own, xs, nz), f32)] * 4
+    for reach, output in rows:
+        part = odd[lead : lead + own + 2 * reach]
+        start, room = starts[output], reaches[output]
+        more_low.append(jnp.pad(part[:reach], ((start + room - reach, border - start - room), (0, 0), (0, 0))))
+        more_high.append(jnp.pad(part[reach + own :], ((start, border - start - reach), (0, 0), (0, 0))))
+        more_own[output] = part[reach : reach + own]
+        lead += own + 2 * reach
+    from_low = lax.ppermute(high + sum(more_high), "slab", upward)
+    from_high = lax.ppermute(low + sum(more_low), "slab", downward)
     outs = []
-    for i, reach in enumerate((OUT_P, OUT_U, OUT_V, OUT_W)):
-        rest = ((0, own - reach), (0, 0), (0, 0))
-        from_below = jnp.pad(from_low[place : place + reach], rest)
-        from_above = jnp.pad(from_high[place : place + reach], ((own - reach, 0), (0, 0), (0, 0)))
-        outs.append(mine[i] + from_below + from_above)
-        place += reach
+    for i, (start, reach) in enumerate(zip(starts, reaches)):
+        from_below = jnp.pad(from_low[start : start + reach], ((0, own - reach), (0, 0), (0, 0)))
+        from_above = jnp.pad(from_high[start : start + reach], ((own - reach, 0), (0, 0), (0, 0)))
+        outs.append(mine[i] + more_own[i] + from_below + from_above)
     return jnp.swapaxes(jnp.stack(outs), 1, 2)[None]
 
 

time: 167 us -> 155 us (0.928)
  blocking collectives: 82.5 us -> 69.6 us
  starting transfers between devices: 34.8 us -> 31.9 us
  Pallas kernels: 21.7 us -> 23.6 us
    all_to_all x1, blocking collectives: 52.7 us -> 39.8 us  [shards(): lax.all_to_all(done, 'stream', split_axis=0, concat_axis=0, tiled=True)]
    pallas_call x2 -> x6, Pallas kernels: 2.88 us -> 15.6 us  [with_edges(): pl.pallas_call(body, out_shape=out_shape, in_specs=[pl.BlockSpec(memory_s...]
    pallas_call x7 -> x4, Pallas kernels: 18.8 us -> 7.99 us  [call(): pl.pallas_call(body, out_shape=out_shape, scratch_shapes=scratch, compile...]
    ppermute x4, starting transfers between devices: 20.4 us -> 16.2 us  [shards(): lax.ppermute(sums, AXES, along_y(steps))]
    ppermute x5 -> x6, starting transfers between devices: 14.4 us -> 15.7 us  [the longest x1 5.04 us: shards(): lax.ppermute(jnp.concatenate([raw[i, own - reach:] for i, reach in enumer...]
    ppermute x5 -> x6, waiting for transfers between devices: 19.4 us -> 20.4 us  [the longest x1 6.93 us: shards(): from_low = lax.ppermute(high + sum(more_high), 'slab', upward)]
    unnamed x19 -> x21, local copies, waits for them, and re-layouts: 3.59 us -> 3.6 us
  transfers between devices with their start and end apart: 9 -> 10, of which waited for: 7 -> 8; matrix products, arithmetic and copies ran while one was open for 0% -> 0% of each run, Pallas kernels for 2% -> 3%
where the time goes in v2:
time: 155 us; the launch traced here: 154 us
  blocking collectives  69.6 us (45%)
  starting transfers between devices  31.9 us (21%)
  Pallas kernels  23.6 us (15%)
  waiting for transfers between devices  22.2 us (14%)
  local copies, waits for them, and re-layouts  5.69 us (4%)
    all_to_all x1, blocking collectives, shards(): lax.all_to_all(done, 'stream', split_axis=0, concat_axis=0, tiled=True)  39.8 us
    all_to_all x1, blocking collectives, shards(): lax.all_to_all(spread, 'stream', split_axis=0, concat_axis=0, tiled=True)  29.8 us
    ppermute x4, starting transfers between devices, shards(): lax.ppermute(sums, AXES, along_y(steps))  16.2 us
    pallas_call x6, Pallas kernels, with_edges(): pl.pallas_call(body, out_shape=out_shape, in_specs=[pl.BlockSpec(memory_s...  15.6 us
    pallas_call x4, Pallas kernels, call(): pl.pallas_call(body, out_shape=out_shape, scratch_shapes=scratch, compile...  7.99 us
    ppermute x1, waiting for transfers between devices, shards(): from_low = lax.ppermute(high + sum(more_high), 'slab', upward)  6.93 us
    ppermute x1, waiting for transfers between devices, shards(): lax.ppermute(jnp.concatenate([raw[i, :reach] for i, reach in enumerate(re...  5.36 us
    ppermute x1, starting transfers between devices, shards(): lax.ppermute(jnp.concatenate([raw[i, own - reach:] for i, reach in enumer...  5.04 us
  transfers between devices with their start and end apart: 10, of which 8 were waited for; matrix products, arithmetic and copies ran while one was open for 0% of the time, Pallas kernels for 3%

profile of v2, /device:TPU:96, one launch (start us, length us, event | category | flops | bytes accessed | tf_op | source)
XLA Modules:
  0.0 153.9 jit_solution(16631732218524113985)
XLA Ops:
  1.4 5.0 %collective-permute-start = (f32[34,16,128]{2,1,0:T(8,128)S(1)}, f32[34,16,128]{2,1,0:T(8,128)S(1)}, u32[]{:S(2)}, u32[]{:S(2)}) collective-permute-start(f32[34,16,128]{2,1,0:T(8,128)S(1)} %pad_maximum_fusion), channel_id=1, source_target_pairs={{0,1},{1,2},{2,3},{3,4},{4,5},{5,6},{6,7},{8,9},{9,10},{10,11},{11... | collective-permute-start | bytes 835592 | tf_op jit(solution)/shard_map/ppermute | solution.py:468
  6.5 1.9 %collective-permute-start.1 = (f32[34,16,128]{2,1,0:T(8,128)S(1)}, f32[34,16,128]{2,1,0:T(8,128)S(1)}, u32[]{:S(2)}, u32[]{:S(2)}) collective-permute-start(f32[34,16,128]{2,1,0:T(8,128)S(1)} %pad_maximum_fusion.1), channel_id=1, source_target_pairs={{1,0},{2,1},{3,2},{4,3},{5,4},{6,5},{7,6},{9,8},{10,9},{11,10},{12... | collective-permute-start | bytes 835592 | tf_op jit(solution)/shard_map/ppermute | solution.py:471
  8.6 1.9 %shard_map.64 = (bf16[10,256,768]{2,1,0:T(8,128)(2,1)S(1)}, bf16[3,384,128]{2,1,0:T(8,128)(2,1)S(1)}) custom-call(f32[256,256]{1,0:T(8,128)S(1)} %copy-done.2, f32[128,128]{1,0:T(8,128)S(1)} %bitcast.55, f32[256,256]{1,0:T(8,128)S(1)} %copy-done.3, f32[128,128]{1,0:T(8,128)S(1)} %bitcast.56), custom_call_target="tpu_custom_call" | custom-call | flops 1000000000 | bytes 655360 | tf_op jit(solution)/shard_map/pallas_call | solution.py:24
  10.6 1.7 %collective-permute-done.low_ref = f32[34,16,128]{2,1,0:T(8,128)S(1)} collective-permute-done((f32[34,16,128]{2,1,0:T(8,128)S(1)}, f32[34,16,128]{2,1,0:T(8,128)S(1)}, u32[]{:S(2)}, u32[]{:S(2)}) %collective-permute-start) | collective-permute-done | bytes 278560 | tf_op jit(solution)/shard_map/ppermute | solution.py:468
  12.3 5.4 %collective-permute-done.1.high_ref = f32[34,16,128]{2,1,0:T(8,128)S(1)} collective-permute-done((f32[34,16,128]{2,1,0:T(8,128)S(1)}, f32[34,16,128]{2,1,0:T(8,128)S(1)}, u32[]{:S(2)}, u32[]{:S(2)}) %collective-permute-start.1) | collective-permute-done | bytes 278560 | tf_op jit(solution)/shard_map/ppermute | solution.py:471
  18.9 29.8 %all_to_all.10.in_ref = f32[16,13,16,128]{3,2,1,0:T(8,128)S(1)} all-to-all(f32[16,13,16,128]{3,2,1,0:T(8,128)S(1)} %shard_map.65), channel_id=1, replica_groups=mesh['section'=2,'stream'=16,'slab'=8] {'stream'}, dimensions={0} | all-to-all | bytes 3407872 | tf_op jit(solution)/shard_map/all_to_all | solution.py:500
  48.7 2.5 %shard_map.66.waves_ref = f32[5,256,128]{2,1,0:T(8,128)S(1)} custom-call(f32[16,13,16,128]{3,2,1,0:T(8,128)S(1)} %all_to_all.10.in_ref, bf16[10,256,768]{2,1,0:T(8,128)(2,1)S(1)} %get-tuple-element.11.left_ref, bf16[3,384,128]{2,1,0:T(8,128)(2,1)S(1)} %get-tuple-element.10.right_ref), custom_call_target="tpu_custom_call" | custom-call | flops 2000000000 | bytes 5931008 | tf_op jit(solution)/shard_map/pallas_call | solution.py:24
  52.0 2.4 %collective-permute-start.5 = (f32[3,256,128]{2,1,0:T(8,128)}, f32[3,256,128]{2,1,0:T(8,128)S(1)}, u32[]{:S(2)}, u32[]{:S(2)}) collective-permute-start(f32[3,256,128]{2,1,0:T(8,128)} %slice.142), channel_id=1, source_target_pairs={{0,8},{32,40},{8,16},{40,48},{16,24},{48,56},{24,120},{56,88},{120... | collective-permute-start | bytes 1179656 | tf_op jit(solution)/shard_map/ppermute | solution.py:503
  54.4 5.6 %collective-permute-start.4 = (f32[3,256,128]{2,1,0:T(8,128)}, f32[3,256,128]{2,1,0:T(8,128)S(1)}, u32[]{:S(2)}, u32[]{:S(2)}) collective-permute-start(f32[3,256,128]{2,1,0:T(8,128)} %slice.142), channel_id=1, source_target_pairs={{8,0},{40,32},{16,8},{48,40},{24,16},{56,48},{120,24},{88,56},{112... | collective-permute-start | bytes 1179656 | tf_op jit(solution)/shard_map/ppermute | solution.py:503
  60.0 1.9 %collective-permute-start.3 = (f32[3,256,128]{2,1,0:T(8,128)}, f32[3,256,128]{2,1,0:T(8,128)}, u32[]{:S(2)}, u32[]{:S(2)}) collective-permute-start(f32[3,256,128]{2,1,0:T(8,128)} %slice.142), channel_id=1, source_target_pairs={{0,32},{32,8},{8,40},{40,16},{16,48},{48,24},{24,56},{56,120},{120... | collective-permute-start | bytes 1179656 | tf_op jit(solution)/shard_map/ppermute | solution.py:503
  61.9 6.3 %collective-permute-start.2 = (f32[3,256,128]{2,1,0:T(8,128)}, f32[3,256,128]{2,1,0:T(8,128)}, u32[]{:S(2)}, u32[]{:S(2)}) collective-permute-start(f32[3,256,128]{2,1,0:T(8,128)} %slice.142), channel_id=1, source_target_pairs={{32,0},{8,32},{40,8},{16,40},{48,16},{24,48},{56,24},{120,56},{88,... | collective-permute-start | bytes 1179656 | tf_op jit(solution)/shard_map/ppermute | solution.py:503
  68.4 2.1 %copy-done.1 = bf16[10,256,768]{2,1,0:T(8,128)(2,1)S(1)} copy-done((bf16[10,256,768]{2,1,0:T(8,128)(2,1)S(1)}, bf16[10,256,768]{2,1,0:T(8,128)(2,1)}, u32[]{:S(2)}) %copy-start.1) | copy-done | bytes 3932184
  73.9 2.1 %shard_map.68.own_ref = f32[4,3,256,128]{3,2,1,0:T(8,128)S(1)} custom-call(f32[256,128]{1,0:T(8,128)S(1)} %broadcast_in_dim.15.region_ref, f32[16,13,16,128]{3,2,1,0:T(8,128)S(1)} %all_to_all.10.in_ref, f32[3,5,256,128]{3,2,1,0:T(8,128)S(1)} %shard_map.67.held_ref, f32[3,256,128]{2,1,0:T(8,128)} %collective-permute-done.2.up1_ref, ...), custom_call_target="tpu_custom_call" | custom-call | flops 1000000000 | bytes 9601024 | tf_op jit(solution)/shard_map/pallas_call | solution.py:24
  76.1 1.6 %collective-permute-start.6 = (f32[4,3,256,128]{3,2,1,0:T(8,128)S(1)}, f32[4,3,256,128]{3,2,1,0:T(8,128)S(1)}, u32[]{:S(2)}, u32[]{:S(2)}) collective-permute-start(f32[4,3,256,128]{3,2,1,0:T(8,128)S(1)} %shard_map.68.own_ref), channel_id=1, source_target_pairs={{0,128},{1,129},{2,130},{3,131},{4,132},{5,133},{6,134},{7,135},{8... | collective-permute-start | bytes 4718600 | tf_op jit(solution)/shard_map/ppermute | solution.py:508
  77.7 2.7 %collective-permute-done.6.source_ref = f32[4,3,256,128]{3,2,1,0:T(8,128)S(1)} collective-permute-done((f32[4,3,256,128]{3,2,1,0:T(8,128)S(1)}, f32[4,3,256,128]{3,2,1,0:T(8,128)S(1)}, u32[]{:S(2)}, u32[]{:S(2)}) %collective-permute-start.6) | collective-permute-done | bytes 1572896 | tf_op jit(solution)/shard_map/ppermute | solution.py:508
  80.4 2.8 %shard_map.69.driven_ref = f32[12,256,128]{2,1,0:T(8,128)S(1)} custom-call(f32[3]{0:T(128)S(1)} %add_convert_fusion.edge_ref.flag_ref, f32[5,256,128]{2,1,0:T(8,128)S(1)} %shard_map.66.waves_ref, f32[4,3,256,128]{3,2,1,0:T(8,128)S(1)} %shard_map.68.own_ref, f32[4,3,256,128]{3,2,1,0:T(8,128)S(1)} %collective-permute-done.6.source_ref, ...), custom_call_target="tpu_custom_call" | custom-call | tf_op jit(solution)/shard_map/pallas_call | solution.py:491
  83.2 5.6 %shard_map.70.last_ref = f32[17,256,128]{2,1,0:T(8,128)S(1)} custom-call(f32[3]{0:T(128)S(1)} %add_convert_fusion.edge_ref.flag_ref, f32[16,13,16,128]{3,2,1,0:T(8,128)S(1)} %all_to_all.10.in_ref, f32[12,256,128]{2,1,0:T(8,128)S(1)} %shard_map.69.driven_ref, f32[4,3,256,128]{3,2,1,0:T(8,128)S(1)} %shard_map.68.own_ref, ...), custom_call_target="tpu_custom_call" | custom-call | tf_op jit(solution)/shard_map/pallas_call | solution.py:491
  88.8 3.4 %shard_map.71 = f32[16,19,16,128]{3,2,1,0:T(8,128)S(1)} custom-call(f32[3]{0:T(128)S(1)} %add_convert_fusion.edge_ref.flag_ref, f32[17,256,128]{2,1,0:T(8,128)S(1)} %shard_map.70.last_ref, bf16[10,256,768]{2,1,0:T(8,128)(2,1)S(1)} %copy-done.1, bf16[3,384,128]{2,1,0:T(8,128)(2,1)S(1)} %get-tuple-element.10.right_ref), custom_call_target="tpu_custom_call" | custom-call | tf_op jit(solution)/shard_map/pallas_call | solution.py:491
  92.2 39.8 %all_to_all.11.back_ref = f32[16,19,16,128]{3,2,1,0:T(8,128)S(1)} all-to-all(f32[16,19,16,128]{3,2,1,0:T(8,128)S(1)} %shard_map.71), channel_id=1, replica_groups=mesh['section'=2,'stream'=16,'slab'=8] {'stream'}, dimensions={0} | all-to-all | bytes 4980736 | tf_op jit(solution)/shard_map/all_to_all | solution.py:512
  134.5 1.5 shard_map.72
  136.5 1.9 %collective-permute-start.8 = (f32[46,16,128]{2,1,0:T(8,128)S(1)}, f32[46,16,128]{2,1,0:T(8,128)S(1)}, u32[]{:S(2)}, u32[]{:S(2)}) collective-permute-start(f32[46,16,128]{2,1,0:T(8,128)S(1)} %add_add_fusion), channel_id=1, source_target_pairs={{0,1},{1,2},{2,3},{3,4},{4,5},{5,6},{6,7},{8,9},{9,10},{10,11},{11... | collective-permute-start | bytes 1130504 | tf_op jit(solution)/shard_map/ppermute | solution.py:531
  138.6 3.9 %collective-permute-start.9 = (f32[46,16,128]{2,1,0:T(8,128)S(1)}, f32[46,16,128]{2,1,0:T(8,128)S(1)}, u32[]{:S(2)}, u32[]{:S(2)}) collective-permute-start(f32[46,16,128]{2,1,0:T(8,128)S(1)} %fusion.2), channel_id=1, source_target_pairs={{1,0},{2,1},{3,2},{4,3},{5,4},{6,5},{7,6},{9,8},{10,9},{11,10},{12... | collective-permute-start | bytes 1130504 | tf_op jit(solution)/shard_map/ppermute | solution.py:532
  142.5 6.9 %collective-permute-done.8 = f32[46,16,128]{2,1,0:T(8,128)S(1)} collective-permute-done((f32[46,16,128]{2,1,0:T(8,128)S(1)}, f32[46,16,128]{2,1,0:T(8,128)S(1)}, u32[]{:S(2)}, u32[]{:S(2)}) %collective-permute-start.8) | collective-permute-done | bytes 376864 | tf_op jit(solution)/shard_map/ppermute | solution.py:531
  149.5 3.2 %collective-permute-done.9 = f32[46,16,128]{2,1,0:T(8,128)S(1)} collective-permute-done((f32[46,16,128]{2,1,0:T(8,128)S(1)}, f32[46,16,128]{2,1,0:T(8,128)S(1)}, u32[]{:S(2)}, u32[]{:S(2)}) %collective-permute-start.9) | collective-permute-done | bytes 376864 | tf_op jit(solution)/shard_map/ppermute | solution.py:532
  (52 shorter events, 11.4 us)
Async XLA Ops:
  0.0 8.4 %copy-start.4 = (f32[128,128]{1,0:T(8,128)S(1)}, f32[128,128]{1,0:T(8,128)}, u32[]{:S(2)}) copy-start(f32[128,128]{1,0:T(8,128)} %param.9) | copy-start | bytes 196612
  0.0 8.5 %copy-start.5 = (f32[128,128]{1,0:T(8,128)S(1)}, f32[128,128]{1,0:T(8,128)}, u32[]{:S(2)}) copy-start(f32[128,128]{1,0:T(8,128)} %param.11) | copy-start | bytes 196612
  0.0 8.6 %copy-start.3 = (f32[256,256]{1,0:T(8,128)S(1)}, f32[256,256]{1,0:T(8,128)}, u32[]{:S(2)}) copy-start(f32[256,256]{1,0:T(8,128)} %fx_ref.1) | copy-start | bytes 786436
  0.0 8.6 %copy-start.2 = (f32[256,256]{1,0:T(8,128)S(1)}, f32[256,256]{1,0:T(8,128)}, u32[]{:S(2)}) copy-start(f32[256,256]{1,0:T(8,128)} %dx_ref.1) | copy-start | bytes 786436
  1.4 10.9 %collective-permute-start = (f32[34,16,128]{2,1,0:T(8,128)S(1)}, f32[34,16,128]{2,1,0:T(8,128)S(1)}, u32[]{:S(2)}, u32[]{:S(2)}) collective-permute-start(f32[34,16,128]{2,1,0:T(8,128)S(1)} %pad_maximum_fusion), channel_id=1, source_target_pairs={{0,1},{1,2},{2,3},{3,4},{4,5},{5,6},{6,7},{8,9},{9,10},{10,11},{11... | collective-permute-start | bytes 835592 | tf_op jit(solution)/shard_map/ppermute | solution.py:468
  6.5 11.2 %collective-permute-start.1 = (f32[34,16,128]{2,1,0:T(8,128)S(1)}, f32[34,16,128]{2,1,0:T(8,128)S(1)}, u32[]{:S(2)}, u32[]{:S(2)}) collective-permute-start(f32[34,16,128]{2,1,0:T(8,128)S(1)} %pad_maximum_fusion.1), channel_id=1, source_target_pairs={{1,0},{2,1},{3,2},{4,3},{5,4},{6,5},{7,6},{9,8},{10,9},{11,10},{12... | collective-permute-start | bytes 835592 | tf_op jit(solution)/shard_map/ppermute | solution.py:471
  10.5 38.2 %copy-start = (bf16[10,256,768]{2,1,0:T(8,128)(2,1)}, bf16[10,256,768]{2,1,0:T(8,128)(2,1)S(1)}, u32[]{:S(2)}) copy-start(bf16[10,256,768]{2,1,0:T(8,128)(2,1)S(1)} %get-tuple-element.11.left_ref) | copy-start | bytes 11796484
  48.7 19.5 %copy-start.8 = (s32[16,1]{0,1:T(1,128)S(1)}, s32[16,1]{0,1:T(1,128)}, u32[]{:S(2)}) copy-start(s32[16,1]{0,1:T(1,128)} %param.7) | copy-start | bytes 196
  52.0 20.0 %collective-permute-start.5 = (f32[3,256,128]{2,1,0:T(8,128)}, f32[3,256,128]{2,1,0:T(8,128)S(1)}, u32[]{:S(2)}, u32[]{:S(2)}) collective-permute-start(f32[3,256,128]{2,1,0:T(8,128)} %slice.142), channel_id=1, source_target_pairs={{0,8},{32,40},{8,16},{40,48},{16,24},{48,56},{24,120},{56,88},{120... | collective-permute-start | bytes 1179656 | tf_op jit(solution)/shard_map/ppermute | solution.py:503
  54.4 17.6 %collective-permute-start.4 = (f32[3,256,128]{2,1,0:T(8,128)}, f32[3,256,128]{2,1,0:T(8,128)S(1)}, u32[]{:S(2)}, u32[]{:S(2)}) collective-permute-start(f32[3,256,128]{2,1,0:T(8,128)} %slice.142), channel_id=1, source_target_pairs={{8,0},{40,32},{16,8},{48,40},{24,16},{56,48},{120,24},{88,56},{112... | collective-permute-start | bytes 1179656 | tf_op jit(solution)/shard_map/ppermute | solution.py:503
  60.0 12.5 %collective-permute-start.3 = (f32[3,256,128]{2,1,0:T(8,128)}, f32[3,256,128]{2,1,0:T(8,128)}, u32[]{:S(2)}, u32[]{:S(2)}) collective-permute-start(f32[3,256,128]{2,1,0:T(8,128)} %slice.142), channel_id=1, source_target_pairs={{0,32},{32,8},{8,40},{40,16},{16,48},{48,24},{24,56},{56,120},{120... | collective-permute-start | bytes 1179656 | tf_op jit(solution)/shard_map/ppermute | solution.py:503
  61.9 11.9 %collective-permute-start.2 = (f32[3,256,128]{2,1,0:T(8,128)}, f32[3,256,128]{2,1,0:T(8,128)}, u32[]{:S(2)}, u32[]{:S(2)}) collective-permute-start(f32[3,256,128]{2,1,0:T(8,128)} %slice.142), channel_id=1, source_target_pairs={{32,0},{8,32},{40,8},{16,40},{48,16},{24,48},{56,24},{120,56},{88,... | collective-permute-start | bytes 1179656 | tf_op jit(solution)/shard_map/ppermute | solution.py:503
  68.4 2.1 %copy-start.1 = (bf16[10,256,768]{2,1,0:T(8,128)(2,1)S(1)}, bf16[10,256,768]{2,1,0:T(8,128)(2,1)}, u32[]{:S(2)}) copy-start(bf16[10,256,768]{2,1,0:T(8,128)(2,1)} %copy-done) | copy-start | bytes 11796484
  76.1 4.3 %collective-permute-start.6 = (f32[4,3,256,128]{3,2,1,0:T(8,128)S(1)}, f32[4,3,256,128]{3,2,1,0:T(8,128)S(1)}, u32[]{:S(2)}, u32[]{:S(2)}) collective-permute-start(f32[4,3,256,128]{3,2,1,0:T(8,128)S(1)} %shard_map.68.own_ref), channel_id=1, source_target_pairs={{0,128},{1,129},{2,130},{3,131},{4,132},{5,133},{6,134},{7,135},{8... | collective-permute-start | bytes 4718600 | tf_op jit(solution)/shard_map/ppermute | solution.py:508
  133.2 5.3 %copy-start.7 = (pred[46]{0:T(512)(128)(4,1)S(1)}, pred[46]{0:T(512)(128)(4,1)}, u32[]{:S(2)}) copy-start(pred[46]{0:T(512)(128)(4,1)} %constant.18.clone.1) | copy-start | bytes 142
  133.2 3.2 %collective-permute-start.7 = (f32[100,16,128]{2,1,0:T(8,128)S(1)}, f32[100,16,128]{2,1,0:T(8,128)S(1)}, u32[]{:S(2)}, u32[]{:S(2)}) collective-permute-start(f32[100,16,128]{2,1,0:T(8,128)S(1)} %shard_map.73), channel_id=1, source_target_pairs={{0,128},{1,129},{2,130},{3,131},{4,132},{5,133},{6,134},{7,135},{8... | collective-permute-start | bytes 2457608 | tf_op jit(solution)/shard_map/ppermute | solution.py:516
  136.4 16.3 %copy-start.6 = (pred[16]{0:T(512)(128)(4,1)S(1)}, pred[16]{0:T(512)(128)(4,1)}, u32[]{:S(2)}) copy-start(pred[16]{0:T(512)(128)(4,1)} %constant.16.clone.1) | copy-start | bytes 52
  136.5 12.9 %collective-permute-start.8 = (f32[46,16,128]{2,1,0:T(8,128)S(1)}, f32[46,16,128]{2,1,0:T(8,128)S(1)}, u32[]{:S(2)}, u32[]{:S(2)}) collective-permute-start(f32[46,16,128]{2,1,0:T(8,128)S(1)} %add_add_fusion), channel_id=1, source_target_pairs={{0,1},{1,2},{2,3},{3,4},{4,5},{5,6},{6,7},{8,9},{9,10},{10,11},{11... | collective-permute-start | bytes 1130504 | tf_op jit(solution)/shard_map/ppermute | solution.py:531
  138.6 14.1 %collective-permute-start.9 = (f32[46,16,128]{2,1,0:T(8,128)S(1)}, f32[46,16,128]{2,1,0:T(8,128)S(1)}, u32[]{:S(2)}, u32[]{:S(2)}) collective-permute-start(f32[46,16,128]{2,1,0:T(8,128)S(1)} %fusion.2), channel_id=1, source_target_pairs={{1,0},{2,1},{3,2},{4,3},{5,4},{6,5},{7,6},{9,8},{10,9},{11,10},{12... | collective-permute-start | bytes 1130504 | tf_op jit(solution)/shard_map/ppermute | solution.py:532

commit v3 on v2

--- a/solution.py
+++ b/solution.py
@@ -135,7 +135,10 @@
     lead = 0
     for i, reach in enumerate((IN_P, IN_U, IN_V, IN_W)):
         ext.append(
-            jnp.concatenate([low_ref[lead : lead + reach], raw_ref[i], high_ref[lead : lead + reach]], axis=0)
+            jnp.concatenate(
+                [low_ref[lead : lead + reach] * low_ok, raw_ref[i], high_ref[lead : lead + reach] * high_ok],
+                axis=0,
+            )
         )
         lead += reach
 
@@ -206,6 +209,10 @@
         ):
             out_ref[lead : lead + value.shape[0]] = value
             lead += value.shape[0]
+
+    @pl.when(edge_ref[2] <= 0)
+    def _():
+        out_ref[...] = jnp.zeros(out_ref.shape, f32)
 
 
 def gather_kernel(edge_ref, back_ref, own_ref, high_ref, low_ref):
@@ -284,7 +291,7 @@
             out_ref[n, k] = start[k] + change[k]
 
 
-def source_kernel(region_ref, in_ref, held_ref, up1_ref, down1_ref, up2_ref, down2_ref, left_ref, right_ref, out_ref):
+def source_kernel(flag_ref, region_ref, in_ref, held_ref, up1_ref, down1_ref, up2_ref, down2_ref, left_ref, right_ref, out_ref):
     do = Products(left_ref, right_ref)
     nx, nz = up1_ref.shape[1:]
     row = lax.broadcasted_iota(jnp.int32, (nx, nz), 0)
@@ -301,7 +308,8 @@
         behind = jnp.where(lane == 0, 0.0, pltpu.roll(value, 1, 1))
         return 0.5 * (ahead - behind)
 
-    near = [up1_ref[n] - down1_ref[n] for n in range(3)]
+    up1, down1, up2, down2 = flag_ref[3], flag_ref[4], flag_ref[5], flag_ref[6]
+    near = [up1 * up1_ref[n] - down1 * down1_ref[n] for n in range(3)]
     half = [0.5 * value for value in near]
     pull_x = do.left("a", half)
     pull_z = do.right(half, "c")
@@ -312,7 +320,7 @@
             u, w = held_ref[n - 1, 0], held_ref[n - 1, 1]
             slope_u = held_ref[n - 1, 2] - tau * pull_x[n - 1]
             slope_w = held_ref[n - 1, 3] - tau * pull_z[n - 1]
-            far = up2_ref[n - 1] - down2_ref[n - 1]
+            far = up2 * up2_ref[n - 1] - down2 * down2_ref[n - 1]
             v = held_ref[n - 1, 4] - tau * ((2.0 / 3.0) * near[n - 1] - (1.0 / 12.0) * far)
         o_x = slope_w - slope_z(v)
         o_y = slope_z(u) - slope_x(w)
@@ -357,7 +365,7 @@
     two = do.right([source_ref[n, 2] for n in range(first, last)], "c")
     return [
         (
-            -(tau**2) * (one[n - first] + two[n - first]),
+            jnp.where(flow, 0.0, -(tau**2) * (one[n - first] + two[n - first])),
             -(tau**2) * jnp.where(flow, own_ref[n, 1], source_ref[n, 1]),
         )
         for n in range(first, last)
@@ -391,10 +399,16 @@
         out_ref[8 + k] = value
     for k, value in enumerate(chain.advance(q7, q6, drive[1], 8)):
         out_ref[k] = value
-    total = [source_ref[0, k] for k in range(3)]
+    flow = flag_ref[2] > 0
+
+    def arrived(n):
+        return [jnp.where(flow, 0.0, source_ref[n, k]) for k in range(3)]
+
+    total = arrived(0)
     for n in (1, 2, 3):
         kept = do.left("e2", total)
-        total = [total[k] + kept[k] + source_ref[n, k] for k in range(3)]
+        fresh = arrived(n)
+        total = [total[k] + kept[k] + fresh[k] for k in range(3)]
     moved = do.left("e1", total)
     begin = [plane(in_ref, i) for i in (3, 9, 10)]
     kept = do.left("e8", begin)
@@ -447,7 +461,8 @@
     def device(y):
         return order[y % streams] * slabs + y // streams
 
-    return [(device(y), device(y + steps)) for y in range(max(0, -steps), min(count, count - steps))]
+    flow = [(device(y), device((y + steps) % count)) for y in range(count)]
+    return flow + [(i, i) for i in range(count, count * lax.axis_size("section"))]
 
 
 def shards(state, source_mask, deriv_x, deriv_z, filter_x, filter_z):
@@ -455,10 +470,17 @@
     slabs, streams = lax.axis_size("slab"), lax.axis_size("stream")
     slab = lax.axis_index("slab")
     nx = xs * streams
-    upward = [(i, i + 1) for i in range(slabs - 1)]
-    downward = [(i + 1, i) for i in range(slabs - 1)]
+    upward = [(i, (i + 1) % slabs) for i in range(slabs)]
+    downward = [((i + 1) % slabs, i) for i in range(slabs)]
+    swap = [(0, 1), (1, 0)]
+    inverse = [0] * streams
+    for j, stream in enumerate(order_of(streams)):
+        inverse[stream] = j
+    y = slab * streams + jnp.asarray(inverse, jnp.int32)[lax.axis_index("stream")]
+    last_y = slabs * streams - 1
     edges = jnp.stack(
         [slab > 0, slab < slabs - 1, lax.axis_index("section") == 0]
+        + [y < last_y, y > 0, y < last_y - 1, y > 1]
     ).astype(f32)
     region = jnp.repeat(source_mask[:, 0].astype(f32), nx // source_mask.shape[0])
     region = jnp.broadcast_to(region[:, None], (nx, nz))
@@ -502,10 +524,10 @@
     sums = waves[2:5]
     near = [lax.ppermute(sums, AXES, along_y(steps)) for steps in (-1, 1, -2, 2)]
     held = call(held_kernel, shape(3, 5, nx, nz), planes, waves, left, right, flops=10**9)
-    source = call(
-        source_kernel, shape(4, 3, nx, nz), region, planes, held, *near, left, right, flops=10**9
-    )
-    moved = lax.ppermute(source, "section", [(0, 1)])
+    source = with_edges(
+        source_kernel, shape(4, 3, nx, nz), region, planes, held, *near, left, right
+    )
+    moved = lax.ppermute(source, "section", swap)
     driven = with_edges(driven_kernel, shape(12, nx, nz), waves, source, moved, left, right)
     last = with_edges(finish_kernel, shape(17, nx, nz), planes, driven, source, moved, left, right)
     done = with_edges(filter_kernel, shape(streams, SLOTS, xs, nz), last, left, right)
@@ -513,7 +535,7 @@
     border = OUT_P + OUT_U + OUT_V + OUT_W
     rows = ((OUT_P, 0), (OUT_U, 1), (2, 3))
     odd = with_edges(gather_odd_kernel, shape(sum(own + 2 * reach for reach, _ in rows), xs, nz), back)
-    odd = lax.ppermute(odd, "section", [(0, 1)])
+    odd = lax.ppermute(odd, "section", swap)
     mine, high, low = with_edges(
         gather_kernel, (shape(4, own, xs, nz), shape(border, xs, nz), shape(border, xs, nz)), back
     )

time: 155 us -> 147 us (0.948)
  starting transfers between devices: 31.9 us -> 22.2 us
    ppermute x2, starting transfers between devices: 2.91 us -> 0.59 us  [the longest x1 0.31 us: shards(): odd = lax.ppermute(odd, 'section', swap)]
    pallas_call x6 -> x7, Pallas kernels: 15.6 us -> 17.9 us  [with_edges(): pl.pallas_call(body, out_shape=out_shape, in_specs=[pl.BlockSpec(memory_s...]
    pallas_call x4 -> x3, Pallas kernels: 7.99 us -> 5.86 us  [call(): pl.pallas_call(body, out_shape=out_shape, scratch_shapes=scratch, compile...]
    ppermute x1, starting transfers between devices: 3.94 us -> 2.08 us  [shards(): from_high = lax.ppermute(low + sum(more_low), 'slab', downward)]
    ppermute x1, waiting for transfers between devices: 5.36 us -> 3.51 us  [shards(): lax.ppermute(jnp.concatenate([raw[i, :reach] for i, reach in enumerate(re...]
    ppermute x1, starting transfers between devices: 1.92 us -> 0.08 us  [shards(): from_low = lax.ppermute(high + sum(more_high), 'slab', upward)]
    ppermute x1, waiting for transfers between devices: 3.24 us -> 1.4 us  [shards(): from_high = lax.ppermute(low + sum(more_low), 'slab', downward)]
    ppermute x1, starting transfers between devices: 1.92 us -> 0.08 us  [shards(): lax.ppermute(jnp.concatenate([raw[i, :reach] for i, reach in enumerate(re...]
  transfers between devices with their start and end apart: 10 -> 10, of which waited for: 8 -> 8; matrix products, arithmetic and copies ran while one was open for 0% -> 1% of each run, Pallas kernels for 3% -> 3%
where the time goes in v3:
time: 147 us; the launch traced here: 146 us
  blocking collectives  70 us (48%)
  Pallas kernels  23.8 us (16%)
  starting transfers between devices  22.2 us (15%)
  waiting for transfers between devices  21.9 us (15%)
  local copies, waits for them, and re-layouts  6.42 us (4%)
    all_to_all x1, blocking collectives, shards(): lax.all_to_all(done, 'stream', split_axis=0, concat_axis=0, tiled=True)  40.2 us
    all_to_all x1, blocking collectives, shards(): lax.all_to_all(spread, 'stream', split_axis=0, concat_axis=0, tiled=True)  29.8 us
    pallas_call x7, Pallas kernels, with_edges(): pl.pallas_call(body, out_shape=out_shape, in_specs=[pl.BlockSpec(memory_s...  17.9 us
    ppermute x4, starting transfers between devices, shards(): lax.ppermute(sums, AXES, along_y(steps))  16.2 us
    ppermute x1, waiting for transfers between devices, shards(): from_low = lax.ppermute(high + sum(more_high), 'slab', upward)  8.58 us
    pallas_call x3, Pallas kernels, call(): pl.pallas_call(body, out_shape=out_shape, scratch_shapes=scratch, compile...  5.86 us
    unnamed x23, local copies, waits for them, and re-layouts  3.61 us
    ppermute x1, waiting for transfers between devices, shards(): lax.ppermute(jnp.concatenate([raw[i, :reach] for i, reach in enumerate(re...  3.51 us
  transfers between devices with their start and end apart: 10, of which 8 were waited for; matrix products, arithmetic and copies ran while one was open for 1% of the time, Pallas kernels for 3%

profile of v3, /device:TPU:96, one launch (start us, length us, event | category | flops | bytes accessed | tf_op | source)
XLA Modules:
  0.0 145.6 jit_solution(11477221176531528309)
XLA Ops:
  0.0 1.3 copy.13
  1.4 3.2 %collective-permute-start = (f32[34,16,128]{2,1,0:T(8,128)S(1)}, f32[34,16,128]{2,1,0:T(8,128)S(1)}, u32[]{:S(2)}, u32[]{:S(2)}) collective-permute-start(f32[34,16,128]{2,1,0:T(8,128)S(1)} %pad_maximum_fusion), channel_id=1, source_target_pairs={{0,1},{1,2},{2,3},{3,4},{4,5},{5,6},{6,7},{7,0},{8,9},{9,10},{10,1... | collective-permute-start | bytes 835592 | tf_op jit(solution)/shard_map/ppermute | solution.py:490
  6.3 1.9 %shard_map.73 = (bf16[10,256,768]{2,1,0:T(8,128)(2,1)S(1)}, bf16[3,384,128]{2,1,0:T(8,128)(2,1)S(1)}) custom-call(f32[256,256]{1,0:T(8,128)S(1)} %copy-done.2, f32[128,128]{1,0:T(8,128)S(1)} %bitcast.60, f32[256,256]{1,0:T(8,128)S(1)} %copy-done.3, f32[128,128]{1,0:T(8,128)S(1)} %bitcast.61), custom_call_target="tpu_custom_call" | custom-call | flops 1000000000 | bytes 655360 | tf_op jit(solution)/shard_map/pallas_call | solution.py:24
  8.2 2.3 %collective-permute-done.low_ref = f32[34,16,128]{2,1,0:T(8,128)S(1)} collective-permute-done((f32[34,16,128]{2,1,0:T(8,128)S(1)}, f32[34,16,128]{2,1,0:T(8,128)S(1)}, u32[]{:S(2)}, u32[]{:S(2)}) %collective-permute-start) | collective-permute-done | bytes 278560 | tf_op jit(solution)/shard_map/ppermute | solution.py:490
  10.5 3.5 %collective-permute-done.1.high_ref = f32[34,16,128]{2,1,0:T(8,128)S(1)} collective-permute-done((f32[34,16,128]{2,1,0:T(8,128)S(1)}, f32[34,16,128]{2,1,0:T(8,128)S(1)}, u32[]{:S(2)}, u32[]{:S(2)}) %collective-permute-start.1) | collective-permute-done | bytes 278560 | tf_op jit(solution)/shard_map/ppermute | solution.py:493
  15.3 29.8 %all_to_all.10.in_ref = f32[16,13,16,128]{3,2,1,0:T(8,128)S(1)} all-to-all(f32[16,13,16,128]{3,2,1,0:T(8,128)S(1)} %shard_map.74), channel_id=1, replica_groups=mesh['section'=2,'stream'=16,'slab'=8] {'stream'}, dimensions={0} | all-to-all | bytes 3407872 | tf_op jit(solution)/shard_map/all_to_all | solution.py:522
  45.1 2.5 %shard_map.75.waves_ref = f32[5,256,128]{2,1,0:T(8,128)S(1)} custom-call(f32[16,13,16,128]{3,2,1,0:T(8,128)S(1)} %all_to_all.10.in_ref, bf16[10,256,768]{2,1,0:T(8,128)(2,1)S(1)} %get-tuple-element.11.left_ref, bf16[3,384,128]{2,1,0:T(8,128)(2,1)S(1)} %get-tuple-element.10.right_ref), custom_call_target="tpu_custom_call" | custom-call | flops 2000000000 | bytes 5931008 | tf_op jit(solution)/shard_map/pallas_call | solution.py:24
  48.4 2.4 %collective-permute-start.5 = (f32[3,256,128]{2,1,0:T(8,128)}, f32[3,256,128]{2,1,0:T(8,128)S(1)}, u32[]{:S(2)}, u32[]{:S(2)}) collective-permute-start(f32[3,256,128]{2,1,0:T(8,128)} %slice.142), channel_id=1, source_target_pairs={{0,8},{32,40},{8,16},{40,48},{16,24},{48,56},{24,120},{56,88},{120... | collective-permute-start | bytes 1179656 | tf_op jit(solution)/shard_map/ppermute | solution.py:525
  50.8 5.6 %collective-permute-start.4 = (f32[3,256,128]{2,1,0:T(8,128)}, f32[3,256,128]{2,1,0:T(8,128)S(1)}, u32[]{:S(2)}, u32[]{:S(2)}) collective-permute-start(f32[3,256,128]{2,1,0:T(8,128)} %slice.142), channel_id=1, source_target_pairs={{0,103},{32,71},{8,0},{40,32},{16,8},{48,40},{24,16},{56,48},{120,... | collective-permute-start | bytes 1179656 | tf_op jit(solution)/shard_map/ppermute | solution.py:525
  56.3 1.9 %collective-permute-start.3 = (f32[3,256,128]{2,1,0:T(8,128)}, f32[3,256,128]{2,1,0:T(8,128)}, u32[]{:S(2)}, u32[]{:S(2)}) collective-permute-start(f32[3,256,128]{2,1,0:T(8,128)} %slice.142), channel_id=1, source_target_pairs={{0,32},{32,8},{8,40},{40,16},{16,48},{48,24},{24,56},{56,120},{120... | collective-permute-start | bytes 1179656 | tf_op jit(solution)/shard_map/ppermute | solution.py:525
  58.3 6.3 %collective-permute-start.2 = (f32[3,256,128]{2,1,0:T(8,128)}, f32[3,256,128]{2,1,0:T(8,128)}, u32[]{:S(2)}, u32[]{:S(2)}) collective-permute-start(f32[3,256,128]{2,1,0:T(8,128)} %slice.142), channel_id=1, source_target_pairs={{0,71},{32,0},{8,32},{40,8},{16,40},{48,16},{24,48},{56,24},{120,5... | collective-permute-start | bytes 1179656 | tf_op jit(solution)/shard_map/ppermute | solution.py:525
  64.8 2.1 %copy-done.1 = bf16[10,256,768]{2,1,0:T(8,128)(2,1)S(1)} copy-done((bf16[10,256,768]{2,1,0:T(8,128)(2,1)S(1)}, bf16[10,256,768]{2,1,0:T(8,128)(2,1)}, u32[]{:S(2)}) %copy-start.1) | copy-done | bytes 3932184
  66.9 1.4 shard_map.76.held_ref
  68.8 1.4 collective-permute-done.2.up1_ref
  70.3 2.3 %shard_map.77.own_ref = f32[4,3,256,128]{3,2,1,0:T(8,128)S(1)} custom-call(f32[7]{0:T(128)S(1)} %convert_element_type.33.edge_ref.flag_ref, f32[256,128]{1,0:T(8,128)S(1)} %broadcast_in_dim.15.region_ref, f32[16,13,16,128]{3,2,1,0:T(8,128)S(1)} %all_to_all.10.in_ref, f32[3,5,256,128]{3,2,1,0:T(8,128)S(1)} %shard_map.76.held_ref, ...), custom_call_target="tpu_custom_call" | custom-call | tf_op jit(solution)/shard_map/pallas_call | solution.py:513
  72.9 3.4 %collective-permute-done.6.source_ref = f32[4,3,256,128]{3,2,1,0:T(8,128)S(1)} collective-permute-done((f32[4,3,256,128]{3,2,1,0:T(8,128)S(1)}, f32[4,3,256,128]{3,2,1,0:T(8,128)S(1)}, u32[]{:S(2)}, u32[]{:S(2)}) %collective-permute-start.6) | collective-permute-done | bytes 1572896 | tf_op jit(solution)/shard_map/ppermute | solution.py:530
  76.3 2.8 %shard_map.78.driven_ref = f32[12,256,128]{2,1,0:T(8,128)S(1)} custom-call(f32[7]{0:T(128)S(1)} %convert_element_type.33.edge_ref.flag_ref, f32[5,256,128]{2,1,0:T(8,128)S(1)} %shard_map.75.waves_ref, f32[4,3,256,128]{3,2,1,0:T(8,128)S(1)} %shard_map.77.own_ref, f32[4,3,256,128]{3,2,1,0:T(8,128)S(1)} %collective-permute-done.6.source_ref, ...), custom_call_target="tpu_custom_call" | custom-call | tf_op jit(solution)/shard_map/pallas_call | solution.py:513
  79.0 5.6 %shard_map.79.last_ref = f32[17,256,128]{2,1,0:T(8,128)S(1)} custom-call(f32[7]{0:T(128)S(1)} %convert_element_type.33.edge_ref.flag_ref, f32[16,13,16,128]{3,2,1,0:T(8,128)S(1)} %all_to_all.10.in_ref, f32[12,256,128]{2,1,0:T(8,128)S(1)} %shard_map.78.driven_ref, f32[4,3,256,128]{3,2,1,0:T(8,128)S(1)} %shard_map.77.own_ref, ...), custom_call_target="tpu_custom_call" | custom-call | tf_op jit(solution)/shard_map/pallas_call | solution.py:513
  84.7 3.4 %shard_map.80 = f32[16,19,16,128]{3,2,1,0:T(8,128)S(1)} custom-call(f32[7]{0:T(128)S(1)} %convert_element_type.33.edge_ref.flag_ref, f32[17,256,128]{2,1,0:T(8,128)S(1)} %shard_map.79.last_ref, bf16[10,256,768]{2,1,0:T(8,128)(2,1)S(1)} %copy-done.1, bf16[3,384,128]{2,1,0:T(8,128)(2,1)S(1)} %get-tuple-element.10.right_ref), custom_call_target="tpu_custom_call" | custom-call | tf_op jit(solution)/shard_map/pallas_call | solution.py:513
  88.1 40.2 %all_to_all.11.back_ref = f32[16,19,16,128]{3,2,1,0:T(8,128)S(1)} all-to-all(f32[16,19,16,128]{3,2,1,0:T(8,128)S(1)} %shard_map.80), channel_id=1, replica_groups=mesh['section'=2,'stream'=16,'slab'=8] {'stream'}, dimensions={0} | all-to-all | bytes 4980736 | tf_op jit(solution)/shard_map/all_to_all | solution.py:534
  129.7 1.5 %shard_map.81 = (f32[4,16,16,128]{3,2,1,0:T(8,128)S(1)}, f32[46,16,128]{2,1,0:T(8,128)S(1)}, f32[46,16,128]{2,1,0:T(8,128)S(1)}) custom-call(f32[7]{0:T(128)S(1)} %convert_element_type.33.edge_ref.flag_ref, f32[16,19,16,128]{3,2,1,0:T(8,128)S(1)} %all_to_all.11.back_ref), custom_call_target="tpu_custom_call" | custom-call | tf_op jit(solution)/shard_map/pallas_call | solution.py:513
  132.4 2.1 %collective-permute-start.9 = (f32[46,16,128]{2,1,0:T(8,128)S(1)}, f32[46,16,128]{2,1,0:T(8,128)S(1)}, u32[]{:S(2)}, u32[]{:S(2)}) collective-permute-start(f32[46,16,128]{2,1,0:T(8,128)S(1)} %fusion.2), channel_id=1, source_target_pairs={{1,0},{2,1},{3,2},{4,3},{5,4},{6,5},{7,6},{0,7},{9,8},{10,9},{11,1... | collective-permute-start | bytes 1130504 | tf_op jit(solution)/shard_map/ppermute | solution.py:554
  134.4 8.6 %collective-permute-done.8 = f32[46,16,128]{2,1,0:T(8,128)S(1)} collective-permute-done((f32[46,16,128]{2,1,0:T(8,128)S(1)}, f32[46,16,128]{2,1,0:T(8,128)S(1)}, u32[]{:S(2)}, u32[]{:S(2)}) %collective-permute-start.8) | collective-permute-done | bytes 376864 | tf_op jit(solution)/shard_map/ppermute | solution.py:553
  143.1 1.4 collective-permute-done.9
  (56 shorter events, 7.8 us)
Async XLA Ops:
  0.0 4.7 %copy-start.9 = (s32[16]{0:T(128)S(1)}, s32[16]{0:T(128)}, u32[]{:S(2)}) copy-start(s32[16]{0:T(128)} %constant.34.clone) | copy-start | bytes 196
  0.0 6.1 %copy-start.4 = (f32[128,128]{1,0:T(8,128)S(1)}, f32[128,128]{1,0:T(8,128)}, u32[]{:S(2)}) copy-start(f32[128,128]{1,0:T(8,128)} %param.10) | copy-start | bytes 196612
  0.0 6.2 %copy-start.5 = (f32[128,128]{1,0:T(8,128)S(1)}, f32[128,128]{1,0:T(8,128)}, u32[]{:S(2)}) copy-start(f32[128,128]{1,0:T(8,128)} %param.12) | copy-start | bytes 196612
  0.0 6.3 %copy-start.3 = (f32[256,256]{1,0:T(8,128)S(1)}, f32[256,256]{1,0:T(8,128)}, u32[]{:S(2)}) copy-start(f32[256,256]{1,0:T(8,128)} %fx_ref.1) | copy-start | bytes 786436
  0.0 6.3 %copy-start.2 = (f32[256,256]{1,0:T(8,128)S(1)}, f32[256,256]{1,0:T(8,128)}, u32[]{:S(2)}) copy-start(f32[256,256]{1,0:T(8,128)} %dx_ref.1) | copy-start | bytes 786436
  1.4 9.1 %collective-permute-start = (f32[34,16,128]{2,1,0:T(8,128)S(1)}, f32[34,16,128]{2,1,0:T(8,128)S(1)}, u32[]{:S(2)}, u32[]{:S(2)}) collective-permute-start(f32[34,16,128]{2,1,0:T(8,128)S(1)} %pad_maximum_fusion), channel_id=1, source_target_pairs={{0,1},{1,2},{2,3},{3,4},{4,5},{5,6},{6,7},{7,0},{8,9},{9,10},{10,1... | collective-permute-start | bytes 835592 | tf_op jit(solution)/shard_map/ppermute | solution.py:490
  4.6 9.4 %collective-permute-start.1 = (f32[34,16,128]{2,1,0:T(8,128)S(1)}, f32[34,16,128]{2,1,0:T(8,128)S(1)}, u32[]{:S(2)}, u32[]{:S(2)}) collective-permute-start(f32[34,16,128]{2,1,0:T(8,128)S(1)} %pad_maximum_fusion.1), channel_id=1, source_target_pairs={{1,0},{2,1},{3,2},{4,3},{5,4},{6,5},{7,6},{0,7},{9,8},{10,9},{11,1... | collective-permute-start | bytes 835592 | tf_op jit(solution)/shard_map/ppermute | solution.py:493
  8.2 36.9 %copy-start = (bf16[10,256,768]{2,1,0:T(8,128)(2,1)}, bf16[10,256,768]{2,1,0:T(8,128)(2,1)S(1)}, u32[]{:S(2)}) copy-start(bf16[10,256,768]{2,1,0:T(8,128)(2,1)S(1)} %get-tuple-element.11.left_ref) | copy-start | bytes 11796484
  45.1 19.5 %copy-start.8 = (s32[16,1]{0,1:T(1,128)S(1)}, s32[16,1]{0,1:T(1,128)}, u32[]{:S(2)}) copy-start(s32[16,1]{0,1:T(1,128)} %param.8) | copy-start | bytes 196
  48.4 20.0 %collective-permute-start.5 = (f32[3,256,128]{2,1,0:T(8,128)}, f32[3,256,128]{2,1,0:T(8,128)S(1)}, u32[]{:S(2)}, u32[]{:S(2)}) collective-permute-start(f32[3,256,128]{2,1,0:T(8,128)} %slice.142), channel_id=1, source_target_pairs={{0,8},{32,40},{8,16},{40,48},{16,24},{48,56},{24,120},{56,88},{120... | collective-permute-start | bytes 1179656 | tf_op jit(solution)/shard_map/ppermute | solution.py:525
  50.8 17.6 %collective-permute-start.4 = (f32[3,256,128]{2,1,0:T(8,128)}, f32[3,256,128]{2,1,0:T(8,128)S(1)}, u32[]{:S(2)}, u32[]{:S(2)}) collective-permute-start(f32[3,256,128]{2,1,0:T(8,128)} %slice.142), channel_id=1, source_target_pairs={{0,103},{32,71},{8,0},{40,32},{16,8},{48,40},{24,16},{56,48},{120,... | collective-permute-start | bytes 1179656 | tf_op jit(solution)/shard_map/ppermute | solution.py:525
  56.3 12.5 %collective-permute-start.3 = (f32[3,256,128]{2,1,0:T(8,128)}, f32[3,256,128]{2,1,0:T(8,128)}, u32[]{:S(2)}, u32[]{:S(2)}) collective-permute-start(f32[3,256,128]{2,1,0:T(8,128)} %slice.142), channel_id=1, source_target_pairs={{0,32},{32,8},{8,40},{40,16},{16,48},{48,24},{24,56},{56,120},{120... | collective-permute-start | bytes 1179656 | tf_op jit(solution)/shard_map/ppermute | solution.py:525
  58.3 11.9 %collective-permute-start.2 = (f32[3,256,128]{2,1,0:T(8,128)}, f32[3,256,128]{2,1,0:T(8,128)}, u32[]{:S(2)}, u32[]{:S(2)}) collective-permute-start(f32[3,256,128]{2,1,0:T(8,128)} %slice.142), channel_id=1, source_target_pairs={{0,71},{32,0},{8,32},{40,8},{16,40},{48,16},{24,48},{56,24},{120,5... | collective-permute-start | bytes 1179656 | tf_op jit(solution)/shard_map/ppermute | solution.py:525
  64.8 2.1 %copy-start.1 = (bf16[10,256,768]{2,1,0:T(8,128)(2,1)S(1)}, bf16[10,256,768]{2,1,0:T(8,128)(2,1)}, u32[]{:S(2)}) copy-start(bf16[10,256,768]{2,1,0:T(8,128)(2,1)} %copy-done) | copy-start | bytes 11796484
  72.6 3.7 %collective-permute-start.6 = (f32[4,3,256,128]{3,2,1,0:T(8,128)S(1)}, f32[4,3,256,128]{3,2,1,0:T(8,128)S(1)}, u32[]{:S(2)}, u32[]{:S(2)}) collective-permute-start(f32[4,3,256,128]{3,2,1,0:T(8,128)S(1)} %shard_map.77.own_ref), channel_id=1, source_target_pairs={{0,128},{128,0},{1,129},{129,1},{2,130},{130,2},{3,131},{131,3},{4... | collective-permute-start | bytes 4718600 | tf_op jit(solution)/shard_map/ppermute | solution.py:530
  129.4 2.8 %copy-start.7 = (pred[46]{0:T(512)(128)(4,1)S(1)}, pred[46]{0:T(512)(128)(4,1)}, u32[]{:S(2)}) copy-start(pred[46]{0:T(512)(128)(4,1)} %constant.33.clone.1) | copy-start | bytes 142
  129.4 2.6 %collective-permute-start.7 = (f32[100,16,128]{2,1,0:T(8,128)S(1)}, f32[100,16,128]{2,1,0:T(8,128)S(1)}, u32[]{:S(2)}, u32[]{:S(2)}) collective-permute-start(f32[100,16,128]{2,1,0:T(8,128)S(1)} %shard_map.82), channel_id=1, source_target_pairs={{0,128},{128,0},{1,129},{129,1},{2,130},{130,2},{3,131},{131,3},{4... | collective-permute-start | bytes 2457608 | tf_op jit(solution)/shard_map/ppermute | solution.py:538
  132.1 12.5 %copy-start.6 = (pred[16]{0:T(512)(128)(4,1)S(1)}, pred[16]{0:T(512)(128)(4,1)}, u32[]{:S(2)}) copy-start(pred[16]{0:T(512)(128)(4,1)} %constant.31.clone.1) | copy-start | bytes 52
  132.1 10.9 %collective-permute-start.8 = (f32[46,16,128]{2,1,0:T(8,128)S(1)}, f32[46,16,128]{2,1,0:T(8,128)S(1)}, u32[]{:S(2)}, u32[]{:S(2)}) collective-permute-start(f32[46,16,128]{2,1,0:T(8,128)S(1)} %add_add_fusion), channel_id=1, source_target_pairs={{0,1},{1,2},{2,3},{3,4},{4,5},{5,6},{6,7},{7,0},{8,9},{9,10},{10,1... | collective-permute-start | bytes 1130504 | tf_op jit(solution)/shard_map/ppermute | solution.py:553
  132.4 12.1 %collective-permute-start.9 = (f32[46,16,128]{2,1,0:T(8,128)S(1)}, f32[46,16,128]{2,1,0:T(8,128)S(1)}, u32[]{:S(2)}, u32[]{:S(2)}) collective-permute-start(f32[46,16,128]{2,1,0:T(8,128)S(1)} %fusion.2), channel_id=1, source_target_pairs={{1,0},{2,1},{3,2},{4,3},{5,4},{6,5},{7,6},{0,7},{9,8},{10,9},{11,1... | collective-permute-start | bytes 1130504 | tf_op jit(solution)/shard_map/ppermute | solution.py:554

commit v4 on v3

--- a/solution.py
+++ b/solution.py
@@ -127,6 +127,20 @@
     return (2.0 / 3.0) * near - (1.0 / 12.0) * far
 
 
+def turn_kernel(state_ref, raw_ref, first_ref, top_ref, bottom_ref):
+    own = state_ref.shape[2]
+    order = order_of(own)
+    lead = 0
+    for i, reach in enumerate((IN_P, IN_U, IN_V, IN_W)):
+        turned = jnp.swapaxes(state_ref[i], 0, 1)
+        raw_ref[i] = turned
+        for j in range(own):
+            first_ref[order[j], i] = turned[j]
+        top_ref[lead : lead + reach] = turned[own - reach :]
+        bottom_ref[lead : lead + reach] = turned[:reach]
+        lead += reach
+
+
 def spread_kernel(edge_ref, raw_ref, low_ref, high_ref, right_ref, out_ref):
     low_ok, high_ok = edge_ref[0], edge_ref[1]
     own, xs, nz = raw_ref.shape[1:]
@@ -147,9 +161,11 @@
         return inside(slope4(once), IN_P, low_ok, high_ok)
 
     def put(place, value):
-        reach = (value.shape[0] - own) // 2
-        for j in range(own):
-            out_ref[order[j], place] = value[reach + j]
+        which, place = PLACES[place]
+        if which == 1:
+            reach = (value.shape[0] - own) // 2
+            for j in range(own):
+                out_ref[order[j], place] = value[reach + j]
 
     def slope2(value):
         return 0.5 * (value[IN_P + 1 : IN_P + 1 + own] - value[IN_P - 1 : IN_P - 1 + own])
@@ -164,8 +180,6 @@
         value = twice(value)
         put(place + 1, value)
         put(place + 2, twice(value))
-    put(9, raw_ref[2])
-    put(10, raw_ref[3])
     put(11, slope2(ext[1]))
     put(12, slope2(ext[3]))
 
@@ -240,15 +254,19 @@
         place += room
 
 
-def plane(ref, index):
-    blocks, _, xs, nz = ref.shape
-    return ref[:, index].reshape(blocks * xs, nz)
-
-
-def waves_kernel(in_ref, left_ref, right_ref, out_ref):
+PLACES = ((0, 0), (1, 0), (1, 1), (0, 1), (1, 2), (1, 3), (1, 4), (1, 5), (1, 6), (0, 2), (0, 3), (1, 7), (1, 8))
+
+
+def plane(refs, index):
+    which, place = PLACES[index]
+    blocks, _, xs, nz = refs[which].shape
+    return refs[which][:, place].reshape(blocks * xs, nz)
+
+
+def waves_kernel(raw_ref, more_ref, left_ref, right_ref, out_ref):
     do = Products(left_ref, right_ref)
-    p0 = [plane(in_ref, i) for i in range(3)]
-    u0 = [plane(in_ref, 3 + i) for i in range(3)]
+    p0 = [plane((raw_ref, more_ref), i) for i in range(3)]
+    u0 = [plane((raw_ref, more_ref), 3 + i) for i in range(3)]
 
     def advance(now, before):
         count = len(before) - 1
@@ -262,7 +280,7 @@
 
     moved = do.left("e1", p0)
     driven = do.left("ta", u0)
-    p1 = [p0[i] + (moved[i] + driven[i] - tau * plane(in_ref, 6 + i)) for i in range(3)]
+    p1 = [p0[i] + (moved[i] + driven[i] - tau * plane((raw_ref, more_ref), 6 + i)) for i in range(3)]
     h2 = p0[0] + moved[0] + p1[0]
     out_ref[2] = h2
     p2 = advance(p1, p0)
@@ -277,9 +295,9 @@
     out_ref[4] = h6
 
 
-def held_kernel(in_ref, waves_ref, left_ref, right_ref, out_ref):
+def held_kernel(raw_ref, more_ref, waves_ref, left_ref, right_ref, out_ref):
     do = Products(left_ref, right_ref)
-    start = [plane(in_ref, i) for i in (3, 10, 11, 12, 9)]
+    start = [plane((raw_ref, more_ref), i) for i in (3, 10, 11, 12, 9)]
     h = [waves_ref[2 + n] for n in range(3)]
     pull_x = do.left("a", h)
     pull_z = do.right(h, "c")
@@ -291,7 +309,7 @@
             out_ref[n, k] = start[k] + change[k]
 
 
-def source_kernel(flag_ref, region_ref, in_ref, held_ref, up1_ref, down1_ref, up2_ref, down2_ref, left_ref, right_ref, out_ref):
+def source_kernel(flag_ref, region_ref, raw_ref, more_ref, held_ref, up1_ref, down1_ref, up2_ref, down2_ref, left_ref, right_ref, out_ref):
     do = Products(left_ref, right_ref)
     nx, nz = up1_ref.shape[1:]
     row = lax.broadcasted_iota(jnp.int32, (nx, nz), 0)
@@ -315,7 +333,7 @@
     pull_z = do.right(half, "c")
     for n in range(4):
         if n == 0:
-            u, w, slope_u, slope_w, v = [plane(in_ref, i) for i in (3, 10, 11, 12, 9)]
+            u, w, slope_u, slope_w, v = [plane((raw_ref, more_ref), i) for i in (3, 10, 11, 12, 9)]
         else:
             u, w = held_ref[n - 1, 0], held_ref[n - 1, 1]
             slope_u = held_ref[n - 1, 2] - tau * pull_x[n - 1]
@@ -388,7 +406,7 @@
             out_ref[first + k] = values[k]
 
 
-def finish_kernel(flag_ref, in_ref, driven_ref, own_ref, source_ref, left_ref, right_ref, out_ref):
+def finish_kernel(flag_ref, raw_ref, more_ref, driven_ref, own_ref, source_ref, left_ref, right_ref, out_ref):
     chain = Chain(left_ref, right_ref)
     do = chain.do
     drive = drives(do, flag_ref, own_ref, source_ref, 2, 4)
@@ -410,7 +428,7 @@
         fresh = arrived(n)
         total = [total[k] + kept[k] + fresh[k] for k in range(3)]
     moved = do.left("e1", total)
-    begin = [plane(in_ref, i) for i in (3, 9, 10)]
+    begin = [plane((raw_ref, more_ref), i) for i in (3, 9, 10)]
     kept = do.left("e8", begin)
     for i in range(3):
         out_ref[14 + i] = begin[i] + kept[i] + tau * (2.0 * total[i] + moved[i])
@@ -485,14 +503,18 @@
     region = jnp.repeat(source_mask[:, 0].astype(f32), nx // source_mask.shape[0])
     region = jnp.broadcast_to(region[:, None], (nx, nz))
 
-    raw = jnp.swapaxes(state[0], 1, 2)
-    reaches = (IN_P, IN_U, IN_V, IN_W)
-    from_low = lax.ppermute(
-        jnp.concatenate([raw[i, own - reach :] for i, reach in enumerate(reaches)]), "slab", upward
+    def shape(*dims):
+        return jax.ShapeDtypeStruct(dims, f32)
+
+    border = IN_P + IN_U + IN_V + IN_W
+    raw, ordered, top, bottom = call(
+        turn_kernel,
+        (shape(4, own, xs, nz), shape(streams, 4, xs, nz), shape(border, xs, nz), shape(border, xs, nz)),
+        state[0],
     )
-    from_high = lax.ppermute(
-        jnp.concatenate([raw[i, :reach] for i, reach in enumerate(reaches)]), "slab", downward
-    )
+    from_low = lax.ppermute(top, "slab", upward)
+    from_high = lax.ppermute(bottom, "slab", downward)
+    first = lax.all_to_all(ordered, "stream", split_axis=0, concat_axis=0, tiled=True)
     left, right = call(
         prepare_kernel,
         (
@@ -506,9 +528,6 @@
         flops=10**9,
     )
 
-    def shape(*dims):
-        return jax.ShapeDtypeStruct(dims, f32)
-
     def with_edges(body, out_shape, *args):
         return pl.pallas_call(
             body,
@@ -518,18 +537,18 @@
             compiler_params=pltpu.CompilerParams(vmem_limit_bytes=40 * 2**20),
         )(edges, *args)
 
-    spread = with_edges(spread_kernel, shape(own, 13, xs, nz), raw, from_low, from_high, right)
-    planes = lax.all_to_all(spread, "stream", split_axis=0, concat_axis=0, tiled=True)
-    waves = call(waves_kernel, shape(5, nx, nz), planes, left, right, flops=2 * 10**9)
+    spread = with_edges(spread_kernel, shape(own, 9, xs, nz), raw, from_low, from_high, right)
+    planes = (first, lax.all_to_all(spread, "stream", split_axis=0, concat_axis=0, tiled=True))
+    waves = call(waves_kernel, shape(5, nx, nz), *planes, left, right, flops=2 * 10**9)
     sums = waves[2:5]
     near = [lax.ppermute(sums, AXES, along_y(steps)) for steps in (-1, 1, -2, 2)]
-    held = call(held_kernel, shape(3, 5, nx, nz), planes, waves, left, right, flops=10**9)
+    held = call(held_kernel, shape(3, 5, nx, nz), *planes, waves, left, right, flops=10**9)
     source = with_edges(
-        source_kernel, shape(4, 3, nx, nz), region, planes, held, *near, left, right
+        source_kernel, shape(4, 3, nx, nz), region, *planes, held, *near, left, right
     )
     moved = lax.ppermute(source, "section", swap)
     driven = with_edges(driven_kernel, shape(12, nx, nz), waves, source, moved, left, right)
-    last = with_edges(finish_kernel, shape(17, nx, nz), planes, driven, source, moved, left, right)
+    last = with_edges(finish_kernel, shape(17, nx, nz), *planes, driven, source, moved, left, right)
     done = with_edges(filter_kernel, shape(streams, SLOTS, xs, nz), last, left, right)
     back = lax.all_to_all(done, "stream", split_axis=0, concat_axis=0, tiled=True)
     border = OUT_P + OUT_U + OUT_V + OUT_W

time: 147 us -> 155 us (1.054)
  local copies, waits for them, and re-layouts: 6.42 us -> 14.4 us
  starting transfers between devices: 22.2 us -> 29.2 us
  waiting for transfers between devices: 21.9 us -> 16.1 us
  blocking collectives: 70 us -> 67.2 us
    unnamed x23 -> x20, local copies, waits for them, and re-layouts: 3.61 us -> 10.9 us
    all_to_all x0 -> x1, starting transfers between devices: none -> 7.03 us  [shards(): lax.all_to_all(ordered, 'stream', split_axis=0, concat_axis=0, tiled=True)]
    ppermute x2, waiting for transfers between devices: 5.81 us -> 0.01 us  [the longest x1 0.01 us: shards(): from_low = lax.ppermute(top, 'slab', upward)]
    all_to_all x1, blocking collectives: 29.8 us -> 24.5 us  [shards(): lax.all_to_all(spread, 'stream', split_axis=0, concat_axis=0, tiled=True)]
    all_to_all x1, blocking collectives: 40.2 us -> 42.8 us  [shards(): lax.all_to_all(done, 'stream', split_axis=0, concat_axis=0, tiled=True)]
    pallas_call x3 -> x4, Pallas kernels: 5.86 us -> 6.77 us  [call(): pl.pallas_call(body, out_shape=out_shape, scratch_shapes=scratch, compile...]
  transfers between devices with their start and end apart: 10 -> 11, of which waited for: 8 -> 6; matrix products, arithmetic and copies ran while one was open for 1% -> 2% of each run, Pallas kernels for 3% -> 4%
where the time goes in v4:
time: 155 us; the launch traced here: 153 us
  blocking collectives  67.2 us (43%)
  starting transfers between devices  29.2 us (19%)
  Pallas kernels  24.7 us (16%)
  waiting for transfers between devices  16.1 us (10%)
  local copies, waits for them, and re-layouts  14.4 us (9%)
    all_to_all x1, blocking collectives, shards(): lax.all_to_all(done, 'stream', split_axis=0, concat_axis=0, tiled=True)  42.8 us
    all_to_all x1, blocking collectives, shards(): lax.all_to_all(spread, 'stream', split_axis=0, concat_axis=0, tiled=True)  24.5 us
    pallas_call x7, Pallas kernels, with_edges(): pl.pallas_call(body, out_shape=out_shape, in_specs=[pl.BlockSpec(memory_s...  17.9 us
    ppermute x4, starting transfers between devices, shards(): lax.ppermute(sums, AXES, along_y(steps))  16.2 us
    unnamed x20, local copies, waits for them, and re-layouts  10.9 us
    ppermute x1, waiting for transfers between devices, shards(): from_low = lax.ppermute(high + sum(more_high), 'slab', upward)  8.58 us
    all_to_all x1, starting transfers between devices, shards(): lax.all_to_all(ordered, 'stream', split_axis=0, concat_axis=0, tiled=True)  7.03 us
    pallas_call x4, Pallas kernels, call(): pl.pallas_call(body, out_shape=out_shape, scratch_shapes=scratch, compile...  6.77 us
  transfers between devices with their start and end apart: 11, of which 6 were waited for; matrix products, arithmetic and copies ran while one was open for 2% of the time, Pallas kernels for 4%

profile of v4, /device:TPU:96, one launch (start us, length us, event | category | flops | bytes accessed | tf_op | source)
XLA Modules:
  0.0 152.9 jit_solution(2481555589335814061)
XLA Ops:
  2.0 7.0 %all-to-all-start = ((f32[16,4,16,128]{3,2,1,0:T(8,128)}), f32[16,4,16,128]{3,2,1,0:T(8,128)S(1)}, u32[]{:S(2)}, u32[]{:S(2)}) async-start(f32[16,4,16,128]{3,2,1,0:T(8,128)} %get-tuple-element.14), calls=%async_computation | async-start | bytes 1048576 | tf_op jit(solution)/shard_map/all_to_all | solution.py:517
  9.0 3.2 %collective-permute-start = (f32[34,16,128]{2,1,0:T(8,128)S(1)}, f32[34,16,128]{2,1,0:T(8,128)S(1)}, u32[]{:S(2)}, u32[]{:S(2)}) collective-permute-start(f32[34,16,128]{2,1,0:T(8,128)S(1)} %get-tuple-element.16), channel_id=1, source_target_pairs={{0,1},{1,2},{2,3},{3,4},{4,5},{5,6},{6,7},{7,0},{8,9},{9,10},{10,1... | collective-permute-start | bytes 835592 | tf_op jit(solution)/shard_map/ppermute | solution.py:515
  18.1 1.9 %shard_map.74 = (bf16[10,256,768]{2,1,0:T(8,128)(2,1)S(1)}, bf16[3,384,128]{2,1,0:T(8,128)(2,1)S(1)}) custom-call(f32[256,256]{1,0:T(8,128)S(1)} %copy-done.4, f32[128,128]{1,0:T(8,128)S(1)} %bitcast.38, f32[256,256]{1,0:T(8,128)S(1)} %copy-done.5, f32[128,128]{1,0:T(8,128)S(1)} %bitcast.39), custom_call_target="tpu_custom_call" | custom-call | flops 1000000000 | bytes 655360 | tf_op jit(solution)/shard_map/pallas_call | solution.py:24
  20.0 1.9 %copy-done = bf16[10,256,768]{2,1,0:T(8,128)(2,1)} copy-done((bf16[10,256,768]{2,1,0:T(8,128)(2,1)}, bf16[10,256,768]{2,1,0:T(8,128)(2,1)S(1)}, u32[]{:S(2)}) %copy-start) | copy-done | bytes 3932184
  23.1 24.5 %all_to_all.15.more_ref = f32[16,9,16,128]{3,2,1,0:T(8,128)S(1)} all-to-all(f32[16,9,16,128]{3,2,1,0:T(8,128)S(1)} %shard_map.75), channel_id=1, replica_groups=mesh['section'=2,'stream'=16,'slab'=8] {'stream'}, dimensions={0} | all-to-all | bytes 2359296 | tf_op jit(solution)/shard_map/all_to_all | solution.py:541
  47.6 2.1 %copy-done.1 = bf16[10,256,768]{2,1,0:T(8,128)(2,1)S(1)} copy-done((bf16[10,256,768]{2,1,0:T(8,128)(2,1)S(1)}, bf16[10,256,768]{2,1,0:T(8,128)(2,1)}, u32[]{:S(2)}) %copy-start.1) | copy-done | bytes 3932184
  49.7 2.5 %shard_map.76.waves_ref = f32[5,256,128]{2,1,0:T(8,128)S(1)} custom-call(f32[16,4,16,128]{3,2,1,0:T(8,128)S(1)} %all-to-all-done.raw_ref, f32[16,9,16,128]{3,2,1,0:T(8,128)S(1)} %all_to_all.15.more_ref, bf16[10,256,768]{2,1,0:T(8,128)(2,1)S(1)} %copy-done.1, bf16[3,384,128]{2,1,0:T(8,128)(2,1)S(1)} %get-tuple-element.18.right_ref), custom_call_target="tpu_custom_call" | custom-call | flops 2000000000 | bytes 5931008 | tf_op jit(solution)/shard_map/pallas_call | solution.py:24
  53.0 2.4 %collective-permute-start.5 = (f32[3,256,128]{2,1,0:T(8,128)}, f32[3,256,128]{2,1,0:T(8,128)S(1)}, u32[]{:S(2)}, u32[]{:S(2)}) collective-permute-start(f32[3,256,128]{2,1,0:T(8,128)} %slice.102), channel_id=1, source_target_pairs={{0,8},{32,40},{8,16},{40,48},{16,24},{48,56},{24,120},{56,88},{120... | collective-permute-start | bytes 1179656 | tf_op jit(solution)/shard_map/ppermute | solution.py:544
  55.4 5.6 %collective-permute-start.4 = (f32[3,256,128]{2,1,0:T(8,128)}, f32[3,256,128]{2,1,0:T(8,128)S(1)}, u32[]{:S(2)}, u32[]{:S(2)}) collective-permute-start(f32[3,256,128]{2,1,0:T(8,128)} %slice.102), channel_id=1, source_target_pairs={{0,103},{32,71},{8,0},{40,32},{16,8},{48,40},{24,16},{56,48},{120,... | collective-permute-start | bytes 1179656 | tf_op jit(solution)/shard_map/ppermute | solution.py:544
  61.0 1.9 %collective-permute-start.3 = (f32[3,256,128]{2,1,0:T(8,128)}, f32[3,256,128]{2,1,0:T(8,128)}, u32[]{:S(2)}, u32[]{:S(2)}) collective-permute-start(f32[3,256,128]{2,1,0:T(8,128)} %slice.102), channel_id=1, source_target_pairs={{0,32},{32,8},{8,40},{40,16},{16,48},{48,24},{24,56},{56,120},{120... | collective-permute-start | bytes 1179656 | tf_op jit(solution)/shard_map/ppermute | solution.py:544
  62.9 6.3 %collective-permute-start.2 = (f32[3,256,128]{2,1,0:T(8,128)}, f32[3,256,128]{2,1,0:T(8,128)}, u32[]{:S(2)}, u32[]{:S(2)}) collective-permute-start(f32[3,256,128]{2,1,0:T(8,128)} %slice.102), channel_id=1, source_target_pairs={{0,71},{32,0},{8,32},{40,8},{16,40},{48,16},{24,48},{56,24},{120,5... | collective-permute-start | bytes 1179656 | tf_op jit(solution)/shard_map/ppermute | solution.py:544
  69.4 2.1 %copy-done.2 = bf16[10,256,768]{2,1,0:T(8,128)(2,1)S(1)} copy-done((bf16[10,256,768]{2,1,0:T(8,128)(2,1)S(1)}, bf16[10,256,768]{2,1,0:T(8,128)(2,1)}, u32[]{:S(2)}) %copy-start.2) | copy-done | bytes 3932184
  71.6 1.4 shard_map.77.held_ref
  73.4 1.5 collective-permute-done.2.up1_ref
  74.9 2.3 %shard_map.78.own_ref = f32[4,3,256,128]{3,2,1,0:T(8,128)S(1)} custom-call(f32[7]{0:T(128)S(1)} %convert_element_type.33.edge_ref.flag_ref, f32[256,128]{1,0:T(8,128)S(1)} %broadcast_in_dim.15.region_ref, f32[16,4,16,128]{3,2,1,0:T(8,128)S(1)} %all-to-all-done.raw_ref, f32[16,9,16,128]{3,2,1,0:T(8,128)S(1)} %all_to_all.15.more_ref, ...), custom_call_target="tpu_custom_call" | custom-call | tf_op jit(solution)/shard_map/pallas_call | solution.py:532
  77.5 3.4 %collective-permute-done.6.source_ref = f32[4,3,256,128]{3,2,1,0:T(8,128)S(1)} collective-permute-done((f32[4,3,256,128]{3,2,1,0:T(8,128)S(1)}, f32[4,3,256,128]{3,2,1,0:T(8,128)S(1)}, u32[]{:S(2)}, u32[]{:S(2)}) %collective-permute-start.6) | collective-permute-done | bytes 1572896 | tf_op jit(solution)/shard_map/ppermute | solution.py:549
  80.9 2.8 %shard_map.79.driven_ref = f32[12,256,128]{2,1,0:T(8,128)S(1)} custom-call(f32[7]{0:T(128)S(1)} %convert_element_type.33.edge_ref.flag_ref, f32[5,256,128]{2,1,0:T(8,128)S(1)} %shard_map.76.waves_ref, f32[4,3,256,128]{3,2,1,0:T(8,128)S(1)} %shard_map.78.own_ref, f32[4,3,256,128]{3,2,1,0:T(8,128)S(1)} %collective-permute-done.6.source_ref, ...), custom_call_target="tpu_custom_call" | custom-call | tf_op jit(solution)/shard_map/pallas_call | solution.py:532
  83.7 5.6 %shard_map.80.last_ref = f32[17,256,128]{2,1,0:T(8,128)S(1)} custom-call(f32[7]{0:T(128)S(1)} %convert_element_type.33.edge_ref.flag_ref, f32[16,4,16,128]{3,2,1,0:T(8,128)S(1)} %all-to-all-done.raw_ref, f32[16,9,16,128]{3,2,1,0:T(8,128)S(1)} %all_to_all.15.more_ref, f32[12,256,128]{2,1,0:T(8,128)S(1)} %shard_map.79.driven_ref, ...), custom_call_target="tpu_custom_call" | custom-call | tf_op jit(solution)/shard_map/pallas_call | solution.py:532
  89.3 3.4 %shard_map.81 = f32[16,19,16,128]{3,2,1,0:T(8,128)S(1)} custom-call(f32[7]{0:T(128)S(1)} %convert_element_type.33.edge_ref.flag_ref, f32[17,256,128]{2,1,0:T(8,128)S(1)} %shard_map.80.last_ref, bf16[10,256,768]{2,1,0:T(8,128)(2,1)S(1)} %copy-done.2, bf16[3,384,128]{2,1,0:T(8,128)(2,1)S(1)} %get-tuple-element.18.right_ref), custom_call_target="tpu_custom_call" | custom-call | tf_op jit(solution)/shard_map/pallas_call | solution.py:532
  92.7 42.8 %all_to_all.16.back_ref = f32[16,19,16,128]{3,2,1,0:T(8,128)S(1)} all-to-all(f32[16,19,16,128]{3,2,1,0:T(8,128)S(1)} %shard_map.81), channel_id=1, replica_groups=mesh['section'=2,'stream'=16,'slab'=8] {'stream'}, dimensions={0} | all-to-all | bytes 4980736 | tf_op jit(solution)/shard_map/all_to_all | solution.py:553
  137.0 1.5 shard_map.82
  139.6 2.1 %collective-permute-start.9 = (f32[46,16,128]{2,1,0:T(8,128)S(1)}, f32[46,16,128]{2,1,0:T(8,128)S(1)}, u32[]{:S(2)}, u32[]{:S(2)}) collective-permute-start(f32[46,16,128]{2,1,0:T(8,128)S(1)} %fusion.2), channel_id=1, source_target_pairs={{1,0},{2,1},{3,2},{4,3},{5,4},{6,5},{7,6},{0,7},{9,8},{10,9},{11,1... | collective-permute-start | bytes 1130504 | tf_op jit(solution)/shard_map/ppermute | solution.py:573
  141.7 8.6 %collective-permute-done.8 = f32[46,16,128]{2,1,0:T(8,128)S(1)} collective-permute-done((f32[46,16,128]{2,1,0:T(8,128)S(1)}, f32[46,16,128]{2,1,0:T(8,128)S(1)}, u32[]{:S(2)}, u32[]{:S(2)}) %collective-permute-start.8) | collective-permute-done | bytes 376864 | tf_op jit(solution)/shard_map/ppermute | solution.py:572
  150.3 1.4 collective-permute-done.9
  (52 shorter events, 13.7 us)
Async XLA Ops:
  0.0 1.0 copy-start.3
  2.0 21.2 %all-to-all-start = ((f32[16,4,16,128]{3,2,1,0:T(8,128)}), f32[16,4,16,128]{3,2,1,0:T(8,128)S(1)}, u32[]{:S(2)}, u32[]{:S(2)}) async-start(f32[16,4,16,128]{3,2,1,0:T(8,128)} %get-tuple-element.14), calls=%async_computation | async-start | bytes 1048576 | tf_op jit(solution)/shard_map/all_to_all | solution.py:517
  9.0 12.9 %collective-permute-start = (f32[34,16,128]{2,1,0:T(8,128)S(1)}, f32[34,16,128]{2,1,0:T(8,128)S(1)}, u32[]{:S(2)}, u32[]{:S(2)}) collective-permute-start(f32[34,16,128]{2,1,0:T(8,128)S(1)} %get-tuple-element.16), channel_id=1, source_target_pairs={{0,1},{1,2},{2,3},{3,4},{4,5},{5,6},{6,7},{7,0},{8,9},{9,10},{10,1... | collective-permute-start | bytes 835592 | tf_op jit(solution)/shard_map/ppermute | solution.py:515
  12.2 9.7 %collective-permute-start.1 = (f32[34,16,128]{2,1,0:T(8,128)S(1)}, f32[34,16,128]{2,1,0:T(8,128)S(1)}, u32[]{:S(2)}, u32[]{:S(2)}) collective-permute-start(f32[34,16,128]{2,1,0:T(8,128)S(1)} %get-tuple-element.17), channel_id=1, source_target_pairs={{1,0},{2,1},{3,2},{4,3},{5,4},{6,5},{7,6},{0,7},{9,8},{10,9},{11,1... | collective-permute-start | bytes 835592 | tf_op jit(solution)/shard_map/ppermute | solution.py:516
  16.2 1.0 copy-start.4
  17.2 0.9 copy-start.5
  20.0 1.9 %copy-start = (bf16[10,256,768]{2,1,0:T(8,128)(2,1)}, bf16[10,256,768]{2,1,0:T(8,128)(2,1)S(1)}, u32[]{:S(2)}) copy-start(bf16[10,256,768]{2,1,0:T(8,128)(2,1)S(1)} %get-tuple-element.19.left_ref) | copy-start | bytes 11796484
  47.6 2.1 %copy-start.1 = (bf16[10,256,768]{2,1,0:T(8,128)(2,1)S(1)}, bf16[10,256,768]{2,1,0:T(8,128)(2,1)}, u32[]{:S(2)}) copy-start(bf16[10,256,768]{2,1,0:T(8,128)(2,1)} %copy-done) | copy-start | bytes 11796484
  49.7 19.5 %copy-start.8 = (s32[16,1]{0,1:T(1,128)S(1)}, s32[16,1]{0,1:T(1,128)}, u32[]{:S(2)}) copy-start(s32[16,1]{0,1:T(1,128)} %param.8) | copy-start | bytes 196
  53.0 20.0 %collective-permute-start.5 = (f32[3,256,128]{2,1,0:T(8,128)}, f32[3,256,128]{2,1,0:T(8,128)S(1)}, u32[]{:S(2)}, u32[]{:S(2)}) collective-permute-start(f32[3,256,128]{2,1,0:T(8,128)} %slice.102), channel_id=1, source_target_pairs={{0,8},{32,40},{8,16},{40,48},{16,24},{48,56},{24,120},{56,88},{120... | collective-permute-start | bytes 1179656 | tf_op jit(solution)/shard_map/ppermute | solution.py:544
  55.4 17.6 %collective-permute-start.4 = (f32[3,256,128]{2,1,0:T(8,128)}, f32[3,256,128]{2,1,0:T(8,128)S(1)}, u32[]{:S(2)}, u32[]{:S(2)}) collective-permute-start(f32[3,256,128]{2,1,0:T(8,128)} %slice.102), channel_id=1, source_target_pairs={{0,103},{32,71},{8,0},{40,32},{16,8},{48,40},{24,16},{56,48},{120,... | collective-permute-start | bytes 1179656 | tf_op jit(solution)/shard_map/ppermute | solution.py:544
  61.0 12.4 %collective-permute-start.3 = (f32[3,256,128]{2,1,0:T(8,128)}, f32[3,256,128]{2,1,0:T(8,128)}, u32[]{:S(2)}, u32[]{:S(2)}) collective-permute-start(f32[3,256,128]{2,1,0:T(8,128)} %slice.102), channel_id=1, source_target_pairs={{0,32},{32,8},{8,40},{40,16},{16,48},{48,24},{24,56},{56,120},{120... | collective-permute-start | bytes 1179656 | tf_op jit(solution)/shard_map/ppermute | solution.py:544
  62.9 11.9 %collective-permute-start.2 = (f32[3,256,128]{2,1,0:T(8,128)}, f32[3,256,128]{2,1,0:T(8,128)}, u32[]{:S(2)}, u32[]{:S(2)}) collective-permute-start(f32[3,256,128]{2,1,0:T(8,128)} %slice.102), channel_id=1, source_target_pairs={{0,71},{32,0},{8,32},{40,8},{16,40},{48,16},{24,48},{56,24},{120,5... | collective-permute-start | bytes 1179656 | tf_op jit(solution)/shard_map/ppermute | solution.py:544
  69.4 2.1 %copy-start.2 = (bf16[10,256,768]{2,1,0:T(8,128)(2,1)S(1)}, bf16[10,256,768]{2,1,0:T(8,128)(2,1)}, u32[]{:S(2)}) copy-start(bf16[10,256,768]{2,1,0:T(8,128)(2,1)} %copy-done) | copy-start | bytes 11796484
  77.2 3.7 %collective-permute-start.6 = (f32[4,3,256,128]{3,2,1,0:T(8,128)S(1)}, f32[4,3,256,128]{3,2,1,0:T(8,128)S(1)}, u32[]{:S(2)}, u32[]{:S(2)}) collective-permute-start(f32[4,3,256,128]{3,2,1,0:T(8,128)S(1)} %shard_map.78.own_ref), channel_id=1, source_target_pairs={{0,128},{128,0},{1,129},{129,1},{2,130},{130,2},{3,131},{131,3},{4... | collective-permute-start | bytes 4718600 | tf_op jit(solution)/shard_map/ppermute | solution.py:549
  136.6 2.8 %copy-start.7 = (pred[46]{0:T(512)(128)(4,1)S(1)}, pred[46]{0:T(512)(128)(4,1)}, u32[]{:S(2)}) copy-start(pred[46]{0:T(512)(128)(4,1)} %constant.33.clone.1) | copy-start | bytes 142
  136.6 2.6 %collective-permute-start.7 = (f32[100,16,128]{2,1,0:T(8,128)S(1)}, f32[100,16,128]{2,1,0:T(8,128)S(1)}, u32[]{:S(2)}, u32[]{:S(2)}) collective-permute-start(f32[100,16,128]{2,1,0:T(8,128)S(1)} %shard_map.83), channel_id=1, source_target_pairs={{0,128},{128,0},{1,129},{129,1},{2,130},{130,2},{3,131},{131,3},{4... | collective-permute-start | bytes 2457608 | tf_op jit(solution)/shard_map/ppermute | solution.py:557
  139.3 12.5 %copy-start.6 = (pred[16]{0:T(512)(128)(4,1)S(1)}, pred[16]{0:T(512)(128)(4,1)}, u32[]{:S(2)}) copy-start(pred[16]{0:T(512)(128)(4,1)} %constant.31.clone.1) | copy-start | bytes 52
  139.4 10.9 %collective-permute-start.8 = (f32[46,16,128]{2,1,0:T(8,128)S(1)}, f32[46,16,128]{2,1,0:T(8,128)S(1)}, u32[]{:S(2)}, u32[]{:S(2)}) collective-permute-start(f32[46,16,128]{2,1,0:T(8,128)S(1)} %add_add_fusion), channel_id=1, source_target_pairs={{0,1},{1,2},{2,3},{3,4},{4,5},{5,6},{6,7},{7,0},{8,9},{9,10},{10,1... | collective-permute-start | bytes 1130504 | tf_op jit(solution)/shard_map/ppermute | solution.py:572
  139.6 12.1 %collective-permute-start.9 = (f32[46,16,128]{2,1,0:T(8,128)S(1)}, f32[46,16,128]{2,1,0:T(8,128)S(1)}, u32[]{:S(2)}, u32[]{:S(2)}) collective-permute-start(f32[46,16,128]{2,1,0:T(8,128)S(1)} %fusion.2), channel_id=1, source_target_pairs={{1,0},{2,1},{3,2},{4,3},{5,4},{6,5},{7,6},{0,7},{9,8},{10,9},{11,1... | collective-permute-start | bytes 1130504 | tf_op jit(solution)/shard_map/ppermute | solution.py:573

commit v5 on v3

--- a/solution.py
+++ b/solution.py
@@ -245,7 +245,7 @@
     return ref[:, index].reshape(blocks * xs, nz)
 
 
-def waves_kernel(in_ref, left_ref, right_ref, out_ref):
+def waves_kernel(in_ref, left_ref, right_ref, out_ref, sums_ref):
     do = Products(left_ref, right_ref)
     p0 = [plane(in_ref, i) for i in range(3)]
     u0 = [plane(in_ref, 3 + i) for i in range(3)]
@@ -258,29 +258,28 @@
         return [
             2.0 * now[i] - before[i] + (one[i] + two[i] + three[i] + tau**2 * before[i + 1])
             for i in range(count)
-        ]
+        ], one[0]
 
     moved = do.left("e1", p0)
     driven = do.left("ta", u0)
     p1 = [p0[i] + (moved[i] + driven[i] - tau * plane(in_ref, 6 + i)) for i in range(3)]
     h2 = p0[0] + moved[0] + p1[0]
-    out_ref[2] = h2
-    p2 = advance(p1, p0)
-    p3 = advance(p2, p1)
-    h4 = h2 + do.left("e2", [h2])[0] + p2[0] + do.left("e1", p2[:1])[0] + p3[0]
-    out_ref[3] = h4
-    p4 = advance(p3, p2)
-    p5 = advance(p4, p3)
-    h6 = h4 + do.left("e2", [h4])[0] + p4[0] + do.left("e1", p4)[0] + p5[0]
+    sums_ref[0] = h2
+    p2, _ = advance(p1, p0)
+    p3, twice = advance(p2, p1)
+    h4 = h2 + do.left("e2", [h2])[0] + p2[0] + 0.5 * twice + p3[0]
+    sums_ref[1] = h4
+    p4, _ = advance(p3, p2)
+    p5, twice = advance(p4, p3)
+    sums_ref[2] = h4 + do.left("e2", [h4])[0] + p4[0] + 0.5 * twice + p5[0]
     out_ref[0] = p4[0]
     out_ref[1] = p5[0]
-    out_ref[4] = h6
-
-
-def held_kernel(in_ref, waves_ref, left_ref, right_ref, out_ref):
+
+
+def held_kernel(in_ref, sums_ref, left_ref, right_ref, out_ref):
     do = Products(left_ref, right_ref)
     start = [plane(in_ref, i) for i in (3, 10, 11, 12, 9)]
-    h = [waves_ref[2 + n] for n in range(3)]
+    h = [sums_ref[n] for n in range(3)]
     pull_x = do.left("a", h)
     pull_z = do.right(h, "c")
     for n, growth in enumerate(("e2", "e4", "e6")):
@@ -291,9 +290,9 @@
             out_ref[n, k] = start[k] + change[k]
 
 
-def source_kernel(flag_ref, region_ref, in_ref, held_ref, up1_ref, down1_ref, up2_ref, down2_ref, left_ref, right_ref, out_ref):
+def source_kernel(flag_ref, region_ref, in_ref, held_ref, up_ref, down_ref, far_ref, left_ref, right_ref, out_ref):
     do = Products(left_ref, right_ref)
-    nx, nz = up1_ref.shape[1:]
+    nx, nz = up_ref.shape[1:]
     row = lax.broadcasted_iota(jnp.int32, (nx, nz), 0)
     lane = lax.broadcasted_iota(jnp.int32, (nx, nz), 1)
     region = region_ref[...]
@@ -308,8 +307,7 @@
         behind = jnp.where(lane == 0, 0.0, pltpu.roll(value, 1, 1))
         return 0.5 * (ahead - behind)
 
-    up1, down1, up2, down2 = flag_ref[3], flag_ref[4], flag_ref[5], flag_ref[6]
-    near = [up1 * up1_ref[n] - down1 * down1_ref[n] for n in range(3)]
+    near = [flag_ref[3] * up_ref[n] - flag_ref[4] * down_ref[n] for n in range(3)]
     half = [0.5 * value for value in near]
     pull_x = do.left("a", half)
     pull_z = do.right(half, "c")
@@ -320,7 +318,7 @@
             u, w = held_ref[n - 1, 0], held_ref[n - 1, 1]
             slope_u = held_ref[n - 1, 2] - tau * pull_x[n - 1]
             slope_w = held_ref[n - 1, 3] - tau * pull_z[n - 1]
-            far = up2 * up2_ref[n - 1] - down2 * down2_ref[n - 1]
+            far = far_ref[n - 1]
             v = held_ref[n - 1, 4] - tau * ((2.0 / 3.0) * near[n - 1] - (1.0 / 12.0) * far)
         o_x = slope_w - slope_z(v)
         o_y = slope_z(u) - slope_x(w)
@@ -350,12 +348,11 @@
             if k < len(drive):
                 terms.append(drive[k])
             out.append(functools.reduce(lambda one, two: one + two, terms))
-        return out
-
-    def grow(self, sums, before, now):
-        moved = self.do.left("e1", before)
+        return out, m_now
+
+    def grow(self, sums, before, twice, now):
         kept = self.do.left("e2", sums) if sums else []
-        out = [before[k] + moved[k] + now[k] for k in range(len(now))]
+        out = [before[k] + 0.5 * twice[k] + now[k] for k in range(len(now))]
         return [out[k] + (sums[k] + kept[k]) if k < len(sums) else out[k] for k in range(len(now))]
 
 
@@ -372,18 +369,18 @@
     ]
 
 
-def driven_kernel(flag_ref, waves_ref, own_ref, source_ref, left_ref, right_ref, out_ref):
+def driven_kernel(flag_ref, waves_ref, sums_ref, own_ref, source_ref, left_ref, right_ref, out_ref):
     chain = Chain(left_ref, right_ref)
     drive = drives(chain.do, flag_ref, own_ref, source_ref, 0, 2)
     q2 = list(drive[0])
     moved = chain.do.left("m1", q2)
     q3 = [2.0 * q2[k] + moved[k] + drive[0][k] for k in range(2)]
-    g4 = chain.grow([], q2, q3)
-    q4 = chain.advance(q3, q2, drive[1], 4)
-    q5 = chain.advance(q4, q3, drive[1], 4)
-    g6 = chain.grow(g4, q4, q5)
-    for first, values, wave in ((0, q4, 0), (4, q5, 1), (8, g6, 4)):
-        out_ref[first] = values[0] + waves_ref[wave]
+    g4 = chain.grow([], q2, moved, q3)
+    q4, _ = chain.advance(q3, q2, drive[1], 4)
+    q5, moved = chain.advance(q4, q3, drive[1], 4)
+    g6 = chain.grow(g4, q4, moved, q5)
+    for first, values, wave in ((0, q4, waves_ref[0]), (4, q5, waves_ref[1]), (8, g6, sums_ref[2])):
+        out_ref[first] = values[0] + wave
         for k in range(1, 4):
             out_ref[first + k] = values[k]
 
@@ -393,11 +390,11 @@
     do = chain.do
     drive = drives(do, flag_ref, own_ref, source_ref, 2, 4)
     q4, q5, g6 = [[driven_ref[first + k] for k in range(4)] for first in (0, 4, 8)]
-    q6 = chain.advance(q5, q4, drive[0], 6)
-    q7 = chain.advance(q6, q5, drive[0], 6)
-    for k, value in enumerate(chain.grow(g6, q6, q7)):
+    q6, _ = chain.advance(q5, q4, drive[0], 6)
+    q7, moved = chain.advance(q6, q5, drive[0], 6)
+    for k, value in enumerate(chain.grow(g6, q6, moved, q7)):
         out_ref[8 + k] = value
-    for k, value in enumerate(chain.advance(q7, q6, drive[1], 8)):
+    for k, value in enumerate(chain.advance(q7, q6, drive[1], 8)[0]):
         out_ref[k] = value
     flow = flag_ref[2] > 0
 
@@ -459,10 +456,13 @@
     order = order_of(streams)
 
     def device(y):
-        return order[y % streams] * slabs + y // streams
-
-    flow = [(device(y), device((y + steps) % count)) for y in range(count)]
-    return flow + [(i, i) for i in range(count, count * lax.axis_size("section"))]
+        return order[y % streams] * slabs + (y // streams) % slabs
+
+    return [
+        (section * count + device(y), section * count + device((y + far) % count))
+        for section, far in ((0, steps), (1, 2 * steps))
+        for y in range(count)
+    ]
 
 
 def shards(state, source_mask, deriv_x, deriv_z, filter_x, filter_z):
@@ -520,15 +520,19 @@
 
     spread = with_edges(spread_kernel, shape(own, 13, xs, nz), raw, from_low, from_high, right)
     planes = lax.all_to_all(spread, "stream", split_axis=0, concat_axis=0, tiled=True)
-    waves = call(waves_kernel, shape(5, nx, nz), planes, left, right, flops=2 * 10**9)
-    sums = waves[2:5]
-    near = [lax.ppermute(sums, AXES, along_y(steps)) for steps in (-1, 1, -2, 2)]
-    held = call(held_kernel, shape(3, 5, nx, nz), planes, waves, left, right, flops=10**9)
+    waves, sums = call(
+        waves_kernel, (shape(2, nx, nz), shape(3, nx, nz)), planes, left, right, flops=2 * 10**9
+    )
+    across = lax.ppermute(sums, "section", swap)
+    carried = jnp.where(edges[2] > 0, sums, across)
+    up, down = [lax.ppermute(carried, AXES, along_y(steps)) for steps in (-1, 1)]
+    far = lax.ppermute(edges[5] * up - edges[6] * down, "section", swap)
+    held = call(held_kernel, shape(3, 5, nx, nz), planes, sums, left, right, flops=10**9)
     source = with_edges(
-        source_kernel, shape(4, 3, nx, nz), region, planes, held, *near, left, right
+        source_kernel, shape(4, 3, nx, nz), region, planes, held, up, down, far, left, right
     )
     moved = lax.ppermute(source, "section", swap)
-    driven = with_edges(driven_kernel, shape(12, nx, nz), waves, source, moved, left, right)
+    driven = with_edges(driven_kernel, shape(12, nx, nz), waves, sums, source, moved, left, right)
     last = with_edges(finish_kernel, shape(17, nx, nz), planes, driven, source, moved, left, right)
     done = with_edges(filter_kernel, shape(streams, SLOTS, xs, nz), last, left, right)
     back = lax.all_to_all(done, "stream", split_axis=0, concat_axis=0, tiled=True)

time: 147 us -> 143 us (0.973)
  starting transfers between devices: 22.2 us -> 10.7 us
  waiting for transfers between devices: 21.9 us -> 29.1 us
  other arithmetic: 0.35 us -> 2.3 us
  blocking collectives: 70 us -> 68.2 us
    ppermute x4, starting transfers between devices: 16.2 us -> 4.6 us  [the longest x2 4.51 us: shards(): lax.ppermute(carried, AXES, along_y(steps))]
    ppermute x4, waiting for transfers between devices: 1.83 us -> 9.31 us  [the longest x2 8.84 us: shards(): lax.ppermute(carried, AXES, along_y(steps))]
    sub x0 -> x1, other arithmetic: none -> 1.91 us  [shards(): far = lax.ppermute(edges[5] * up - edges[6] * down, 'section', swap)]
    all_to_all x1, blocking collectives: 40.2 us -> 38.5 us  [shards(): lax.all_to_all(done, 'stream', split_axis=0, concat_axis=0, tiled=True)]
where the time goes in v5:
time: 143 us; the launch traced here: 142 us
  blocking collectives  68.2 us (48%)
  waiting for transfers between devices  29.1 us (20%)
  Pallas kernels  23.4 us (16%)
  starting transfers between devices  10.7 us (7%)
  local copies, waits for them, and re-layouts  6.2 us (4%)
  other arithmetic  2.3 us (2%)
  between operations  1.59 us (1%)
    all_to_all x1, blocking collectives, shards(): lax.all_to_all(done, 'stream', split_axis=0, concat_axis=0, tiled=True)  38.5 us
    all_to_all x1, blocking collectives, shards(): lax.all_to_all(spread, 'stream', split_axis=0, concat_axis=0, tiled=True)  29.8 us
    pallas_call x7, Pallas kernels, with_edges(): pl.pallas_call(body, out_shape=out_shape, in_specs=[pl.BlockSpec(memory_s...  17.6 us
    ppermute x2, waiting for transfers between devices, shards(): lax.ppermute(carried, AXES, along_y(steps))  8.84 us
    ppermute x1, waiting for transfers between devices, shards(): from_low = lax.ppermute(high + sum(more_high), 'slab', upward)  8.58 us
    pallas_call x3, Pallas kernels, call(): pl.pallas_call(body, out_shape=out_shape, scratch_shapes=scratch, compile...  5.87 us
    ppermute x2, starting transfers between devices, shards(): lax.ppermute(carried, AXES, along_y(steps))  4.51 us
    unnamed x23, local copies, waits for them, and re-layouts  3.61 us
  transfers between devices with their start and end apart: 10, of which 8 were waited for; matrix products, arithmetic and copies ran while one was open for 1% of the time, Pallas kernels for 3%

profile of v5, /device:TPU:96, one launch (start us, length us, event | category | flops | bytes accessed | tf_op | source)
XLA Modules:
  0.0 141.5 jit_solution(8149434108578888559)
XLA Ops:
  0.0 1.3 copy.13
  1.4 3.2 %collective-permute-start = (f32[34,16,128]{2,1,0:T(8,128)S(1)}, f32[34,16,128]{2,1,0:T(8,128)S(1)}, u32[]{:S(2)}, u32[]{:S(2)}) collective-permute-start(f32[34,16,128]{2,1,0:T(8,128)S(1)} %pad_maximum_fusion), channel_id=1, source_target_pairs={{0,1},{1,2},{2,3},{3,4},{4,5},{5,6},{6,7},{7,0},{8,9},{9,10},{10,1... | collective-permute-start | bytes 835592 | tf_op jit(solution)/shard_map/ppermute | solution.py:490
  6.2 1.9 %shard_map.73 = (bf16[10,256,768]{2,1,0:T(8,128)(2,1)S(1)}, bf16[3,384,128]{2,1,0:T(8,128)(2,1)S(1)}) custom-call(f32[256,256]{1,0:T(8,128)S(1)} %copy-done.2, f32[128,128]{1,0:T(8,128)S(1)} %bitcast.63, f32[256,256]{1,0:T(8,128)S(1)} %copy-done.3, f32[128,128]{1,0:T(8,128)S(1)} %bitcast.64), custom_call_target="tpu_custom_call" | custom-call | flops 1000000000 | bytes 655360 | tf_op jit(solution)/shard_map/pallas_call | solution.py:24
  8.1 2.4 %collective-permute-done.low_ref = f32[34,16,128]{2,1,0:T(8,128)S(1)} collective-permute-done((f32[34,16,128]{2,1,0:T(8,128)S(1)}, f32[34,16,128]{2,1,0:T(8,128)S(1)}, u32[]{:S(2)}, u32[]{:S(2)}) %collective-permute-start) | collective-permute-done | bytes 278560 | tf_op jit(solution)/shard_map/ppermute | solution.py:490
  10.5 3.5 %collective-permute-done.1.high_ref = f32[34,16,128]{2,1,0:T(8,128)S(1)} collective-permute-done((f32[34,16,128]{2,1,0:T(8,128)S(1)}, f32[34,16,128]{2,1,0:T(8,128)S(1)}, u32[]{:S(2)}, u32[]{:S(2)}) %collective-permute-start.1) | collective-permute-done | bytes 278560 | tf_op jit(solution)/shard_map/ppermute | solution.py:493
  14.0 1.3 shard_map.74
  15.3 29.8 %all_to_all.10.in_ref = f32[16,13,16,128]{3,2,1,0:T(8,128)S(1)} all-to-all(f32[16,13,16,128]{3,2,1,0:T(8,128)S(1)} %shard_map.74), channel_id=1, replica_groups=mesh['section'=2,'stream'=16,'slab'=8] {'stream'}, dimensions={0} | all-to-all | bytes 3407872 | tf_op jit(solution)/shard_map/all_to_all | solution.py:522
  45.1 2.6 %shard_map.75 = (f32[2,256,128]{2,1,0:T(8,128)S(1)}, f32[3,256,128]{2,1,0:T(8,128)S(1)}) custom-call(f32[16,13,16,128]{3,2,1,0:T(8,128)S(1)} %all_to_all.10.in_ref, bf16[10,256,768]{2,1,0:T(8,128)(2,1)S(1)} %get-tuple-element.13.left_ref, bf16[3,384,128]{2,1,0:T(8,128)(2,1)S(1)} %get-tuple-element.12.right_ref), custom_call_target="tpu_custom_call" | custom-call | flops 2000000000 | bytes 5931008 | tf_op jit(solution)/shard_map/pallas_call | solution.py:24
  50.0 3.9 %collective-permute-start.3 = (f32[3,256,128]{2,1,0:T(8,128)S(1)}, f32[3,256,128]{2,1,0:T(8,128)S(1)}, u32[]{:S(2)}, u32[]{:S(2)}) collective-permute-start(f32[3,256,128]{2,1,0:T(8,128)S(1)} %broadcast_select_fusion), channel_id=1, source_target_pairs={{0,71},{32,0},{8,32},{40,8},{16,40},{48,16},{24,48},{56,24},{120,5... | collective-permute-start | bytes 1179656 | tf_op jit(solution)/shard_map/ppermute | solution.py:528
  54.0 8.8 %collective-permute-done.4.down_ref = f32[3,256,128]{2,1,0:T(8,128)S(1)} collective-permute-done((f32[3,256,128]{2,1,0:T(8,128)S(1)}, f32[3,256,128]{2,1,0:T(8,128)S(1)}, u32[]{:S(2)}, u32[]{:S(2)}) %collective-permute-start.4) | collective-permute-done | bytes 393248 | tf_op jit(solution)/shard_map/ppermute | solution.py:528
  62.8 1.9 %multiply_subtract_fusion = f32[3,256,128]{2,1,0:T(8,128)} fusion(f32[3,256,128]{2,1,0:T(8,128)S(1)} %collective-permute-done.4.down_ref, f32[3,256,128]{2,1,0:T(8,128)S(1)} %collective-permute-done.3.up_ref, f32[]{:T(128)} %bitcast.24, f32[]{:T(128)} %bitcast.23), kind=kLoop, calls=%fused_computation.2 | loop fusion | flops 294912 | bytes 1179656 | tf_op jit(solution)/shard_map/sub | solution.py:529
  64.9 2.1 %copy-done.1 = bf16[10,256,768]{2,1,0:T(8,128)(2,1)S(1)} copy-done((bf16[10,256,768]{2,1,0:T(8,128)(2,1)S(1)}, bf16[10,256,768]{2,1,0:T(8,128)(2,1)}, u32[]{:S(2)}) %copy-start.1) | copy-done | bytes 3932184
  67.0 1.4 %shard_map.76.held_ref = f32[3,5,256,128]{3,2,1,0:T(8,128)S(1)} custom-call(f32[16,13,16,128]{3,2,1,0:T(8,128)S(1)} %all_to_all.10.in_ref, f32[3,256,128]{2,1,0:T(8,128)S(1)} %get-tuple-element.15.sums_ref, bf16[10,256,768]{2,1,0:T(8,128)(2,1)S(1)} %copy-done.1, bf16[3,384,128]{2,1,0:T(8,128)(2,1)S(1)} %get-tuple-element.12.right_ref), custom_call_target="tpu_custom_call" | custom-call | flops 1000000000 | bytes 6324224 | tf_op jit(solution)/shard_map/pallas_call | solution.py:24
  68.6 2.2 %shard_map.77.own_ref = f32[4,3,256,128]{3,2,1,0:T(8,128)S(1)} custom-call(f32[7]{0:T(128)S(1)} %convert_element_type.33.edge_ref.flag_ref, f32[256,128]{1,0:T(8,128)S(1)} %broadcast_in_dim.15.region_ref, f32[16,13,16,128]{3,2,1,0:T(8,128)S(1)} %all_to_all.10.in_ref, f32[3,5,256,128]{3,2,1,0:T(8,128)S(1)} %shard_map.76.held_ref, ...), custom_call_target="tpu_custom_call" | custom-call | tf_op jit(solution)/shard_map/pallas_call | solution.py:513
  71.3 3.0 %collective-permute-done.6.source_ref = f32[4,3,256,128]{3,2,1,0:T(8,128)S(1)} collective-permute-done((f32[4,3,256,128]{3,2,1,0:T(8,128)S(1)}, f32[4,3,256,128]{3,2,1,0:T(8,128)S(1)}, u32[]{:S(2)}, u32[]{:S(2)}) %collective-permute-start.6) | collective-permute-done | bytes 1572896 | tf_op jit(solution)/shard_map/ppermute | solution.py:534
  74.4 2.7 %shard_map.78.driven_ref = f32[12,256,128]{2,1,0:T(8,128)S(1)} custom-call(f32[7]{0:T(128)S(1)} %convert_element_type.33.edge_ref.flag_ref, f32[2,256,128]{2,1,0:T(8,128)S(1)} %get-tuple-element.14.waves_ref, f32[3,256,128]{2,1,0:T(8,128)S(1)} %get-tuple-element.15.sums_ref, f32[4,3,256,128]{3,2,1,0:T(8,128)S(1)} %shard_map.77.own_ref, ...), custom_call_target="tpu_custom_call" | custom-call | tf_op jit(solution)/shard_map/pallas_call | solution.py:513
  77.0 5.3 %shard_map.79.last_ref = f32[17,256,128]{2,1,0:T(8,128)S(1)} custom-call(f32[7]{0:T(128)S(1)} %convert_element_type.33.edge_ref.flag_ref, f32[16,13,16,128]{3,2,1,0:T(8,128)S(1)} %all_to_all.10.in_ref, f32[12,256,128]{2,1,0:T(8,128)S(1)} %shard_map.78.driven_ref, f32[4,3,256,128]{3,2,1,0:T(8,128)S(1)} %shard_map.77.own_ref, ...), custom_call_target="tpu_custom_call" | custom-call | tf_op jit(solution)/shard_map/pallas_call | solution.py:513
  82.3 3.6 %shard_map.80 = f32[16,19,16,128]{3,2,1,0:T(8,128)S(1)} custom-call(f32[7]{0:T(128)S(1)} %convert_element_type.33.edge_ref.flag_ref, f32[17,256,128]{2,1,0:T(8,128)S(1)} %shard_map.79.last_ref, bf16[10,256,768]{2,1,0:T(8,128)(2,1)S(1)} %copy-done.1, bf16[3,384,128]{2,1,0:T(8,128)(2,1)S(1)} %get-tuple-element.12.right_ref), custom_call_target="tpu_custom_call" | custom-call | tf_op jit(solution)/shard_map/pallas_call | solution.py:513
  86.0 38.5 %all_to_all.11.back_ref = f32[16,19,16,128]{3,2,1,0:T(8,128)S(1)} all-to-all(f32[16,19,16,128]{3,2,1,0:T(8,128)S(1)} %shard_map.80), channel_id=1, replica_groups=mesh['section'=2,'stream'=16,'slab'=8] {'stream'}, dimensions={0} | all-to-all | bytes 4980736 | tf_op jit(solution)/shard_map/all_to_all | solution.py:538
  124.4 1.1 shard_map.82
  125.6 1.5 %shard_map.81 = (f32[4,16,16,128]{3,2,1,0:T(8,128)S(1)}, f32[46,16,128]{2,1,0:T(8,128)S(1)}, f32[46,16,128]{2,1,0:T(8,128)S(1)}) custom-call(f32[7]{0:T(128)S(1)} %convert_element_type.33.edge_ref.flag_ref, f32[16,19,16,128]{3,2,1,0:T(8,128)S(1)} %all_to_all.11.back_ref), custom_call_target="tpu_custom_call" | custom-call | tf_op jit(solution)/shard_map/pallas_call | solution.py:513
  128.3 2.1 %collective-permute-start.9 = (f32[46,16,128]{2,1,0:T(8,128)S(1)}, f32[46,16,128]{2,1,0:T(8,128)S(1)}, u32[]{:S(2)}, u32[]{:S(2)}) collective-permute-start(f32[46,16,128]{2,1,0:T(8,128)S(1)} %fusion.2), channel_id=1, source_target_pairs={{1,0},{2,1},{3,2},{4,3},{5,4},{6,5},{7,6},{0,7},{9,8},{10,9},{11,1... | collective-permute-start | bytes 1130504 | tf_op jit(solution)/shard_map/ppermute | solution.py:558
  130.4 8.6 %collective-permute-done.8 = f32[46,16,128]{2,1,0:T(8,128)S(1)} collective-permute-done((f32[46,16,128]{2,1,0:T(8,128)S(1)}, f32[46,16,128]{2,1,0:T(8,128)S(1)}, u32[]{:S(2)}, u32[]{:S(2)}) %collective-permute-start.8) | collective-permute-done | bytes 376864 | tf_op jit(solution)/shard_map/ppermute | solution.py:557
  139.0 1.4 collective-permute-done.9
  (58 shorter events, 6.0 us)
Async XLA Ops:
  0.0 4.7 %copy-start.9 = (s32[16]{0:T(128)S(1)}, s32[16]{0:T(128)}, u32[]{:S(2)}) copy-start(s32[16]{0:T(128)} %constant.37.clone) | copy-start | bytes 196
  0.0 6.0 %copy-start.4 = (f32[128,128]{1,0:T(8,128)S(1)}, f32[128,128]{1,0:T(8,128)}, u32[]{:S(2)}) copy-start(f32[128,128]{1,0:T(8,128)} %param.10) | copy-start | bytes 196612
  0.0 6.1 %copy-start.5 = (f32[128,128]{1,0:T(8,128)S(1)}, f32[128,128]{1,0:T(8,128)}, u32[]{:S(2)}) copy-start(f32[128,128]{1,0:T(8,128)} %param.12) | copy-start | bytes 196612
  0.0 6.2 %copy-start.3 = (f32[256,256]{1,0:T(8,128)S(1)}, f32[256,256]{1,0:T(8,128)}, u32[]{:S(2)}) copy-start(f32[256,256]{1,0:T(8,128)} %fx_ref.1) | copy-start | bytes 786436
  0.0 6.2 %copy-start.2 = (f32[256,256]{1,0:T(8,128)S(1)}, f32[256,256]{1,0:T(8,128)}, u32[]{:S(2)}) copy-start(f32[256,256]{1,0:T(8,128)} %dx_ref.1) | copy-start | bytes 786436
  1.4 9.1 %collective-permute-start = (f32[34,16,128]{2,1,0:T(8,128)S(1)}, f32[34,16,128]{2,1,0:T(8,128)S(1)}, u32[]{:S(2)}, u32[]{:S(2)}) collective-permute-start(f32[34,16,128]{2,1,0:T(8,128)S(1)} %pad_maximum_fusion), channel_id=1, source_target_pairs={{0,1},{1,2},{2,3},{3,4},{4,5},{5,6},{6,7},{7,0},{8,9},{9,10},{10,1... | collective-permute-start | bytes 835592 | tf_op jit(solution)/shard_map/ppermute | solution.py:490
  4.6 9.4 %collective-permute-start.1 = (f32[34,16,128]{2,1,0:T(8,128)S(1)}, f32[34,16,128]{2,1,0:T(8,128)S(1)}, u32[]{:S(2)}, u32[]{:S(2)}) collective-permute-start(f32[34,16,128]{2,1,0:T(8,128)S(1)} %pad_maximum_fusion.1), channel_id=1, source_target_pairs={{1,0},{2,1},{3,2},{4,3},{5,4},{6,5},{7,6},{0,7},{9,8},{10,9},{11,1... | collective-permute-start | bytes 835592 | tf_op jit(solution)/shard_map/ppermute | solution.py:493
  8.1 36.9 %copy-start = (bf16[10,256,768]{2,1,0:T(8,128)(2,1)}, bf16[10,256,768]{2,1,0:T(8,128)(2,1)S(1)}, u32[]{:S(2)}) copy-start(bf16[10,256,768]{2,1,0:T(8,128)(2,1)S(1)} %get-tuple-element.13.left_ref) | copy-start | bytes 11796484
  47.6 17.1 %copy-start.8 = (s32[16,1]{0,1:T(1,128)S(1)}, s32[16,1]{0,1:T(1,128)}, u32[]{:S(2)}) copy-start(s32[16,1]{0,1:T(1,128)} %param.8) | copy-start | bytes 196
  47.6 1.8 %collective-permute-start.2 = (f32[3,256,128]{2,1,0:T(8,128)S(1)}, f32[3,256,128]{2,1,0:T(8,128)S(1)}, u32[]{:S(2)}, u32[]{:S(2)}) collective-permute-start(f32[3,256,128]{2,1,0:T(8,128)S(1)} %get-tuple-element.15.sums_ref), channel_id=1, source_target_pairs={{0,128},{128,0},{1,129},{129,1},{2,130},{130,2},{3,131},{131,3},{4... | collective-permute-start | bytes 1179656 | tf_op jit(solution)/shard_map/ppermute | solution.py:526
  49.5 13.3 %collective-permute-start.4 = (f32[3,256,128]{2,1,0:T(8,128)S(1)}, f32[3,256,128]{2,1,0:T(8,128)S(1)}, u32[]{:S(2)}, u32[]{:S(2)}) collective-permute-start(f32[3,256,128]{2,1,0:T(8,128)S(1)} %broadcast_select_fusion), channel_id=1, source_target_pairs={{0,32},{32,8},{8,40},{40,16},{16,48},{48,24},{24,56},{56,120},{120... | collective-permute-start | bytes 1179656 | tf_op jit(solution)/shard_map/ppermute | solution.py:528
  50.0 12.8 %collective-permute-start.3 = (f32[3,256,128]{2,1,0:T(8,128)S(1)}, f32[3,256,128]{2,1,0:T(8,128)S(1)}, u32[]{:S(2)}, u32[]{:S(2)}) collective-permute-start(f32[3,256,128]{2,1,0:T(8,128)S(1)} %broadcast_select_fusion), channel_id=1, source_target_pairs={{0,71},{32,0},{8,32},{40,8},{16,40},{48,16},{24,48},{56,24},{120,5... | collective-permute-start | bytes 1179656 | tf_op jit(solution)/shard_map/ppermute | solution.py:528
  64.7 3.7 %collective-permute-start.5 = (f32[3,256,128]{2,1,0:T(8,128)}, f32[3,256,128]{2,1,0:T(8,128)}, u32[]{:S(2)}, u32[]{:S(2)}) collective-permute-start(f32[3,256,128]{2,1,0:T(8,128)} %multiply_subtract_fusion), channel_id=1, source_target_pairs={{0,128},{128,0},{1,129},{129,1},{2,130},{130,2},{3,131},{131,3},{4... | collective-permute-start | bytes 1179656 | tf_op jit(solution)/shard_map/ppermute | solution.py:529
  64.9 2.1 %copy-start.1 = (bf16[10,256,768]{2,1,0:T(8,128)(2,1)S(1)}, bf16[10,256,768]{2,1,0:T(8,128)(2,1)}, u32[]{:S(2)}) copy-start(bf16[10,256,768]{2,1,0:T(8,128)(2,1)} %copy-done) | copy-start | bytes 11796484
  70.7 3.6 %collective-permute-start.6 = (f32[4,3,256,128]{3,2,1,0:T(8,128)S(1)}, f32[4,3,256,128]{3,2,1,0:T(8,128)S(1)}, u32[]{:S(2)}, u32[]{:S(2)}) collective-permute-start(f32[4,3,256,128]{3,2,1,0:T(8,128)S(1)} %shard_map.77.own_ref), channel_id=1, source_target_pairs={{0,128},{128,0},{1,129},{129,1},{2,130},{130,2},{3,131},{131,3},{4... | collective-permute-start | bytes 4718600 | tf_op jit(solution)/shard_map/ppermute | solution.py:534
  125.5 2.6 %copy-start.7 = (pred[46]{0:T(512)(128)(4,1)S(1)}, pred[46]{0:T(512)(128)(4,1)}, u32[]{:S(2)}) copy-start(pred[46]{0:T(512)(128)(4,1)} %constant.36.clone.1) | copy-start | bytes 142
  125.5 2.4 %collective-permute-start.7 = (f32[100,16,128]{2,1,0:T(8,128)S(1)}, f32[100,16,128]{2,1,0:T(8,128)S(1)}, u32[]{:S(2)}, u32[]{:S(2)}) collective-permute-start(f32[100,16,128]{2,1,0:T(8,128)S(1)} %shard_map.82), channel_id=1, source_target_pairs={{0,128},{128,0},{1,129},{129,1},{2,130},{130,2},{3,131},{131,3},{4... | collective-permute-start | bytes 2457608 | tf_op jit(solution)/shard_map/ppermute | solution.py:542
  128.0 12.5 %copy-start.6 = (pred[16]{0:T(512)(128)(4,1)S(1)}, pred[16]{0:T(512)(128)(4,1)}, u32[]{:S(2)}) copy-start(pred[16]{0:T(512)(128)(4,1)} %constant.34.clone.1) | copy-start | bytes 52
  128.1 10.9 %collective-permute-start.8 = (f32[46,16,128]{2,1,0:T(8,128)S(1)}, f32[46,16,128]{2,1,0:T(8,128)S(1)}, u32[]{:S(2)}, u32[]{:S(2)}) collective-permute-start(f32[46,16,128]{2,1,0:T(8,128)S(1)} %add_add_fusion), channel_id=1, source_target_pairs={{0,1},{1,2},{2,3},{3,4},{4,5},{5,6},{6,7},{7,0},{8,9},{9,10},{10,1... | collective-permute-start | bytes 1130504 | tf_op jit(solution)/shard_map/ppermute | solution.py:557
  128.3 12.1 %collective-permute-start.9 = (f32[46,16,128]{2,1,0:T(8,128)S(1)}, f32[46,16,128]{2,1,0:T(8,128)S(1)}, u32[]{:S(2)}, u32[]{:S(2)}) collective-permute-start(f32[46,16,128]{2,1,0:T(8,128)S(1)} %fusion.2), channel_id=1, source_target_pairs={{1,0},{2,1},{3,2},{4,3},{5,4},{6,5},{7,6},{0,7},{9,8},{10,9},{11,1... | collective-permute-start | bytes 1130504 | tf_op jit(solution)/shard_map/ppermute | solution.py:558

commit v6 on v5

--- a/solution.py
+++ b/solution.py
@@ -25,7 +25,7 @@
         body,
         out_shape=out_shape,
         scratch_shapes=scratch,
-        compiler_params=pltpu.CompilerParams(vmem_limit_bytes=40 * 2**20),
+        compiler_params=pltpu.CompilerParams(vmem_limit_bytes=24 * 2**20),
         cost_estimate=pl.CostEstimate(flops=flops, bytes_accessed=moved, transcendentals=0),
     )(*args)
 
@@ -96,6 +96,15 @@
         right_ref[i] = right_form(others[name])
 
 
+def prepare_later_kernel(after_ref, *refs):
+    prepare_kernel(*refs)
+
+
+def far_kernel(flag_ref, up_ref, down_ref, after_ref, out_ref):
+    for n in range(out_ref.shape[0]):
+        out_ref[n] = flag_ref[5] * up_ref[n] - flag_ref[6] * down_ref[n]
+
+
 class Products:
     def __init__(self, left_ref, right_ref):
         self.left_ref, self.right_ref = left_ref, right_ref
@@ -290,12 +299,13 @@
             out_ref[n, k] = start[k] + change[k]
 
 
-def source_kernel(flag_ref, region_ref, in_ref, held_ref, up_ref, down_ref, far_ref, left_ref, right_ref, out_ref):
+def source_kernel(flag_ref, in_ref, held_ref, up_ref, down_ref, far_ref, left_ref, right_ref, out_ref):
     do = Products(left_ref, right_ref)
     nx, nz = up_ref.shape[1:]
     row = lax.broadcasted_iota(jnp.int32, (nx, nz), 0)
     lane = lax.broadcasted_iota(jnp.int32, (nx, nz), 1)
-    region = region_ref[...]
+    blocks = flag_ref.shape[0] - 7
+    region = jnp.concatenate([jnp.full((nx // blocks, nz), flag_ref[7 + i], f32) for i in range(blocks)], axis=0)
 
     def slope_x(value):
         ahead = jnp.where(row == nx - 1, 0.0, pltpu.roll(value, nx - 1, 0))
@@ -478,13 +488,9 @@
         inverse[stream] = j
     y = slab * streams + jnp.asarray(inverse, jnp.int32)[lax.axis_index("stream")]
     last_y = slabs * streams - 1
-    edges = jnp.stack(
-        [slab > 0, slab < slabs - 1, lax.axis_index("section") == 0]
-        + [y < last_y, y > 0, y < last_y - 1, y > 1]
-    ).astype(f32)
-    region = jnp.repeat(source_mask[:, 0].astype(f32), nx // source_mask.shape[0])
-    region = jnp.broadcast_to(region[:, None], (nx, nz))
-
+    flags = [slab > 0, slab < slabs - 1, lax.axis_index("section") == 0]
+    flags += [y < last_y, y > 0, y < last_y - 1, y > 1]
+    edges = jnp.concatenate([jnp.stack(flags).astype(f32), source_mask[:, 0].astype(f32)])
     raw = jnp.swapaxes(state[0], 1, 2)
     reaches = (IN_P, IN_U, IN_V, IN_W)
     from_low = lax.ppermute(
@@ -493,18 +499,12 @@
     from_high = lax.ppermute(
         jnp.concatenate([raw[i, :reach] for i, reach in enumerate(reaches)]), "slab", downward
     )
-    left, right = call(
-        prepare_kernel,
-        (
-            jax.ShapeDtypeStruct((len(LEFT), nx, 3 * nx), bf16),
-            jax.ShapeDtypeStruct((len(RIGHT), 3 * nz, nz), bf16),
-        ),
-        deriv_x,
-        deriv_z.T,
-        filter_x,
-        filter_z.T,
-        flops=10**9,
-    )
+    forms = (
+        jax.ShapeDtypeStruct((len(LEFT), nx, 3 * nx), bf16),
+        jax.ShapeDtypeStruct((len(RIGHT), 3 * nz, nz), bf16),
+    )
+    matrices = (deriv_x, deriv_z.T, filter_x, filter_z.T)
+    left, right = call(prepare_kernel, forms, *matrices, flops=10**9)
 
     def shape(*dims):
         return jax.ShapeDtypeStruct(dims, f32)
@@ -515,7 +515,7 @@
             out_shape=out_shape,
             in_specs=[pl.BlockSpec(memory_space=pltpu.SMEM)]
             + [pl.BlockSpec(memory_space=pltpu.VMEM)] * len(args),
-            compiler_params=pltpu.CompilerParams(vmem_limit_bytes=40 * 2**20),
+            compiler_params=pltpu.CompilerParams(vmem_limit_bytes=24 * 2**20),
         )(edges, *args)
 
     spread = with_edges(spread_kernel, shape(own, 13, xs, nz), raw, from_low, from_high, right)
@@ -526,10 +526,24 @@
     across = lax.ppermute(sums, "section", swap)
     carried = jnp.where(edges[2] > 0, sums, across)
     up, down = [lax.ppermute(carried, AXES, along_y(steps)) for steps in (-1, 1)]
-    far = lax.ppermute(edges[5] * up - edges[6] * down, "section", swap)
+    vmem, anywhere = pl.BlockSpec(memory_space=pltpu.VMEM), pl.BlockSpec(memory_space=pl.ANY)
+    left, right = pl.pallas_call(
+        prepare_later_kernel,
+        out_shape=forms,
+        in_specs=[anywhere] + [vmem] * 4,
+        compiler_params=pltpu.CompilerParams(vmem_limit_bytes=24 * 2**20),
+        cost_estimate=pl.CostEstimate(flops=10**9, bytes_accessed=8 * 10**6, transcendentals=0),
+    )(sums, *matrices)
     held = call(held_kernel, shape(3, 5, nx, nz), planes, sums, left, right, flops=10**9)
+    far = pl.pallas_call(
+        far_kernel,
+        out_shape=shape(3, nx, nz),
+        in_specs=[pl.BlockSpec(memory_space=pltpu.SMEM), vmem, vmem, anywhere],
+        compiler_params=pltpu.CompilerParams(vmem_limit_bytes=8 * 2**20),
+    )(edges, up, down, held)
+    far = lax.ppermute(far, "section", swap)
     source = with_edges(
-        source_kernel, shape(4, 3, nx, nz), region, planes, held, up, down, far, left, right
+        source_kernel, shape(4, 3, nx, nz), planes, held, up, down, far, left, right
     )
     moved = lax.ppermute(source, "section", swap)
     driven = with_edges(driven_kernel, shape(12, nx, nz), waves, sums, source, moved, left, right)

time: 143 us -> 139 us (0.972)
  local copies, waits for them, and re-layouts: 6.2 us -> 3.87 us
  Pallas kernels: 23.4 us -> 25.6 us
  other arithmetic: 2.3 us -> 0.47 us
  waiting for transfers between devices: 29.1 us -> 27.4 us
    ppermute x2, waiting for transfers between devices: 8.84 us -> 5.45 us  [shards(): lax.ppermute(carried, AXES, along_y(steps))]
    pallas_call x0 -> x2, Pallas kernels: none -> 2.46 us  [the longest x1 1.87 us: shards(): pl.pallas_call(prepare_later_kernel, out_shape=forms, in_specs=[anywhere]...]
    unnamed x23 -> x19, local copies, waits for them, and re-layouts: 3.61 us -> 1.48 us
    sub x1 -> x0, other arithmetic: 1.91 us -> none  [shards(): far = lax.ppermute(edges[5] * up - edges[6] * down, 'section', swap)]
    ppermute x1, waiting for transfers between devices: 0.01 us -> 1.71 us  [shards(): far = lax.ppermute(far, 'section', swap)]
  transfers between devices with their start and end apart: 10 -> 10, of which waited for: 8 -> 9; matrix products, arithmetic and copies ran while one was open for 1% -> 1% of each run, Pallas kernels for 3% -> 5%
where the time goes in v6:
time: 139 us; the launch traced here: 138 us
  blocking collectives  68 us (49%)
  waiting for transfers between devices  27.4 us (20%)
  Pallas kernels  25.6 us (18%)
  starting transfers between devices  10.6 us (8%)
  local copies, waits for them, and re-layouts  3.87 us (3%)
  between operations  1.64 us (1%)
    all_to_all x1, blocking collectives, shards(): lax.all_to_all(done, 'stream', split_axis=0, concat_axis=0, tiled=True)  38.3 us
    all_to_all x1, blocking collectives, shards(): lax.all_to_all(spread, 'stream', split_axis=0, concat_axis=0, tiled=True)  29.8 us
    pallas_call x7, Pallas kernels, with_edges(): pl.pallas_call(body, out_shape=out_shape, in_specs=[pl.BlockSpec(memory_s...  17.1 us
    ppermute x1, waiting for transfers between devices, shards(): from_low = lax.ppermute(high + sum(more_high), 'slab', upward)  8.58 us
    pallas_call x3, Pallas kernels, call(): pl.pallas_call(body, out_shape=out_shape, scratch_shapes=scratch, compile...  6.01 us
    ppermute x2, waiting for transfers between devices, shards(): lax.ppermute(carried, AXES, along_y(steps))  5.45 us
    ppermute x2, starting transfers between devices, shards(): lax.ppermute(carried, AXES, along_y(steps))  4.51 us
    ppermute x1, waiting for transfers between devices, shards(): lax.ppermute(jnp.concatenate([raw[i, :reach] for i, reach in enumerate(re...  3.51 us
  transfers between devices with their start and end apart: 10, of which 9 were waited for; matrix products, arithmetic and copies ran while one was open for 1% of the time, Pallas kernels for 5%

profile of v6, /device:TPU:96, one launch (start us, length us, event | category | flops | bytes accessed | tf_op | source)
XLA Modules:
  0.0 137.6 jit_solution(3570486373428476050)
XLA Ops:
  0.0 1.3 copy.13
  1.4 3.2 %collective-permute-start = (f32[34,16,128]{2,1,0:T(8,128)S(1)}, f32[34,16,128]{2,1,0:T(8,128)S(1)}, u32[]{:S(2)}, u32[]{:S(2)}) collective-permute-start(f32[34,16,128]{2,1,0:T(8,128)S(1)} %pad_maximum_fusion), channel_id=1, source_target_pairs={{0,1},{1,2},{2,3},{3,4},{4,5},{5,6},{6,7},{7,0},{8,9},{9,10},{10,1... | collective-permute-start | bytes 835592 | tf_op jit(solution)/shard_map/ppermute | solution.py:496
  6.3 1.9 %shard_map.73 = (bf16[10,256,768]{2,1,0:T(8,128)(2,1)S(1)}, bf16[3,384,128]{2,1,0:T(8,128)(2,1)S(1)}) custom-call(f32[256,256]{1,0:T(8,128)S(1)} %copy-done, f32[128,128]{1,0:T(8,128)S(1)} %bitcast.61, f32[256,256]{1,0:T(8,128)S(1)} %copy-done.1, f32[128,128]{1,0:T(8,128)S(1)} %bitcast.63), custom_call_target="tpu_custom_call" | custom-call | flops 1000000000 | bytes 655360 | tf_op jit(solution)/shard_map/pallas_call | solution.py:24
  8.3 2.2 %collective-permute-done.low_ref = f32[34,16,128]{2,1,0:T(8,128)S(1)} collective-permute-done((f32[34,16,128]{2,1,0:T(8,128)S(1)}, f32[34,16,128]{2,1,0:T(8,128)S(1)}, u32[]{:S(2)}, u32[]{:S(2)}) %collective-permute-start) | collective-permute-done | bytes 278560 | tf_op jit(solution)/shard_map/ppermute | solution.py:496
  10.5 3.5 %collective-permute-done.1.high_ref = f32[34,16,128]{2,1,0:T(8,128)S(1)} collective-permute-done((f32[34,16,128]{2,1,0:T(8,128)S(1)}, f32[34,16,128]{2,1,0:T(8,128)S(1)}, u32[]{:S(2)}, u32[]{:S(2)}) %collective-permute-start.1) | collective-permute-done | bytes 278560 | tf_op jit(solution)/shard_map/ppermute | solution.py:499
  14.0 1.3 shard_map.74
  15.3 29.8 %all_to_all.10.in_ref = f32[16,13,16,128]{3,2,1,0:T(8,128)S(1)} all-to-all(f32[16,13,16,128]{3,2,1,0:T(8,128)S(1)} %shard_map.74), channel_id=1, replica_groups=mesh['section'=2,'stream'=16,'slab'=8] {'stream'}, dimensions={0} | all-to-all | bytes 3407872 | tf_op jit(solution)/shard_map/all_to_all | solution.py:522
  45.0 2.6 %shard_map.75 = (f32[2,256,128]{2,1,0:T(8,128)S(1)}, f32[3,256,128]{2,1,0:T(8,128)S(1)}) custom-call(f32[16,13,16,128]{3,2,1,0:T(8,128)S(1)} %all_to_all.10.in_ref, bf16[10,256,768]{2,1,0:T(8,128)(2,1)S(1)} %get-tuple-element.15.left_ref, bf16[3,384,128]{2,1,0:T(8,128)(2,1)S(1)} %get-tuple-element.14.right_ref), custom_call_target="tpu_custom_call" | custom-call | flops 2000000000 | bytes 5931008 | tf_op jit(solution)/shard_map/pallas_call | solution.py:24
  50.1 3.9 %collective-permute-start.3 = (f32[3,256,128]{2,1,0:T(8,128)S(1)}, f32[3,256,128]{2,1,0:T(8,128)S(1)}, u32[]{:S(2)}, u32[]{:S(2)}) collective-permute-start(f32[3,256,128]{2,1,0:T(8,128)S(1)} %broadcast_select_fusion), channel_id=1, source_target_pairs={{0,71},{32,0},{8,32},{40,8},{16,40},{48,16},{24,48},{56,24},{120,5... | collective-permute-start | bytes 1179656 | tf_op jit(solution)/shard_map/ppermute | solution.py:528
  54.0 1.9 %shard_map.76 = (bf16[10,256,768]{2,1,0:T(8,128)(2,1)S(1)}, bf16[3,384,128]{2,1,0:T(8,128)(2,1)S(1)}) custom-call(f32[3,256,128]{2,1,0:T(8,128)S(1)} %get-tuple-element.17.after_ref.sums_ref, f32[256,256]{1,0:T(8,128)S(1)} %copy-done, f32[128,128]{1,0:T(8,128)S(1)} %bitcast.62, f32[256,256]{1,0:T(8,128)S(1)} %copy-done.1, f32[128,128]{1,0:T(8,128)S(1)} %bitcast.64), custom_call_target="tpu_custom_call" | custom-call | flops 1000000000 | bytes 8000000 | tf_op jit(solution)/shard_map/pallas_call | solution.py:530
  55.9 1.5 %shard_map.77.after_ref.held_ref = f32[3,5,256,128]{3,2,1,0:T(8,128)S(1)} custom-call(f32[16,13,16,128]{3,2,1,0:T(8,128)S(1)} %all_to_all.10.in_ref, f32[3,256,128]{2,1,0:T(8,128)S(1)} %get-tuple-element.17.after_ref.sums_ref, bf16[10,256,768]{2,1,0:T(8,128)(2,1)S(1)} %get-tuple-element.18.left_ref, bf16[3,384,128]{2,1,0:T(8,128)(2,1)S(1)} %get-tuple-element.19.right_ref), custom_call_target="tpu_custom_call" | custom-call | flops 1000000000 | bytes 6324224 | tf_op jit(solution)/shard_map/pallas_call | solution.py:24
  57.4 5.4 %collective-permute-done.4.down_ref = f32[3,256,128]{2,1,0:T(8,128)S(1)} collective-permute-done((f32[3,256,128]{2,1,0:T(8,128)S(1)}, f32[3,256,128]{2,1,0:T(8,128)S(1)}, u32[]{:S(2)}, u32[]{:S(2)}) %collective-permute-start.4) | collective-permute-done | bytes 393248 | tf_op jit(solution)/shard_map/ppermute | solution.py:528
  63.8 1.7 %collective-permute-done.5.far_ref = f32[3,256,128]{2,1,0:T(8,128)S(1)} collective-permute-done((f32[3,256,128]{2,1,0:T(8,128)S(1)}, f32[3,256,128]{2,1,0:T(8,128)S(1)}, u32[]{:S(2)}, u32[]{:S(2)}) %collective-permute-start.5) | collective-permute-done | bytes 393248 | tf_op jit(solution)/shard_map/ppermute | solution.py:544
  65.5 1.7 %shard_map.79.own_ref = f32[4,3,256,128]{3,2,1,0:T(8,128)S(1)} custom-call(f32[23]{0:T(128)S(1)} %pad_maximum_fusion.2.edge_ref.flag_ref, f32[16,13,16,128]{3,2,1,0:T(8,128)S(1)} %all_to_all.10.in_ref, f32[3,5,256,128]{3,2,1,0:T(8,128)S(1)} %shard_map.77.after_ref.held_ref, f32[3,256,128]{2,1,0:T(8,128)S(1)} %collective-permute-done.3.up_ref, ...), custom_call_target="tpu_custom_call" | custom-call | tf_op jit(solution)/shard_map/pallas_call | solution.py:513
  67.4 3.3 %collective-permute-done.6.source_ref = f32[4,3,256,128]{3,2,1,0:T(8,128)S(1)} collective-permute-done((f32[4,3,256,128]{3,2,1,0:T(8,128)S(1)}, f32[4,3,256,128]{3,2,1,0:T(8,128)S(1)}, u32[]{:S(2)}, u32[]{:S(2)}) %collective-permute-start.6) | collective-permute-done | bytes 1572896 | tf_op jit(solution)/shard_map/ppermute | solution.py:548
  70.7 2.7 %shard_map.80.driven_ref = f32[12,256,128]{2,1,0:T(8,128)S(1)} custom-call(f32[23]{0:T(128)S(1)} %pad_maximum_fusion.2.edge_ref.flag_ref, f32[2,256,128]{2,1,0:T(8,128)S(1)} %get-tuple-element.16.waves_ref, f32[3,256,128]{2,1,0:T(8,128)S(1)} %get-tuple-element.17.after_ref.sums_ref, f32[4,3,256,128]{3,2,1,0:T(8,128)S(1)} %shard_map.79.own_ref, ...), custom_call_target="tpu_custom_call" | custom-call | tf_op jit(solution)/shard_map/pallas_call | solution.py:513
  73.4 5.4 %shard_map.81.last_ref = f32[17,256,128]{2,1,0:T(8,128)S(1)} custom-call(f32[23]{0:T(128)S(1)} %pad_maximum_fusion.2.edge_ref.flag_ref, f32[16,13,16,128]{3,2,1,0:T(8,128)S(1)} %all_to_all.10.in_ref, f32[12,256,128]{2,1,0:T(8,128)S(1)} %shard_map.80.driven_ref, f32[4,3,256,128]{3,2,1,0:T(8,128)S(1)} %shard_map.79.own_ref, ...), custom_call_target="tpu_custom_call" | custom-call | tf_op jit(solution)/shard_map/pallas_call | solution.py:513
  78.8 3.4 %shard_map.82 = f32[16,19,16,128]{3,2,1,0:T(8,128)S(1)} custom-call(f32[23]{0:T(128)S(1)} %pad_maximum_fusion.2.edge_ref.flag_ref, f32[17,256,128]{2,1,0:T(8,128)S(1)} %shard_map.81.last_ref, bf16[10,256,768]{2,1,0:T(8,128)(2,1)S(1)} %get-tuple-element.18.left_ref, bf16[3,384,128]{2,1,0:T(8,128)(2,1)S(1)} %get-tuple-element.19.right_ref), custom_call_target="tpu_custom_call" | custom-call | tf_op jit(solution)/shard_map/pallas_call | solution.py:513
  82.2 38.3 %all_to_all.11.back_ref = f32[16,19,16,128]{3,2,1,0:T(8,128)S(1)} all-to-all(f32[16,19,16,128]{3,2,1,0:T(8,128)S(1)} %shard_map.82), channel_id=1, replica_groups=mesh['section'=2,'stream'=16,'slab'=8] {'stream'}, dimensions={0} | all-to-all | bytes 4980736 | tf_op jit(solution)/shard_map/all_to_all | solution.py:552
  120.5 1.1 shard_map.84
  121.7 1.5 %shard_map.83 = (f32[4,16,16,128]{3,2,1,0:T(8,128)S(1)}, f32[46,16,128]{2,1,0:T(8,128)S(1)}, f32[46,16,128]{2,1,0:T(8,128)S(1)}) custom-call(f32[23]{0:T(128)S(1)} %pad_maximum_fusion.2.edge_ref.flag_ref, f32[16,19,16,128]{3,2,1,0:T(8,128)S(1)} %all_to_all.11.back_ref), custom_call_target="tpu_custom_call" | custom-call | tf_op jit(solution)/shard_map/pallas_call | solution.py:513
  124.4 2.1 %collective-permute-start.9 = (f32[46,16,128]{2,1,0:T(8,128)S(1)}, f32[46,16,128]{2,1,0:T(8,128)S(1)}, u32[]{:S(2)}, u32[]{:S(2)}) collective-permute-start(f32[46,16,128]{2,1,0:T(8,128)S(1)} %fusion.2), channel_id=1, source_target_pairs={{1,0},{2,1},{3,2},{4,3},{5,4},{6,5},{7,6},{0,7},{9,8},{10,9},{11,1... | collective-permute-start | bytes 1130504 | tf_op jit(solution)/shard_map/ppermute | solution.py:572
  126.5 8.6 %collective-permute-done.8 = f32[46,16,128]{2,1,0:T(8,128)S(1)} collective-permute-done((f32[46,16,128]{2,1,0:T(8,128)S(1)}, f32[46,16,128]{2,1,0:T(8,128)S(1)}, u32[]{:S(2)}, u32[]{:S(2)}) %collective-permute-start.8) | collective-permute-done | bytes 376864 | tf_op jit(solution)/shard_map/ppermute | solution.py:571
  135.1 1.4 %collective-permute-done.9 = f32[46,16,128]{2,1,0:T(8,128)S(1)} collective-permute-done((f32[46,16,128]{2,1,0:T(8,128)S(1)}, f32[46,16,128]{2,1,0:T(8,128)S(1)}, u32[]{:S(2)}, u32[]{:S(2)}) %collective-permute-start.9) | collective-permute-done | bytes 376864 | tf_op jit(solution)/shard_map/ppermute | solution.py:572
  (53 shorter events, 6.4 us)
Async XLA Ops:
  0.0 4.7 %copy-start.7 = (s32[16]{0:T(128)S(1)}, s32[16]{0:T(128)}, u32[]{:S(2)}) copy-start(s32[16]{0:T(128)} %constant.37.clone) | copy-start | bytes 196
  0.0 6.1 %copy-start.2 = (f32[128,128]{1,0:T(8,128)S(1)}, f32[128,128]{1,0:T(8,128)}, u32[]{:S(2)}) copy-start(f32[128,128]{1,0:T(8,128)} %param.10) | copy-start | bytes 196612
  0.0 6.2 %copy-start.3 = (f32[128,128]{1,0:T(8,128)S(1)}, f32[128,128]{1,0:T(8,128)}, u32[]{:S(2)}) copy-start(f32[128,128]{1,0:T(8,128)} %param.12) | copy-start | bytes 196612
  0.0 6.3 %copy-start.1 = (f32[256,256]{1,0:T(8,128)S(1)}, f32[256,256]{1,0:T(8,128)}, u32[]{:S(2)}) copy-start(f32[256,256]{1,0:T(8,128)} %refs_2_.1) | copy-start | bytes 786436
  0.0 6.3 %copy-start = (f32[256,256]{1,0:T(8,128)S(1)}, f32[256,256]{1,0:T(8,128)}, u32[]{:S(2)}) copy-start(f32[256,256]{1,0:T(8,128)} %refs_0_.1) | copy-start | bytes 786436
  1.4 9.1 %collective-permute-start = (f32[34,16,128]{2,1,0:T(8,128)S(1)}, f32[34,16,128]{2,1,0:T(8,128)S(1)}, u32[]{:S(2)}, u32[]{:S(2)}) collective-permute-start(f32[34,16,128]{2,1,0:T(8,128)S(1)} %pad_maximum_fusion), channel_id=1, source_target_pairs={{0,1},{1,2},{2,3},{3,4},{4,5},{5,6},{6,7},{7,0},{8,9},{9,10},{10,1... | collective-permute-start | bytes 835592 | tf_op jit(solution)/shard_map/ppermute | solution.py:496
  4.6 9.4 %collective-permute-start.1 = (f32[34,16,128]{2,1,0:T(8,128)S(1)}, f32[34,16,128]{2,1,0:T(8,128)S(1)}, u32[]{:S(2)}, u32[]{:S(2)}) collective-permute-start(f32[34,16,128]{2,1,0:T(8,128)S(1)} %pad_maximum_fusion.1), channel_id=1, source_target_pairs={{1,0},{2,1},{3,2},{4,3},{5,4},{6,5},{7,6},{0,7},{9,8},{10,9},{11,1... | collective-permute-start | bytes 835592 | tf_op jit(solution)/shard_map/ppermute | solution.py:499
  6.1 2.1 %copy-start.6 = (s32[16,1]{0,1:T(1,128)S(1)}, s32[16,1]{0,1:T(1,128)}, u32[]{:S(2)}) copy-start(s32[16,1]{0,1:T(1,128)} %param.8) | copy-start | bytes 196
  47.7 1.8 %collective-permute-start.2 = (f32[3,256,128]{2,1,0:T(8,128)S(1)}, f32[3,256,128]{2,1,0:T(8,128)S(1)}, u32[]{:S(2)}, u32[]{:S(2)}) collective-permute-start(f32[3,256,128]{2,1,0:T(8,128)S(1)} %get-tuple-element.17.after_ref.sums_ref), channel_id=1, source_target_pairs={{0,128},{128,0},{1,129},{129,1},{2,130},{130,2},{3,131},{131,3},{4... | collective-permute-start | bytes 1179656 | tf_op jit(solution)/shard_map/ppermute | solution.py:526
  49.5 13.3 %collective-permute-start.4 = (f32[3,256,128]{2,1,0:T(8,128)S(1)}, f32[3,256,128]{2,1,0:T(8,128)S(1)}, u32[]{:S(2)}, u32[]{:S(2)}) collective-permute-start(f32[3,256,128]{2,1,0:T(8,128)S(1)} %broadcast_select_fusion), channel_id=1, source_target_pairs={{0,32},{32,8},{8,40},{40,16},{16,48},{48,24},{24,56},{56,120},{120... | collective-permute-start | bytes 1179656 | tf_op jit(solution)/shard_map/ppermute | solution.py:528
  50.1 12.8 %collective-permute-start.3 = (f32[3,256,128]{2,1,0:T(8,128)S(1)}, f32[3,256,128]{2,1,0:T(8,128)S(1)}, u32[]{:S(2)}, u32[]{:S(2)}) collective-permute-start(f32[3,256,128]{2,1,0:T(8,128)S(1)} %broadcast_select_fusion), channel_id=1, source_target_pairs={{0,71},{32,0},{8,32},{40,8},{16,40},{48,16},{24,48},{56,24},{120,5... | collective-permute-start | bytes 1179656 | tf_op jit(solution)/shard_map/ppermute | solution.py:528
  63.5 2.0 %collective-permute-start.5 = (f32[3,256,128]{2,1,0:T(8,128)S(1)}, f32[3,256,128]{2,1,0:T(8,128)S(1)}, u32[]{:S(2)}, u32[]{:S(2)}) collective-permute-start(f32[3,256,128]{2,1,0:T(8,128)S(1)} %shard_map.78), channel_id=1, source_target_pairs={{0,128},{128,0},{1,129},{129,1},{2,130},{130,2},{3,131},{131,3},{4... | collective-permute-start | bytes 1179656 | tf_op jit(solution)/shard_map/ppermute | solution.py:544
  67.2 3.5 %collective-permute-start.6 = (f32[4,3,256,128]{3,2,1,0:T(8,128)S(1)}, f32[4,3,256,128]{3,2,1,0:T(8,128)S(1)}, u32[]{:S(2)}, u32[]{:S(2)}) collective-permute-start(f32[4,3,256,128]{3,2,1,0:T(8,128)S(1)} %shard_map.79.own_ref), channel_id=1, source_target_pairs={{0,128},{128,0},{1,129},{129,1},{2,130},{130,2},{3,131},{131,3},{4... | collective-permute-start | bytes 4718600 | tf_op jit(solution)/shard_map/ppermute | solution.py:548
  121.6 2.6 %copy-start.5 = (pred[46]{0:T(512)(128)(4,1)S(1)}, pred[46]{0:T(512)(128)(4,1)}, u32[]{:S(2)}) copy-start(pred[46]{0:T(512)(128)(4,1)} %constant.36.clone.1) | copy-start | bytes 142
  121.6 2.4 %collective-permute-start.7 = (f32[100,16,128]{2,1,0:T(8,128)S(1)}, f32[100,16,128]{2,1,0:T(8,128)S(1)}, u32[]{:S(2)}, u32[]{:S(2)}) collective-permute-start(f32[100,16,128]{2,1,0:T(8,128)S(1)} %shard_map.84), channel_id=1, source_target_pairs={{0,128},{128,0},{1,129},{129,1},{2,130},{130,2},{3,131},{131,3},{4... | collective-permute-start | bytes 2457608 | tf_op jit(solution)/shard_map/ppermute | solution.py:556
  124.1 12.5 %copy-start.4 = (pred[16]{0:T(512)(128)(4,1)S(1)}, pred[16]{0:T(512)(128)(4,1)}, u32[]{:S(2)}) copy-start(pred[16]{0:T(512)(128)(4,1)} %constant.34.clone.1) | copy-start | bytes 52
  124.2 10.9 %collective-permute-start.8 = (f32[46,16,128]{2,1,0:T(8,128)S(1)}, f32[46,16,128]{2,1,0:T(8,128)S(1)}, u32[]{:S(2)}, u32[]{:S(2)}) collective-permute-start(f32[46,16,128]{2,1,0:T(8,128)S(1)} %add_add_fusion), channel_id=1, source_target_pairs={{0,1},{1,2},{2,3},{3,4},{4,5},{5,6},{6,7},{7,0},{8,9},{9,10},{10,1... | collective-permute-start | bytes 1130504 | tf_op jit(solution)/shard_map/ppermute | solution.py:571
  124.4 12.1 %collective-permute-start.9 = (f32[46,16,128]{2,1,0:T(8,128)S(1)}, f32[46,16,128]{2,1,0:T(8,128)S(1)}, u32[]{:S(2)}, u32[]{:S(2)}) collective-permute-start(f32[46,16,128]{2,1,0:T(8,128)S(1)} %fusion.2), channel_id=1, source_target_pairs={{1,0},{2,1},{3,2},{4,3},{5,4},{6,5},{7,6},{0,7},{9,8},{10,9},{11,1... | collective-permute-start | bytes 1130504 | tf_op jit(solution)/shard_map/ppermute | solution.py:572

commit v7 on v6

--- a/solution.py
+++ b/solution.py
@@ -54,18 +54,14 @@
     return jnp.concatenate([high, high, low], axis=0)
 
 
-def times_left(form, planes):
-    high, low = halves(jnp.concatenate(planes, axis=1))
-    out = jnp.dot(form, jnp.concatenate([high, low, high], axis=0), preferred_element_type=f32)
-    width = planes[0].shape[1]
-    return [out[:, i * width : (i + 1) * width] for i in range(len(planes))]
-
-
-def times_right(planes, form):
-    high, low = halves(jnp.concatenate(planes, axis=0))
-    out = jnp.dot(jnp.concatenate([high, low, high], axis=1), form, preferred_element_type=f32)
-    length = planes[0].shape[0]
-    return [out[i * length : (i + 1) * length] for i in range(len(planes))]
+def times_left(form, high, low):
+    high, low = jnp.concatenate(high, axis=1), jnp.concatenate(low, axis=1)
+    return jnp.dot(form, jnp.concatenate([high, low, high], axis=0), preferred_element_type=f32)
+
+
+def times_right(high, low, form):
+    high, low = jnp.concatenate(high, axis=0), jnp.concatenate(low, axis=0)
+    return jnp.dot(jnp.concatenate([high, low, high], axis=1), form, preferred_element_type=f32)
 
 
 def prepare_kernel(dx_ref, dzt_ref, fx_ref, fzt_ref, left_ref, right_ref):
@@ -108,12 +104,24 @@
 class Products:
     def __init__(self, left_ref, right_ref):
         self.left_ref, self.right_ref = left_ref, right_ref
+        self.split = {}
+
+    def halves(self, planes):
+        for value in planes:
+            if id(value) not in self.split:
+                self.split[id(value)] = (value, *halves(value))
+        found = [self.split[id(value)] for value in planes]
+        return [one[1] for one in found], [one[2] for one in found]
 
     def left(self, name, planes):
-        return times_left(self.left_ref[LEFT.index(name)], planes)
+        out = times_left(self.left_ref[LEFT.index(name)], *self.halves(planes))
+        width = planes[0].shape[1]
+        return [out[:, i * width : (i + 1) * width] for i in range(len(planes))]
 
     def right(self, planes, name):
-        return times_right(planes, self.right_ref[RIGHT.index(name)])
+        out = times_right(*self.halves(planes), self.right_ref[RIGHT.index(name)])
+        length = planes[0].shape[0]
+        return [out[i * length : (i + 1) * length] for i in range(len(planes))]
 
 
 def inside(value, reach, low_ok, high_ok):
@@ -164,7 +172,8 @@
         return 0.5 * (value[IN_P + 1 : IN_P + 1 + own] - value[IN_P - 1 : IN_P - 1 + own])
 
     rows = ext[3].shape[0]
-    through = times_right([ext[3].reshape(rows * xs, nz)], right_ref[RIGHT.index("c")])[0]
+    high, low = halves(ext[3].reshape(rows * xs, nz))
+    through = times_right([high], [low], right_ref[RIGHT.index("c")])
     cut = IN_V - IN_W
     rate = through.reshape(rows, xs, nz) + slope4(ext[2])[cut : cut + rows]
     rate = inside(rate, IN_W, low_ok, high_ok)
@@ -285,12 +294,16 @@
     out_ref[1] = p5[0]
 
 
-def held_kernel(in_ref, sums_ref, left_ref, right_ref, out_ref):
+def held_kernel(in_ref, sums_ref, left_ref, right_ref, out_ref, later_ref):
     do = Products(left_ref, right_ref)
     start = [plane(in_ref, i) for i in (3, 10, 11, 12, 9)]
     h = [sums_ref[n] for n in range(3)]
     pull_x = do.left("a", h)
     pull_z = do.right(h, "c")
+    begin = [start[0], start[4], start[1]]
+    kept = do.left("e8", begin)
+    for i in range(3):
+        later_ref[i] = begin[i] + kept[i]
     for n, growth in enumerate(("e2", "e4", "e6")):
         change = do.left(growth, start)
         out_ref[n, 0] = start[0] + change[0] - tau * pull_x[n]
@@ -395,7 +408,7 @@
             out_ref[first + k] = values[k]
 
 
-def finish_kernel(flag_ref, in_ref, driven_ref, own_ref, source_ref, left_ref, right_ref, out_ref):
+def finish_kernel(flag_ref, later_ref, driven_ref, own_ref, source_ref, left_ref, right_ref, out_ref):
     chain = Chain(left_ref, right_ref)
     do = chain.do
     drive = drives(do, flag_ref, own_ref, source_ref, 2, 4)
@@ -417,10 +430,8 @@
         fresh = arrived(n)
         total = [total[k] + kept[k] + fresh[k] for k in range(3)]
     moved = do.left("e1", total)
-    begin = [plane(in_ref, i) for i in (3, 9, 10)]
-    kept = do.left("e8", begin)
     for i in range(3):
-        out_ref[14 + i] = begin[i] + kept[i] + tau * (2.0 * total[i] + moved[i])
+        out_ref[14 + i] = later_ref[i] + tau * (2.0 * total[i] + moved[i])
 
 
 def filter_kernel(flag_ref, last_ref, left_ref, right_ref, out_ref):
@@ -432,11 +443,18 @@
         for i, value in enumerate(values):
             out_ref[:, place + i] = (value + fx[i] + fz[i]).reshape(blocks, xs, nz)
 
+    loaded = {}
+
+    def load(k):
+        if k not in loaded:
+            loaded[k] = last_ref[k]
+        return loaded[k]
+
     def p(k):
         return last_ref[k]
 
     def h(k):
-        return last_ref[8 + k]
+        return load(8 + k)
 
     def third(*which):
         return [-tau * value for value in do.right([h(k) for k in which], "c")]
@@ -448,12 +466,16 @@
 
     @pl.when(flag_ref[2] > 0)
     def _():
+        loaded.clear()
+        do.split.clear()
         axial = do.left("ta", [h(1), h(3), h(5)])
         emit(10, [p(1), p(3), p(5), p(7)] + axial + third(1))
         out_ref[:, 18] = jnp.zeros((blocks, xs, nz), f32)
 
     @pl.when(flag_ref[2] <= 0)
     def _():
+        loaded.clear()
+        do.split.clear()
         axial = do.left("ta", [h(4)])
         depth = third(4, 3, 5)
         emit(10, [p(6), axial[0], depth[0], -tau * h(4), depth[1], depth[2]])
@@ -491,14 +513,12 @@
     flags = [slab > 0, slab < slabs - 1, lax.axis_index("section") == 0]
     flags += [y < last_y, y > 0, y < last_y - 1, y > 1]
     edges = jnp.concatenate([jnp.stack(flags).astype(f32), source_mask[:, 0].astype(f32)])
+    reaches = (IN_P, IN_U, IN_V, IN_W)
+    top = jnp.concatenate([state[0, i, :, own - reach :] for i, reach in enumerate(reaches)], axis=1)
+    bottom = jnp.concatenate([state[0, i, :, :reach] for i, reach in enumerate(reaches)], axis=1)
+    from_low = jnp.swapaxes(lax.ppermute(top, "slab", upward), 0, 1)
+    from_high = jnp.swapaxes(lax.ppermute(bottom, "slab", downward), 0, 1)
     raw = jnp.swapaxes(state[0], 1, 2)
-    reaches = (IN_P, IN_U, IN_V, IN_W)
-    from_low = lax.ppermute(
-        jnp.concatenate([raw[i, own - reach :] for i, reach in enumerate(reaches)]), "slab", upward
-    )
-    from_high = lax.ppermute(
-        jnp.concatenate([raw[i, :reach] for i, reach in enumerate(reaches)]), "slab", downward
-    )
     forms = (
         jax.ShapeDtypeStruct((len(LEFT), nx, 3 * nx), bf16),
         jax.ShapeDtypeStruct((len(RIGHT), 3 * nz, nz), bf16),
@@ -534,7 +554,8 @@
         compiler_params=pltpu.CompilerParams(vmem_limit_bytes=24 * 2**20),
         cost_estimate=pl.CostEstimate(flops=10**9, bytes_accessed=8 * 10**6, transcendentals=0),
     )(sums, *matrices)
-    held = call(held_kernel, shape(3, 5, nx, nz), planes, sums, left, right, flops=10**9)
+    held, later = call(
+        held_kernel, (shape(3, 5, nx, nz), shape(3, nx, nz)), planes, sums, left, right, flops=10**9)
     far = pl.pallas_call(
         far_kernel,
         out_shape=shape(3, nx, nz),
@@ -547,7 +568,7 @@
     )
     moved = lax.ppermute(source, "section", swap)
     driven = with_edges(driven_kernel, shape(12, nx, nz), waves, sums, source, moved, left, right)
-    last = with_edges(finish_kernel, shape(17, nx, nz), planes, driven, source, moved, left, right)
+    last = with_edges(finish_kernel, shape(17, nx, nz), later, driven, source, moved, left, right)
     done = with_edges(filter_kernel, shape(streams, SLOTS, xs, nz), last, left, right)
     back = lax.all_to_all(done, "stream", split_axis=0, concat_axis=0, tiled=True)
     border = OUT_P + OUT_U + OUT_V + OUT_W

time: 139 us -> 139 us (level)
  no operation moved by 1% of the time
where the time goes in v7:
time: 139 us; the launch traced here: 137 us
  blocking collectives  68 us (49%)
  waiting for transfers between devices  27.1 us (19%)
  Pallas kernels  25.5 us (18%)
  starting transfers between devices  10.7 us (8%)
  local copies, waits for them, and re-layouts  3.92 us (3%)
  between operations  1.72 us (1%)
    all_to_all x1, blocking collectives, shards(): lax.all_to_all(done, 'stream', split_axis=0, concat_axis=0, tiled=True)  38.2 us
    all_to_all x1, blocking collectives, shards(): lax.all_to_all(spread, 'stream', split_axis=0, concat_axis=0, tiled=True)  29.8 us
    pallas_call x7, Pallas kernels, with_edges(): pl.pallas_call(body, out_shape=out_shape, in_specs=[pl.BlockSpec(memory_s...  16.9 us
    ppermute x1, waiting for transfers between devices, shards(): from_low = lax.ppermute(high + sum(more_high), 'slab', upward)  8.58 us
    pallas_call x3, Pallas kernels, call(): pl.pallas_call(body, out_shape=out_shape, scratch_shapes=scratch, compile...  6.21 us
    ppermute x2, waiting for transfers between devices, shards(): lax.ppermute(carried, AXES, along_y(steps))  5.24 us
    ppermute x2, starting transfers between devices, shards(): lax.ppermute(carried, AXES, along_y(steps))  4.51 us
    ppermute x1, waiting for transfers between devices, shards(): from_high = jnp.swapaxes(lax.ppermute(bottom, 'slab', downward), 0, 1)  3.51 us
  transfers between devices with their start and end apart: 10, of which 9 were waited for; matrix products, arithmetic and copies ran while one was open for 1% of the time, Pallas kernels for 5%

profile of v7, /device:TPU:96, one launch (start us, length us, event | category | flops | bytes accessed | tf_op | source)
XLA Modules:
  0.0 137.4 jit_solution(6651453941194674793)
XLA Ops:
  0.0 1.3 copy.22
  1.4 3.2 %collective-permute-start = (f32[16,34,128]{2,0,1:T(8,128)S(1)}, f32[16,34,128]{2,0,1:T(8,128)S(1)}, u32[]{:S(2)}, u32[]{:S(2)}) collective-permute-start(f32[16,34,128]{2,0,1:T(8,128)S(1)} %pad_maximum_fusion), channel_id=1, source_target_pairs={{0,1},{1,2},{2,3},{3,4},{4,5},{5,6},{6,7},{7,0},{8,9},{9,10},{10,1... | collective-permute-start | bytes 835592 | tf_op jit(solution)/shard_map/ppermute | solution.py:519
  6.5 1.9 %shard_map.73 = (bf16[10,256,768]{2,1,0:T(8,128)(2,1)S(1)}, bf16[3,384,128]{2,1,0:T(8,128)(2,1)S(1)}) custom-call(f32[256,256]{1,0:T(8,128)S(1)} %copy-done, f32[128,128]{1,0:T(8,128)S(1)} %bitcast.62, f32[256,256]{1,0:T(8,128)S(1)} %copy-done.1, f32[128,128]{1,0:T(8,128)S(1)} %bitcast.64), custom_call_target="tpu_custom_call" | custom-call | flops 1000000000 | bytes 655360 | tf_op jit(solution)/shard_map/pallas_call | solution.py:24
  8.4 2.1 %collective-permute-done = f32[16,34,128]{2,0,1:T(8,128)S(1)} collective-permute-done((f32[16,34,128]{2,0,1:T(8,128)S(1)}, f32[16,34,128]{2,0,1:T(8,128)S(1)}, u32[]{:S(2)}, u32[]{:S(2)}) %collective-permute-start) | collective-permute-done | bytes 278560 | tf_op jit(solution)/shard_map/ppermute | solution.py:519
  10.5 3.5 %collective-permute-done.1 = f32[16,34,128]{2,0,1:T(8,128)S(1)} collective-permute-done((f32[16,34,128]{2,0,1:T(8,128)S(1)}, f32[16,34,128]{2,0,1:T(8,128)S(1)}, u32[]{:S(2)}, u32[]{:S(2)}) %collective-permute-start.1) | collective-permute-done | bytes 278560 | tf_op jit(solution)/shard_map/ppermute | solution.py:520
  14.0 1.3 shard_map.74
  15.3 29.8 %all_to_all.10.in_ref = f32[16,13,16,128]{3,2,1,0:T(8,128)S(1)} all-to-all(f32[16,13,16,128]{3,2,1,0:T(8,128)S(1)} %shard_map.74), channel_id=1, replica_groups=mesh['section'=2,'stream'=16,'slab'=8] {'stream'}, dimensions={0} | all-to-all | bytes 3407872 | tf_op jit(solution)/shard_map/all_to_all | solution.py:542
  45.0 2.6 %shard_map.75 = (f32[2,256,128]{2,1,0:T(8,128)S(1)}, f32[3,256,128]{2,1,0:T(8,128)S(1)}) custom-call(f32[16,13,16,128]{3,2,1,0:T(8,128)S(1)} %all_to_all.10.in_ref, bf16[10,256,768]{2,1,0:T(8,128)(2,1)S(1)} %get-tuple-element.17.left_ref, bf16[3,384,128]{2,1,0:T(8,128)(2,1)S(1)} %get-tuple-element.16.right_ref), custom_call_target="tpu_custom_call" | custom-call | flops 2000000000 | bytes 5931008 | tf_op jit(solution)/shard_map/pallas_call | solution.py:24
  50.1 3.9 %collective-permute-start.3 = (f32[3,256,128]{2,1,0:T(8,128)S(1)}, f32[3,256,128]{2,1,0:T(8,128)S(1)}, u32[]{:S(2)}, u32[]{:S(2)}) collective-permute-start(f32[3,256,128]{2,1,0:T(8,128)S(1)} %broadcast_select_fusion), channel_id=1, source_target_pairs={{0,71},{32,0},{8,32},{40,8},{16,40},{48,16},{24,48},{56,24},{120,5... | collective-permute-start | bytes 1179656 | tf_op jit(solution)/shard_map/ppermute | solution.py:548
  54.1 1.9 %shard_map.76 = (bf16[10,256,768]{2,1,0:T(8,128)(2,1)S(1)}, bf16[3,384,128]{2,1,0:T(8,128)(2,1)S(1)}) custom-call(f32[3,256,128]{2,1,0:T(8,128)S(1)} %get-tuple-element.18.after_ref.sums_ref, f32[256,256]{1,0:T(8,128)S(1)} %copy-done, f32[128,128]{1,0:T(8,128)S(1)} %bitcast.63, f32[256,256]{1,0:T(8,128)S(1)} %copy-done.1, f32[128,128]{1,0:T(8,128)S(1)} %bitcast.65), custom_call_target="tpu_custom_call" | custom-call | flops 1000000000 | bytes 8000000 | tf_op jit(solution)/shard_map/pallas_call | solution.py:550
  55.9 1.7 %shard_map.77 = (f32[3,5,256,128]{3,2,1,0:T(8,128)S(1)}, f32[3,256,128]{2,1,0:T(8,128)S(1)}) custom-call(f32[16,13,16,128]{3,2,1,0:T(8,128)S(1)} %all_to_all.10.in_ref, f32[3,256,128]{2,1,0:T(8,128)S(1)} %get-tuple-element.18.after_ref.sums_ref, bf16[10,256,768]{2,1,0:T(8,128)(2,1)S(1)} %get-tuple-element.19.left_ref, ...), custom_call_target="tpu_custom_call" | custom-call | flops 1000000000 | bytes 6324224 | tf_op jit(solution)/shard_map/pallas_call | solution.py:24
  57.6 5.2 %collective-permute-done.4.down_ref = f32[3,256,128]{2,1,0:T(8,128)S(1)} collective-permute-done((f32[3,256,128]{2,1,0:T(8,128)S(1)}, f32[3,256,128]{2,1,0:T(8,128)S(1)}, u32[]{:S(2)}, u32[]{:S(2)}) %collective-permute-start.4) | collective-permute-done | bytes 393248 | tf_op jit(solution)/shard_map/ppermute | solution.py:548
  63.6 1.7 %collective-permute-done.5.far_ref = f32[3,256,128]{2,1,0:T(8,128)S(1)} collective-permute-done((f32[3,256,128]{2,1,0:T(8,128)S(1)}, f32[3,256,128]{2,1,0:T(8,128)S(1)}, u32[]{:S(2)}, u32[]{:S(2)}) %collective-permute-start.5) | collective-permute-done | bytes 393248 | tf_op jit(solution)/shard_map/ppermute | solution.py:565
  65.3 1.7 %shard_map.79.own_ref = f32[4,3,256,128]{3,2,1,0:T(8,128)S(1)} custom-call(f32[23]{0:T(128)S(1)} %pad_maximum_fusion.2.edge_ref.flag_ref, f32[16,13,16,128]{3,2,1,0:T(8,128)S(1)} %all_to_all.10.in_ref, f32[3,5,256,128]{3,2,1,0:T(8,128)S(1)} %get-tuple-element.23.after_ref.held_ref, f32[3,256,128]{2,1,0:T(8,128)S(1)} %collective-permute-done.3.up_ref, ...), custom_call_target="tpu_custom_call" | custom-call | tf_op jit(solution)/shard_map/pallas_call | solution.py:533
  67.2 3.3 %collective-permute-done.6.source_ref = f32[4,3,256,128]{3,2,1,0:T(8,128)S(1)} collective-permute-done((f32[4,3,256,128]{3,2,1,0:T(8,128)S(1)}, f32[4,3,256,128]{3,2,1,0:T(8,128)S(1)}, u32[]{:S(2)}, u32[]{:S(2)}) %collective-permute-start.6) | collective-permute-done | bytes 1572896 | tf_op jit(solution)/shard_map/ppermute | solution.py:569
  70.5 2.7 %shard_map.80.driven_ref = f32[12,256,128]{2,1,0:T(8,128)S(1)} custom-call(f32[23]{0:T(128)S(1)} %pad_maximum_fusion.2.edge_ref.flag_ref, f32[2,256,128]{2,1,0:T(8,128)S(1)} %get-tuple-element.22.waves_ref, f32[3,256,128]{2,1,0:T(8,128)S(1)} %get-tuple-element.18.after_ref.sums_ref, f32[4,3,256,128]{3,2,1,0:T(8,128)S(1)} %shard_map.79.own_ref, ...), custom_call_target="tpu_custom_call" | custom-call | tf_op jit(solution)/shard_map/pallas_call | solution.py:533
  73.2 5.2 %shard_map.81.last_ref = f32[17,256,128]{2,1,0:T(8,128)S(1)} custom-call(f32[23]{0:T(128)S(1)} %pad_maximum_fusion.2.edge_ref.flag_ref, f32[3,256,128]{2,1,0:T(8,128)S(1)} %get-tuple-element.21.later_ref, f32[12,256,128]{2,1,0:T(8,128)S(1)} %shard_map.80.driven_ref, f32[4,3,256,128]{3,2,1,0:T(8,128)S(1)} %shard_map.79.own_ref, ...), custom_call_target="tpu_custom_call" | custom-call | tf_op jit(solution)/shard_map/pallas_call | solution.py:533
  78.4 3.4 %shard_map.82 = f32[16,19,16,128]{3,2,1,0:T(8,128)S(1)} custom-call(f32[23]{0:T(128)S(1)} %pad_maximum_fusion.2.edge_ref.flag_ref, f32[17,256,128]{2,1,0:T(8,128)S(1)} %shard_map.81.last_ref, bf16[10,256,768]{2,1,0:T(8,128)(2,1)S(1)} %get-tuple-element.19.left_ref, bf16[3,384,128]{2,1,0:T(8,128)(2,1)S(1)} %get-tuple-element.20.right_ref), custom_call_target="tpu_custom_call" | custom-call | tf_op jit(solution)/shard_map/pallas_call | solution.py:533
  81.9 38.2 %all_to_all.11.back_ref = f32[16,19,16,128]{3,2,1,0:T(8,128)S(1)} all-to-all(f32[16,19,16,128]{3,2,1,0:T(8,128)S(1)} %shard_map.82), channel_id=1, replica_groups=mesh['section'=2,'stream'=16,'slab'=8] {'stream'}, dimensions={0} | all-to-all | bytes 4980736 | tf_op jit(solution)/shard_map/all_to_all | solution.py:573
  120.1 1.1 shard_map.84
  121.5 1.5 %shard_map.83 = (f32[4,16,16,128]{3,2,1,0:T(8,128)S(1)}, f32[46,16,128]{2,1,0:T(8,128)S(1)}, f32[46,16,128]{2,1,0:T(8,128)S(1)}) custom-call(f32[23]{0:T(128)S(1)} %pad_maximum_fusion.2.edge_ref.flag_ref, f32[16,19,16,128]{3,2,1,0:T(8,128)S(1)} %all_to_all.11.back_ref), custom_call_target="tpu_custom_call" | custom-call | tf_op jit(solution)/shard_map/pallas_call | solution.py:533
  124.2 2.1 %collective-permute-start.9 = (f32[46,16,128]{2,1,0:T(8,128)S(1)}, f32[46,16,128]{2,1,0:T(8,128)S(1)}, u32[]{:S(2)}, u32[]{:S(2)}) collective-permute-start(f32[46,16,128]{2,1,0:T(8,128)S(1)} %fusion.2), channel_id=1, source_target_pairs={{1,0},{2,1},{3,2},{4,3},{5,4},{6,5},{7,6},{0,7},{9,8},{10,9},{11,1... | collective-permute-start | bytes 1130504 | tf_op jit(solution)/shard_map/ppermute | solution.py:593
  126.3 8.6 %collective-permute-done.8 = f32[46,16,128]{2,1,0:T(8,128)S(1)} collective-permute-done((f32[46,16,128]{2,1,0:T(8,128)S(1)}, f32[46,16,128]{2,1,0:T(8,128)S(1)}, u32[]{:S(2)}, u32[]{:S(2)}) %collective-permute-start.8) | collective-permute-done | bytes 376864 | tf_op jit(solution)/shard_map/ppermute | solution.py:592
  134.9 1.4 %collective-permute-done.9 = f32[46,16,128]{2,1,0:T(8,128)S(1)} collective-permute-done((f32[46,16,128]{2,1,0:T(8,128)S(1)}, f32[46,16,128]{2,1,0:T(8,128)S(1)}, u32[]{:S(2)}, u32[]{:S(2)}) %collective-permute-start.9) | collective-permute-done | bytes 376864 | tf_op jit(solution)/shard_map/ppermute | solution.py:593
  (53 shorter events, 6.5 us)
Async XLA Ops:
  0.0 4.7 %copy-start.7 = (s32[16]{0:T(128)S(1)}, s32[16]{0:T(128)}, u32[]{:S(2)}) copy-start(s32[16]{0:T(128)} %constant.37.clone) | copy-start | bytes 196
  0.0 6.2 %copy-start.2 = (f32[128,128]{1,0:T(8,128)S(1)}, f32[128,128]{1,0:T(8,128)}, u32[]{:S(2)}) copy-start(f32[128,128]{1,0:T(8,128)} %param.10) | copy-start | bytes 196612
  0.0 6.3 %copy-start.3 = (f32[128,128]{1,0:T(8,128)S(1)}, f32[128,128]{1,0:T(8,128)}, u32[]{:S(2)}) copy-start(f32[128,128]{1,0:T(8,128)} %param.12) | copy-start | bytes 196612
  0.0 6.4 %copy-start.1 = (f32[256,256]{1,0:T(8,128)S(1)}, f32[256,256]{1,0:T(8,128)}, u32[]{:S(2)}) copy-start(f32[256,256]{1,0:T(8,128)} %refs_2_.1) | copy-start | bytes 786436
  0.0 6.4 %copy-start = (f32[256,256]{1,0:T(8,128)S(1)}, f32[256,256]{1,0:T(8,128)}, u32[]{:S(2)}) copy-start(f32[256,256]{1,0:T(8,128)} %refs_0_.1) | copy-start | bytes 786436
  1.4 9.1 %collective-permute-start = (f32[16,34,128]{2,0,1:T(8,128)S(1)}, f32[16,34,128]{2,0,1:T(8,128)S(1)}, u32[]{:S(2)}, u32[]{:S(2)}) collective-permute-start(f32[16,34,128]{2,0,1:T(8,128)S(1)} %pad_maximum_fusion), channel_id=1, source_target_pairs={{0,1},{1,2},{2,3},{3,4},{4,5},{5,6},{6,7},{7,0},{8,9},{9,10},{10,1... | collective-permute-start | bytes 835592 | tf_op jit(solution)/shard_map/ppermute | solution.py:519
  4.6 9.4 %collective-permute-start.1 = (f32[16,34,128]{2,0,1:T(8,128)S(1)}, f32[16,34,128]{2,0,1:T(8,128)S(1)}, u32[]{:S(2)}, u32[]{:S(2)}) collective-permute-start(f32[16,34,128]{2,0,1:T(8,128)S(1)} %pad_maximum_fusion.1), channel_id=1, source_target_pairs={{1,0},{2,1},{3,2},{4,3},{5,4},{6,5},{7,6},{0,7},{9,8},{10,9},{11,1... | collective-permute-start | bytes 835592 | tf_op jit(solution)/shard_map/ppermute | solution.py:520
  6.2 2.1 %copy-start.6 = (s32[16,1]{0,1:T(1,128)S(1)}, s32[16,1]{0,1:T(1,128)}, u32[]{:S(2)}) copy-start(s32[16,1]{0,1:T(1,128)} %param.8) | copy-start | bytes 196
  47.7 1.8 %collective-permute-start.2 = (f32[3,256,128]{2,1,0:T(8,128)S(1)}, f32[3,256,128]{2,1,0:T(8,128)S(1)}, u32[]{:S(2)}, u32[]{:S(2)}) collective-permute-start(f32[3,256,128]{2,1,0:T(8,128)S(1)} %get-tuple-element.18.after_ref.sums_ref), channel_id=1, source_target_pairs={{0,128},{128,0},{1,129},{129,1},{2,130},{130,2},{3,131},{131,3},{4... | collective-permute-start | bytes 1179656 | tf_op jit(solution)/shard_map/ppermute | solution.py:546
  49.5 13.3 %collective-permute-start.4 = (f32[3,256,128]{2,1,0:T(8,128)S(1)}, f32[3,256,128]{2,1,0:T(8,128)S(1)}, u32[]{:S(2)}, u32[]{:S(2)}) collective-permute-start(f32[3,256,128]{2,1,0:T(8,128)S(1)} %broadcast_select_fusion), channel_id=1, source_target_pairs={{0,32},{32,8},{8,40},{40,16},{16,48},{48,24},{24,56},{56,120},{120... | collective-permute-start | bytes 1179656 | tf_op jit(solution)/shard_map/ppermute | solution.py:548
  50.1 12.8 %collective-permute-start.3 = (f32[3,256,128]{2,1,0:T(8,128)S(1)}, f32[3,256,128]{2,1,0:T(8,128)S(1)}, u32[]{:S(2)}, u32[]{:S(2)}) collective-permute-start(f32[3,256,128]{2,1,0:T(8,128)S(1)} %broadcast_select_fusion), channel_id=1, source_target_pairs={{0,71},{32,0},{8,32},{40,8},{16,40},{48,16},{24,48},{56,24},{120,5... | collective-permute-start | bytes 1179656 | tf_op jit(solution)/shard_map/ppermute | solution.py:548
  63.5 1.8 %collective-permute-start.5 = (f32[3,256,128]{2,1,0:T(8,128)S(1)}, f32[3,256,128]{2,1,0:T(8,128)S(1)}, u32[]{:S(2)}, u32[]{:S(2)}) collective-permute-start(f32[3,256,128]{2,1,0:T(8,128)S(1)} %shard_map.78), channel_id=1, source_target_pairs={{0,128},{128,0},{1,129},{129,1},{2,130},{130,2},{3,131},{131,3},{4... | collective-permute-start | bytes 1179656 | tf_op jit(solution)/shard_map/ppermute | solution.py:565
  67.0 3.5 %collective-permute-start.6 = (f32[4,3,256,128]{3,2,1,0:T(8,128)S(1)}, f32[4,3,256,128]{3,2,1,0:T(8,128)S(1)}, u32[]{:S(2)}, u32[]{:S(2)}) collective-permute-start(f32[4,3,256,128]{3,2,1,0:T(8,128)S(1)} %shard_map.79.own_ref), channel_id=1, source_target_pairs={{0,128},{128,0},{1,129},{129,1},{2,130},{130,2},{3,131},{131,3},{4... | collective-permute-start | bytes 4718600 | tf_op jit(solution)/shard_map/ppermute | solution.py:569
  121.2 2.8 %copy-start.5 = (pred[46]{0:T(512)(128)(4,1)S(1)}, pred[46]{0:T(512)(128)(4,1)}, u32[]{:S(2)}) copy-start(pred[46]{0:T(512)(128)(4,1)} %constant.36.clone.1) | copy-start | bytes 142
  121.2 2.6 %collective-permute-start.7 = (f32[100,16,128]{2,1,0:T(8,128)S(1)}, f32[100,16,128]{2,1,0:T(8,128)S(1)}, u32[]{:S(2)}, u32[]{:S(2)}) collective-permute-start(f32[100,16,128]{2,1,0:T(8,128)S(1)} %shard_map.84), channel_id=1, source_target_pairs={{0,128},{128,0},{1,129},{129,1},{2,130},{130,2},{3,131},{131,3},{4... | collective-permute-start | bytes 2457608 | tf_op jit(solution)/shard_map/ppermute | solution.py:577
  123.9 12.5 %copy-start.4 = (pred[16]{0:T(512)(128)(4,1)S(1)}, pred[16]{0:T(512)(128)(4,1)}, u32[]{:S(2)}) copy-start(pred[16]{0:T(512)(128)(4,1)} %constant.34.clone.1) | copy-start | bytes 52
  124.0 10.9 %collective-permute-start.8 = (f32[46,16,128]{2,1,0:T(8,128)S(1)}, f32[46,16,128]{2,1,0:T(8,128)S(1)}, u32[]{:S(2)}, u32[]{:S(2)}) collective-permute-start(f32[46,16,128]{2,1,0:T(8,128)S(1)} %add_add_fusion), channel_id=1, source_target_pairs={{0,1},{1,2},{2,3},{3,4},{4,5},{5,6},{6,7},{7,0},{8,9},{9,10},{10,1... | collective-permute-start | bytes 1130504 | tf_op jit(solution)/shard_map/ppermute | solution.py:592
  124.2 12.1 %collective-permute-start.9 = (f32[46,16,128]{2,1,0:T(8,128)S(1)}, f32[46,16,128]{2,1,0:T(8,128)S(1)}, u32[]{:S(2)}, u32[]{:S(2)}) collective-permute-start(f32[46,16,128]{2,1,0:T(8,128)S(1)} %fusion.2), channel_id=1, source_target_pairs={{1,0},{2,1},{3,2},{4,3},{5,4},{6,5},{7,6},{0,7},{9,8},{10,9},{11,1... | collective-permute-start | bytes 1130504 | tf_op jit(solution)/shard_map/ppermute | solution.py:593

commit v8 on v7

--- a/solution.py
+++ b/solution.py
@@ -96,7 +96,7 @@
     prepare_kernel(*refs)
 
 
-def far_kernel(flag_ref, up_ref, down_ref, after_ref, out_ref):
+def far_kernel(flag_ref, up_ref, down_ref, after_ref, later_ref, out_ref):
     for n in range(out_ref.shape[0]):
         out_ref[n] = flag_ref[5] * up_ref[n] - flag_ref[6] * down_ref[n]
 
@@ -312,9 +312,8 @@
             out_ref[n, k] = start[k] + change[k]
 
 
-def source_kernel(flag_ref, in_ref, held_ref, up_ref, down_ref, far_ref, left_ref, right_ref, out_ref):
-    do = Products(left_ref, right_ref)
-    nx, nz = up_ref.shape[1:]
+def minus_lamb(flag_ref, u, w, slope_u, slope_w, v):
+    nx, nz = u.shape
     row = lax.broadcasted_iota(jnp.int32, (nx, nz), 0)
     lane = lax.broadcasted_iota(jnp.int32, (nx, nz), 1)
     blocks = flag_ref.shape[0] - 7
@@ -330,25 +329,34 @@
         behind = jnp.where(lane == 0, 0.0, pltpu.roll(value, 1, 1))
         return 0.5 * (ahead - behind)
 
+    o_x = slope_w - slope_z(v)
+    o_y = slope_z(u) - slope_x(w)
+    o_z = slope_x(v) - slope_u
+    return region * (o_z * v - o_y * w), region * (o_x * w - o_z * u), region * (o_y * u - o_x * v)
+
+
+def first_source_kernel(flag_ref, in_ref, out_ref):
+    for k, value in enumerate(minus_lamb(flag_ref, *[plane(in_ref, i) for i in (3, 10, 11, 12, 9)])):
+        out_ref[k] = value
+
+
+def source_kernel(flag_ref, held_ref, up_ref, down_ref, far_ref, left_ref, right_ref, out_ref):
+    do = Products(left_ref, right_ref)
     near = [flag_ref[3] * up_ref[n] - flag_ref[4] * down_ref[n] for n in range(3)]
     half = [0.5 * value for value in near]
     pull_x = do.left("a", half)
     pull_z = do.right(half, "c")
-    for n in range(4):
-        if n == 0:
-            u, w, slope_u, slope_w, v = [plane(in_ref, i) for i in (3, 10, 11, 12, 9)]
-        else:
-            u, w = held_ref[n - 1, 0], held_ref[n - 1, 1]
-            slope_u = held_ref[n - 1, 2] - tau * pull_x[n - 1]
-            slope_w = held_ref[n - 1, 3] - tau * pull_z[n - 1]
-            far = far_ref[n - 1]
-            v = held_ref[n - 1, 4] - tau * ((2.0 / 3.0) * near[n - 1] - (1.0 / 12.0) * far)
-        o_x = slope_w - slope_z(v)
-        o_y = slope_z(u) - slope_x(w)
-        o_z = slope_x(v) - slope_u
-        out_ref[n, 0] = region * (o_z * v - o_y * w)
-        out_ref[n, 1] = region * (o_x * w - o_z * u)
-        out_ref[n, 2] = region * (o_y * u - o_x * v)
+    for n in range(3):
+        slope_u = held_ref[n, 2] - tau * pull_x[n]
+        slope_w = held_ref[n, 3] - tau * pull_z[n]
+        v = held_ref[n, 4] - tau * ((2.0 / 3.0) * near[n] - (1.0 / 12.0) * far_ref[n])
+        values = minus_lamb(flag_ref, held_ref[n, 0], held_ref[n, 1], slope_u, slope_w, v)
+        for k, value in enumerate(values):
+            out_ref[n, k] = value
+
+
+def source_at(refs, n, k):
+    return refs[0][k] if n == 0 else refs[1][n - 1, k]
 
 
 class Chain:
@@ -379,22 +387,22 @@
         return [out[k] + (sums[k] + kept[k]) if k < len(sums) else out[k] for k in range(len(now))]
 
 
-def drives(do, flag_ref, own_ref, source_ref, first, last):
+def drives(do, flag_ref, own, moved, first, last):
     flow = flag_ref[2] > 0
-    one = do.left("a", [source_ref[n, 0] for n in range(first, last)])
-    two = do.right([source_ref[n, 2] for n in range(first, last)], "c")
+    one = do.left("a", [source_at(moved, n, 0) for n in range(first, last)])
+    two = do.right([source_at(moved, n, 2) for n in range(first, last)], "c")
     return [
         (
             jnp.where(flow, 0.0, -(tau**2) * (one[n - first] + two[n - first])),
-            -(tau**2) * jnp.where(flow, own_ref[n, 1], source_ref[n, 1]),
+            -(tau**2) * jnp.where(flow, source_at(own, n, 1), source_at(moved, n, 1)),
         )
         for n in range(first, last)
     ]
 
 
-def driven_kernel(flag_ref, waves_ref, sums_ref, own_ref, source_ref, left_ref, right_ref, out_ref):
+def driven_kernel(flag_ref, waves_ref, sums_ref, own0_ref, own_ref, moved0_ref, moved_ref, left_ref, right_ref, out_ref):
     chain = Chain(left_ref, right_ref)
-    drive = drives(chain.do, flag_ref, own_ref, source_ref, 0, 2)
+    drive = drives(chain.do, flag_ref, (own0_ref, own_ref), (moved0_ref, moved_ref), 0, 2)
     q2 = list(drive[0])
     moved = chain.do.left("m1", q2)
     q3 = [2.0 * q2[k] + moved[k] + drive[0][k] for k in range(2)]
@@ -408,10 +416,10 @@
             out_ref[first + k] = values[k]
 
 
-def finish_kernel(flag_ref, later_ref, driven_ref, own_ref, source_ref, left_ref, right_ref, out_ref):
+def finish_kernel(flag_ref, later_ref, driven_ref, own_ref, moved0_ref, moved_ref, left_ref, right_ref, out_ref):
     chain = Chain(left_ref, right_ref)
     do = chain.do
-    drive = drives(do, flag_ref, own_ref, source_ref, 2, 4)
+    drive = drives(do, flag_ref, (None, own_ref), (moved0_ref, moved_ref), 2, 4)
     q4, q5, g6 = [[driven_ref[first + k] for k in range(4)] for first in (0, 4, 8)]
     q6, _ = chain.advance(q5, q4, drive[0], 6)
     q7, moved = chain.advance(q6, q5, drive[0], 6)
@@ -422,7 +430,7 @@
     flow = flag_ref[2] > 0
 
     def arrived(n):
-        return [jnp.where(flow, 0.0, source_ref[n, k]) for k in range(3)]
+        return [jnp.where(flow, 0.0, source_at((moved0_ref, moved_ref), n, k)) for k in range(3)]
 
     total = arrived(0)
     for n in (1, 2, 3):
@@ -543,6 +551,8 @@
     waves, sums = call(
         waves_kernel, (shape(2, nx, nz), shape(3, nx, nz)), planes, left, right, flops=2 * 10**9
     )
+    source0 = with_edges(first_source_kernel, shape(3, nx, nz), planes)
+    moved0 = lax.ppermute(source0, "section", swap)
     across = lax.ppermute(sums, "section", swap)
     carried = jnp.where(edges[2] > 0, sums, across)
     up, down = [lax.ppermute(carried, AXES, along_y(steps)) for steps in (-1, 1)]
@@ -559,16 +569,16 @@
     far = pl.pallas_call(
         far_kernel,
         out_shape=shape(3, nx, nz),
-        in_specs=[pl.BlockSpec(memory_space=pltpu.SMEM), vmem, vmem, anywhere],
+        in_specs=[pl.BlockSpec(memory_space=pltpu.SMEM), vmem, vmem, anywhere, anywhere],
         compiler_params=pltpu.CompilerParams(vmem_limit_bytes=8 * 2**20),
-    )(edges, up, down, held)
+    )(edges, up, down, held, moved0)
     far = lax.ppermute(far, "section", swap)
-    source = with_edges(
-        source_kernel, shape(4, 3, nx, nz), planes, held, up, down, far, left, right
+    source = with_edges(source_kernel, shape(3, 3, nx, nz), held, up, down, far, left, right)
+    moved = lax.ppermute(source, "section", swap)
+    driven = with_edges(
+        driven_kernel, shape(12, nx, nz), waves, sums, source0, source, moved0, moved, left, right
     )
-    moved = lax.ppermute(source, "section", swap)
-    driven = with_edges(driven_kernel, shape(12, nx, nz), waves, sums, source, moved, left, right)
-    last = with_edges(finish_kernel, shape(17, nx, nz), later, driven, source, moved, left, right)
+    last = with_edges(finish_kernel, shape(17, nx, nz), later, driven, source, moved0, moved, left, right)
     done = with_edges(filter_kernel, shape(streams, SLOTS, xs, nz), last, left, right)
     back = lax.all_to_all(done, "stream", split_axis=0, concat_axis=0, tiled=True)
     border = OUT_P + OUT_U + OUT_V + OUT_W

time: 139 us -> 139 us (level)
    pallas_call x7 -> x8, Pallas kernels: 16.9 us -> 17.5 us  [with_edges(): pl.pallas_call(body, out_shape=out_shape, in_specs=[pl.BlockSpec(memory_s...]
  transfers between devices with their start and end apart: 10 -> 11, of which waited for: 9 -> 8; matrix products, arithmetic and copies ran while one was open for 1% -> 1% of each run, Pallas kernels for 5% -> 6%
where the time goes in v8:
time: 139 us; the launch traced here: 137 us
  blocking collectives  68 us (49%)
  waiting for transfers between devices  26.2 us (19%)
  Pallas kernels  26.1 us (19%)
  starting transfers between devices  11.3 us (8%)
  local copies, waits for them, and re-layouts  3.83 us (3%)
  between operations  1.61 us (1%)
    all_to_all x1, blocking collectives, shards(): lax.all_to_all(done, 'stream', split_axis=0, concat_axis=0, tiled=True)  38.2 us
    all_to_all x1, blocking collectives, shards(): lax.all_to_all(spread, 'stream', split_axis=0, concat_axis=0, tiled=True)  29.8 us
    pallas_call x8, Pallas kernels, with_edges(): pl.pallas_call(body, out_shape=out_shape, in_specs=[pl.BlockSpec(memory_s...  17.5 us
    ppermute x1, waiting for transfers between devices, shards(): from_low = lax.ppermute(high + sum(more_high), 'slab', upward)  8.58 us
    pallas_call x3, Pallas kernels, call(): pl.pallas_call(body, out_shape=out_shape, scratch_shapes=scratch, compile...  6.15 us
    ppermute x2, waiting for transfers between devices, shards(): lax.ppermute(carried, AXES, along_y(steps))  5.14 us
    ppermute x2, starting transfers between devices, shards(): lax.ppermute(carried, AXES, along_y(steps))  4.51 us
    ppermute x1, waiting for transfers between devices, shards(): from_high = jnp.swapaxes(lax.ppermute(bottom, 'slab', downward), 0, 1)  3.51 us
  transfers between devices with their start and end apart: 11, of which 8 were waited for; matrix products, arithmetic and copies ran while one was open for 1% of the time, Pallas kernels for 6%

profile of v8, /device:TPU:96, one launch (start us, length us, event | category | flops | bytes accessed | tf_op | source)
XLA Modules:
  0.0 137.4 jit_solution(5559465239144908882)
XLA Ops:
  0.0 1.3 copy.22
  1.4 3.2 %collective-permute-start = (f32[16,34,128]{2,0,1:T(8,128)S(1)}, f32[16,34,128]{2,0,1:T(8,128)S(1)}, u32[]{:S(2)}, u32[]{:S(2)}) collective-permute-start(f32[16,34,128]{2,0,1:T(8,128)S(1)} %pad_maximum_fusion), channel_id=1, source_target_pairs={{0,1},{1,2},{2,3},{3,4},{4,5},{5,6},{6,7},{7,0},{8,9},{9,10},{10,1... | collective-permute-start | bytes 835592 | tf_op jit(solution)/shard_map/ppermute | solution.py:527
  6.2 1.9 %shard_map.73 = (bf16[10,256,768]{2,1,0:T(8,128)(2,1)S(1)}, bf16[3,384,128]{2,1,0:T(8,128)(2,1)S(1)}) custom-call(f32[256,256]{1,0:T(8,128)S(1)} %copy-done, f32[128,128]{1,0:T(8,128)S(1)} %bitcast.62, f32[256,256]{1,0:T(8,128)S(1)} %copy-done.1, f32[128,128]{1,0:T(8,128)S(1)} %bitcast.64), custom_call_target="tpu_custom_call" | custom-call | flops 1000000000 | bytes 655360 | tf_op jit(solution)/shard_map/pallas_call | solution.py:24
  8.2 2.3 %collective-permute-done = f32[16,34,128]{2,0,1:T(8,128)S(1)} collective-permute-done((f32[16,34,128]{2,0,1:T(8,128)S(1)}, f32[16,34,128]{2,0,1:T(8,128)S(1)}, u32[]{:S(2)}, u32[]{:S(2)}) %collective-permute-start) | collective-permute-done | bytes 278560 | tf_op jit(solution)/shard_map/ppermute | solution.py:527
  10.5 3.5 %collective-permute-done.1 = f32[16,34,128]{2,0,1:T(8,128)S(1)} collective-permute-done((f32[16,34,128]{2,0,1:T(8,128)S(1)}, f32[16,34,128]{2,0,1:T(8,128)S(1)}, u32[]{:S(2)}, u32[]{:S(2)}) %collective-permute-start.1) | collective-permute-done | bytes 278560 | tf_op jit(solution)/shard_map/ppermute | solution.py:528
  14.0 1.3 shard_map.74
  15.3 29.8 %all_to_all.10.in_ref = f32[16,13,16,128]{3,2,1,0:T(8,128)S(1)} all-to-all(f32[16,13,16,128]{3,2,1,0:T(8,128)S(1)} %shard_map.74), channel_id=1, replica_groups=mesh['section'=2,'stream'=16,'slab'=8] {'stream'}, dimensions={0} | all-to-all | bytes 3407872 | tf_op jit(solution)/shard_map/all_to_all | solution.py:550
  45.0 2.6 %shard_map.75 = (f32[2,256,128]{2,1,0:T(8,128)S(1)}, f32[3,256,128]{2,1,0:T(8,128)S(1)}) custom-call(f32[16,13,16,128]{3,2,1,0:T(8,128)S(1)} %all_to_all.10.in_ref, bf16[10,256,768]{2,1,0:T(8,128)(2,1)S(1)} %get-tuple-element.17.left_ref, bf16[3,384,128]{2,1,0:T(8,128)(2,1)S(1)} %get-tuple-element.16.right_ref), custom_call_target="tpu_custom_call" | custom-call | flops 2000000000 | bytes 5931008 | tf_op jit(solution)/shard_map/pallas_call | solution.py:24
  50.9 3.9 %collective-permute-start.3 = (f32[3,256,128]{2,1,0:T(8,128)S(1)}, f32[3,256,128]{2,1,0:T(8,128)S(1)}, u32[]{:S(2)}, u32[]{:S(2)}) collective-permute-start(f32[3,256,128]{2,1,0:T(8,128)S(1)} %broadcast_select_fusion), channel_id=1, source_target_pairs={{0,71},{32,0},{8,32},{40,8},{16,40},{48,16},{24,48},{56,24},{120,5... | collective-permute-start | bytes 1179656 | tf_op jit(solution)/shard_map/ppermute | solution.py:558
  54.9 1.9 %shard_map.76 = (bf16[10,256,768]{2,1,0:T(8,128)(2,1)S(1)}, bf16[3,384,128]{2,1,0:T(8,128)(2,1)S(1)}) custom-call(f32[3,256,128]{2,1,0:T(8,128)S(1)} %get-tuple-element.18.after_ref.sums_ref, f32[256,256]{1,0:T(8,128)S(1)} %copy-done, f32[128,128]{1,0:T(8,128)S(1)} %bitcast.63, f32[256,256]{1,0:T(8,128)S(1)} %copy-done.1, f32[128,128]{1,0:T(8,128)S(1)} %bitcast.65), custom_call_target="tpu_custom_call" | custom-call | flops 1000000000 | bytes 8000000 | tf_op jit(solution)/shard_map/pallas_call | solution.py:560
  56.8 1.7 %shard_map.77 = (f32[3,5,256,128]{3,2,1,0:T(8,128)S(1)}, f32[3,256,128]{2,1,0:T(8,128)S(1)}) custom-call(f32[16,13,16,128]{3,2,1,0:T(8,128)S(1)} %all_to_all.10.in_ref, f32[3,256,128]{2,1,0:T(8,128)S(1)} %get-tuple-element.18.after_ref.sums_ref, bf16[10,256,768]{2,1,0:T(8,128)(2,1)S(1)} %get-tuple-element.19.left_ref, ...), custom_call_target="tpu_custom_call" | custom-call | flops 1000000000 | bytes 6324224 | tf_op jit(solution)/shard_map/pallas_call | solution.py:24
  58.5 5.1 %collective-permute-done.4.down_ref = f32[3,256,128]{2,1,0:T(8,128)S(1)} collective-permute-done((f32[3,256,128]{2,1,0:T(8,128)S(1)}, f32[3,256,128]{2,1,0:T(8,128)S(1)}, u32[]{:S(2)}, u32[]{:S(2)}) %collective-permute-start.4) | collective-permute-done | bytes 393248 | tf_op jit(solution)/shard_map/ppermute | solution.py:558
  64.3 1.7 %collective-permute-done.6.far_ref = f32[3,256,128]{2,1,0:T(8,128)S(1)} collective-permute-done((f32[3,256,128]{2,1,0:T(8,128)S(1)}, f32[3,256,128]{2,1,0:T(8,128)S(1)}, u32[]{:S(2)}, u32[]{:S(2)}) %collective-permute-start.6) | collective-permute-done | bytes 393248 | tf_op jit(solution)/shard_map/ppermute | solution.py:575
  66.0 1.5 %shard_map.80.own_ref = f32[3,3,256,128]{3,2,1,0:T(8,128)S(1)} custom-call(f32[23]{0:T(128)S(1)} %pad_maximum_fusion.2.edge_ref.flag_ref, f32[3,5,256,128]{3,2,1,0:T(8,128)S(1)} %get-tuple-element.23.after_ref.held_ref, f32[3,256,128]{2,1,0:T(8,128)S(1)} %collective-permute-done.3.up_ref, f32[3,256,128]{2,1,0:T(8,128)S(1)} %collective-permute-done.4.down_ref, ...), custom_call_target="tpu_custom_call" | custom-call | tf_op jit(solution)/shard_map/pallas_call | solution.py:541
  67.8 2.7 %collective-permute-done.7.moved_ref = f32[3,3,256,128]{3,2,1,0:T(8,128)S(1)} collective-permute-done((f32[3,3,256,128]{3,2,1,0:T(8,128)S(1)}, f32[3,3,256,128]{3,2,1,0:T(8,128)S(1)}, u32[]{:S(2)}, u32[]{:S(2)}) %collective-permute-start.7) | collective-permute-done | bytes 1179680 | tf_op jit(solution)/shard_map/ppermute | solution.py:577
  70.5 2.7 %shard_map.81.driven_ref = f32[12,256,128]{2,1,0:T(8,128)S(1)} custom-call(f32[23]{0:T(128)S(1)} %pad_maximum_fusion.2.edge_ref.flag_ref, f32[2,256,128]{2,1,0:T(8,128)S(1)} %get-tuple-element.22.waves_ref, f32[3,256,128]{2,1,0:T(8,128)S(1)} %get-tuple-element.18.after_ref.sums_ref, f32[3,256,128]{2,1,0:T(8,128)S(1)} %shard_map.78.own0_ref, ...), custom_call_target="tpu_custom_call" | custom-call | tf_op jit(solution)/shard_map/pallas_call | solution.py:541
  73.2 5.2 %shard_map.82.last_ref = f32[17,256,128]{2,1,0:T(8,128)S(1)} custom-call(f32[23]{0:T(128)S(1)} %pad_maximum_fusion.2.edge_ref.flag_ref, f32[3,256,128]{2,1,0:T(8,128)S(1)} %get-tuple-element.21.later_ref, f32[12,256,128]{2,1,0:T(8,128)S(1)} %shard_map.81.driven_ref, f32[3,3,256,128]{3,2,1,0:T(8,128)S(1)} %shard_map.80.own_ref, ...), custom_call_target="tpu_custom_call" | custom-call | tf_op jit(solution)/shard_map/pallas_call | solution.py:541
  78.4 3.4 %shard_map.83 = f32[16,19,16,128]{3,2,1,0:T(8,128)S(1)} custom-call(f32[23]{0:T(128)S(1)} %pad_maximum_fusion.2.edge_ref.flag_ref, f32[17,256,128]{2,1,0:T(8,128)S(1)} %shard_map.82.last_ref, bf16[10,256,768]{2,1,0:T(8,128)(2,1)S(1)} %get-tuple-element.19.left_ref, bf16[3,384,128]{2,1,0:T(8,128)(2,1)S(1)} %get-tuple-element.20.right_ref), custom_call_target="tpu_custom_call" | custom-call | tf_op jit(solution)/shard_map/pallas_call | solution.py:541
  81.9 38.2 %all_to_all.11.back_ref = f32[16,19,16,128]{3,2,1,0:T(8,128)S(1)} all-to-all(f32[16,19,16,128]{3,2,1,0:T(8,128)S(1)} %shard_map.83), channel_id=1, replica_groups=mesh['section'=2,'stream'=16,'slab'=8] {'stream'}, dimensions={0} | all-to-all | bytes 4980736 | tf_op jit(solution)/shard_map/all_to_all | solution.py:583
  120.1 1.1 shard_map.85
  121.5 1.5 %shard_map.84 = (f32[4,16,16,128]{3,2,1,0:T(8,128)S(1)}, f32[46,16,128]{2,1,0:T(8,128)S(1)}, f32[46,16,128]{2,1,0:T(8,128)S(1)}) custom-call(f32[23]{0:T(128)S(1)} %pad_maximum_fusion.2.edge_ref.flag_ref, f32[16,19,16,128]{3,2,1,0:T(8,128)S(1)} %all_to_all.11.back_ref), custom_call_target="tpu_custom_call" | custom-call | tf_op jit(solution)/shard_map/pallas_call | solution.py:541
  124.2 2.1 %collective-permute-start.10 = (f32[46,16,128]{2,1,0:T(8,128)S(1)}, f32[46,16,128]{2,1,0:T(8,128)S(1)}, u32[]{:S(2)}, u32[]{:S(2)}) collective-permute-start(f32[46,16,128]{2,1,0:T(8,128)S(1)} %fusion.2), channel_id=1, source_target_pairs={{1,0},{2,1},{3,2},{4,3},{5,4},{6,5},{7,6},{0,7},{9,8},{10,9},{11,1... | collective-permute-start | bytes 1130504 | tf_op jit(solution)/shard_map/ppermute | solution.py:603
  126.3 8.6 %collective-permute-done.9 = f32[46,16,128]{2,1,0:T(8,128)S(1)} collective-permute-done((f32[46,16,128]{2,1,0:T(8,128)S(1)}, f32[46,16,128]{2,1,0:T(8,128)S(1)}, u32[]{:S(2)}, u32[]{:S(2)}) %collective-permute-start.9) | collective-permute-done | bytes 376864 | tf_op jit(solution)/shard_map/ppermute | solution.py:602
  134.9 1.4 %collective-permute-done.10 = f32[46,16,128]{2,1,0:T(8,128)S(1)} collective-permute-done((f32[46,16,128]{2,1,0:T(8,128)S(1)}, f32[46,16,128]{2,1,0:T(8,128)S(1)}, u32[]{:S(2)}, u32[]{:S(2)}) %collective-permute-start.10) | collective-permute-done | bytes 376864 | tf_op jit(solution)/shard_map/ppermute | solution.py:603
  (56 shorter events, 7.3 us)
Async XLA Ops:
  0.0 4.7 %copy-start.7 = (s32[16]{0:T(128)S(1)}, s32[16]{0:T(128)}, u32[]{:S(2)}) copy-start(s32[16]{0:T(128)} %constant.37.clone) | copy-start | bytes 196
  0.0 6.0 %copy-start.2 = (f32[128,128]{1,0:T(8,128)S(1)}, f32[128,128]{1,0:T(8,128)}, u32[]{:S(2)}) copy-start(f32[128,128]{1,0:T(8,128)} %param.10) | copy-start | bytes 196612
  0.0 6.1 %copy-start.3 = (f32[128,128]{1,0:T(8,128)S(1)}, f32[128,128]{1,0:T(8,128)}, u32[]{:S(2)}) copy-start(f32[128,128]{1,0:T(8,128)} %param.12) | copy-start | bytes 196612
  0.0 6.2 %copy-start.1 = (f32[256,256]{1,0:T(8,128)S(1)}, f32[256,256]{1,0:T(8,128)}, u32[]{:S(2)}) copy-start(f32[256,256]{1,0:T(8,128)} %refs_2_.1) | copy-start | bytes 786436
  0.0 6.2 %copy-start = (f32[256,256]{1,0:T(8,128)S(1)}, f32[256,256]{1,0:T(8,128)}, u32[]{:S(2)}) copy-start(f32[256,256]{1,0:T(8,128)} %refs_0_.1) | copy-start | bytes 786436
  1.4 9.1 %collective-permute-start = (f32[16,34,128]{2,0,1:T(8,128)S(1)}, f32[16,34,128]{2,0,1:T(8,128)S(1)}, u32[]{:S(2)}, u32[]{:S(2)}) collective-permute-start(f32[16,34,128]{2,0,1:T(8,128)S(1)} %pad_maximum_fusion), channel_id=1, source_target_pairs={{0,1},{1,2},{2,3},{3,4},{4,5},{5,6},{6,7},{7,0},{8,9},{9,10},{10,1... | collective-permute-start | bytes 835592 | tf_op jit(solution)/shard_map/ppermute | solution.py:527
  4.6 9.4 %collective-permute-start.1 = (f32[16,34,128]{2,0,1:T(8,128)S(1)}, f32[16,34,128]{2,0,1:T(8,128)S(1)}, u32[]{:S(2)}, u32[]{:S(2)}) collective-permute-start(f32[16,34,128]{2,0,1:T(8,128)S(1)} %pad_maximum_fusion.1), channel_id=1, source_target_pairs={{1,0},{2,1},{3,2},{4,3},{5,4},{6,5},{7,6},{0,7},{9,8},{10,9},{11,1... | collective-permute-start | bytes 835592 | tf_op jit(solution)/shard_map/ppermute | solution.py:528
  6.0 2.1 %copy-start.6 = (s32[16,1]{0,1:T(1,128)S(1)}, s32[16,1]{0,1:T(1,128)}, u32[]{:S(2)}) copy-start(s32[16,1]{0,1:T(1,128)} %param.8) | copy-start | bytes 196
  47.6 2.7 %collective-permute-start.2 = (f32[3,256,128]{2,1,0:T(8,128)S(1)}, f32[3,256,128]{2,1,0:T(8,128)S(1)}, u32[]{:S(2)}, u32[]{:S(2)}) collective-permute-start(f32[3,256,128]{2,1,0:T(8,128)S(1)} %get-tuple-element.18.after_ref.sums_ref), channel_id=1, source_target_pairs={{0,128},{128,0},{1,129},{129,1},{2,130},{130,2},{3,131},{131,3},{4... | collective-permute-start | bytes 1179656 | tf_op jit(solution)/shard_map/ppermute | solution.py:556
  49.7 8.7 %collective-permute-start.5 = (f32[3,256,128]{2,1,0:T(8,128)S(1)}, f32[3,256,128]{2,1,0:T(8,128)S(1)}, u32[]{:S(2)}, u32[]{:S(2)}) collective-permute-start(f32[3,256,128]{2,1,0:T(8,128)S(1)} %shard_map.78.own0_ref), channel_id=1, source_target_pairs={{0,128},{128,0},{1,129},{129,1},{2,130},{130,2},{3,131},{131,3},{4... | collective-permute-start | bytes 1179656 | tf_op jit(solution)/shard_map/ppermute | solution.py:555
  50.4 13.2 %collective-permute-start.4 = (f32[3,256,128]{2,1,0:T(8,128)S(1)}, f32[3,256,128]{2,1,0:T(8,128)S(1)}, u32[]{:S(2)}, u32[]{:S(2)}) collective-permute-start(f32[3,256,128]{2,1,0:T(8,128)S(1)} %broadcast_select_fusion), channel_id=1, source_target_pairs={{0,32},{32,8},{8,40},{40,16},{16,48},{48,24},{24,56},{56,120},{120... | collective-permute-start | bytes 1179656 | tf_op jit(solution)/shard_map/ppermute | solution.py:558
  50.9 12.7 %collective-permute-start.3 = (f32[3,256,128]{2,1,0:T(8,128)S(1)}, f32[3,256,128]{2,1,0:T(8,128)S(1)}, u32[]{:S(2)}, u32[]{:S(2)}) collective-permute-start(f32[3,256,128]{2,1,0:T(8,128)S(1)} %broadcast_select_fusion), channel_id=1, source_target_pairs={{0,71},{32,0},{8,32},{40,8},{16,40},{48,16},{24,48},{56,24},{120,5... | collective-permute-start | bytes 1179656 | tf_op jit(solution)/shard_map/ppermute | solution.py:558
  64.2 1.8 %collective-permute-start.6 = (f32[3,256,128]{2,1,0:T(8,128)S(1)}, f32[3,256,128]{2,1,0:T(8,128)S(1)}, u32[]{:S(2)}, u32[]{:S(2)}) collective-permute-start(f32[3,256,128]{2,1,0:T(8,128)S(1)} %shard_map.79), channel_id=1, source_target_pairs={{0,128},{128,0},{1,129},{129,1},{2,130},{130,2},{3,131},{131,3},{4... | collective-permute-start | bytes 1179656 | tf_op jit(solution)/shard_map/ppermute | solution.py:575
  67.6 2.9 %collective-permute-start.7 = (f32[3,3,256,128]{3,2,1,0:T(8,128)S(1)}, f32[3,3,256,128]{3,2,1,0:T(8,128)S(1)}, u32[]{:S(2)}, u32[]{:S(2)}) collective-permute-start(f32[3,3,256,128]{3,2,1,0:T(8,128)S(1)} %shard_map.80.own_ref), channel_id=1, source_target_pairs={{0,128},{128,0},{1,129},{129,1},{2,130},{130,2},{3,131},{131,3},{4... | collective-permute-start | bytes 3538952 | tf_op jit(solution)/shard_map/ppermute | solution.py:577
  121.2 2.8 %copy-start.5 = (pred[46]{0:T(512)(128)(4,1)S(1)}, pred[46]{0:T(512)(128)(4,1)}, u32[]{:S(2)}) copy-start(pred[46]{0:T(512)(128)(4,1)} %constant.36.clone.1) | copy-start | bytes 142
  121.2 2.6 %collective-permute-start.8 = (f32[100,16,128]{2,1,0:T(8,128)S(1)}, f32[100,16,128]{2,1,0:T(8,128)S(1)}, u32[]{:S(2)}, u32[]{:S(2)}) collective-permute-start(f32[100,16,128]{2,1,0:T(8,128)S(1)} %shard_map.85), channel_id=1, source_target_pairs={{0,128},{128,0},{1,129},{129,1},{2,130},{130,2},{3,131},{131,3},{4... | collective-permute-start | bytes 2457608 | tf_op jit(solution)/shard_map/ppermute | solution.py:587
  123.9 12.5 %copy-start.4 = (pred[16]{0:T(512)(128)(4,1)S(1)}, pred[16]{0:T(512)(128)(4,1)}, u32[]{:S(2)}) copy-start(pred[16]{0:T(512)(128)(4,1)} %constant.34.clone.1) | copy-start | bytes 52
  124.0 10.9 %collective-permute-start.9 = (f32[46,16,128]{2,1,0:T(8,128)S(1)}, f32[46,16,128]{2,1,0:T(8,128)S(1)}, u32[]{:S(2)}, u32[]{:S(2)}) collective-permute-start(f32[46,16,128]{2,1,0:T(8,128)S(1)} %add_add_fusion), channel_id=1, source_target_pairs={{0,1},{1,2},{2,3},{3,4},{4,5},{5,6},{6,7},{7,0},{8,9},{9,10},{10,1... | collective-permute-start | bytes 1130504 | tf_op jit(solution)/shard_map/ppermute | solution.py:602
  124.2 12.1 %collective-permute-start.10 = (f32[46,16,128]{2,1,0:T(8,128)S(1)}, f32[46,16,128]{2,1,0:T(8,128)S(1)}, u32[]{:S(2)}, u32[]{:S(2)}) collective-permute-start(f32[46,16,128]{2,1,0:T(8,128)S(1)} %fusion.2), channel_id=1, source_target_pairs={{1,0},{2,1},{3,2},{4,3},{5,4},{6,5},{7,6},{0,7},{9,8},{10,9},{11,1... | collective-permute-start | bytes 1130504 | tf_op jit(solution)/shard_map/ppermute | solution.py:603

commit v9 on v8

--- a/solution.py
+++ b/solution.py
@@ -335,7 +335,7 @@
     return region * (o_z * v - o_y * w), region * (o_x * w - o_z * u), region * (o_y * u - o_x * v)
 
 
-def first_source_kernel(flag_ref, in_ref, out_ref):
+def first_source_kernel(flag_ref, in_ref, after_ref, out_ref):
     for k, value in enumerate(minus_lamb(flag_ref, *[plane(in_ref, i) for i in (3, 10, 11, 12, 9)])):
         out_ref[k] = value
 
@@ -551,8 +551,6 @@
     waves, sums = call(
         waves_kernel, (shape(2, nx, nz), shape(3, nx, nz)), planes, left, right, flops=2 * 10**9
     )
-    source0 = with_edges(first_source_kernel, shape(3, nx, nz), planes)
-    moved0 = lax.ppermute(source0, "section", swap)
     across = lax.ppermute(sums, "section", swap)
     carried = jnp.where(edges[2] > 0, sums, across)
     up, down = [lax.ppermute(carried, AXES, along_y(steps)) for steps in (-1, 1)]
@@ -563,9 +561,16 @@
         in_specs=[anywhere] + [vmem] * 4,
         compiler_params=pltpu.CompilerParams(vmem_limit_bytes=24 * 2**20),
         cost_estimate=pl.CostEstimate(flops=10**9, bytes_accessed=8 * 10**6, transcendentals=0),
-    )(sums, *matrices)
+    )(across, *matrices)
     held, later = call(
         held_kernel, (shape(3, 5, nx, nz), shape(3, nx, nz)), planes, sums, left, right, flops=10**9)
+    source0 = pl.pallas_call(
+        first_source_kernel,
+        out_shape=shape(3, nx, nz),
+        in_specs=[pl.BlockSpec(memory_space=pltpu.SMEM), vmem, anywhere],
+        compiler_params=pltpu.CompilerParams(vmem_limit_bytes=24 * 2**20),
+    )(edges, planes, held)
+    moved0 = lax.ppermute(source0, "section", swap)
     far = pl.pallas_call(
         far_kernel,
         out_shape=shape(3, nx, nz),

time: 139 us -> 138 us (level)
    pallas_call x8 -> x7, Pallas kernels: 17.5 us -> 16.6 us  [with_edges(): pl.pallas_call(body, out_shape=out_shape, in_specs=[pl.BlockSpec(memory_s...]
  transfers between devices with their start and end apart: 11 -> 11, of which waited for: 8 -> 9; matrix products, arithmetic and copies ran while one was open for 1% -> 1% of each run, Pallas kernels for 6% -> 6%
where the time goes in v9:
time: 138 us; the launch traced here: 137 us
  blocking collectives  68 us (49%)
  Pallas kernels  26 us (19%)
  waiting for transfers between devices  25.9 us (19%)
  starting transfers between devices  11 us (8%)
  local copies, waits for them, and re-layouts  3.83 us (3%)
  between operations  1.61 us (1%)
    all_to_all x1, blocking collectives, shards(): lax.all_to_all(done, 'stream', split_axis=0, concat_axis=0, tiled=True)  38.3 us
    all_to_all x1, blocking collectives, shards(): lax.all_to_all(spread, 'stream', split_axis=0, concat_axis=0, tiled=True)  29.8 us
    pallas_call x7, Pallas kernels, with_edges(): pl.pallas_call(body, out_shape=out_shape, in_specs=[pl.BlockSpec(memory_s...  16.6 us
    ppermute x1, waiting for transfers between devices, shards(): from_low = lax.ppermute(high + sum(more_high), 'slab', upward)  8.58 us
    pallas_call x3, Pallas kernels, call(): pl.pallas_call(body, out_shape=out_shape, scratch_shapes=scratch, compile...  6.15 us
    ppermute x2, starting transfers between devices, shards(): lax.ppermute(carried, AXES, along_y(steps))  4.51 us
    ppermute x2, waiting for transfers between devices, shards(): lax.ppermute(carried, AXES, along_y(steps))  4.38 us
    ppermute x1, waiting for transfers between devices, shards(): from_high = jnp.swapaxes(lax.ppermute(bottom, 'slab', downward), 0, 1)  3.51 us
  transfers between devices with their start and end apart: 11, of which 9 were waited for; matrix products, arithmetic and copies ran while one was open for 1% of the time, Pallas kernels for 6%

profile of v9, /device:TPU:96, one launch (start us, length us, event | category | flops | bytes accessed | tf_op | source)
XLA Modules:
  0.0 136.8 jit_solution(2872980857421968695)
XLA Ops:
  0.0 1.3 copy.22
  1.4 3.2 %collective-permute-start = (f32[16,34,128]{2,0,1:T(8,128)S(1)}, f32[16,34,128]{2,0,1:T(8,128)S(1)}, u32[]{:S(2)}, u32[]{:S(2)}) collective-permute-start(f32[16,34,128]{2,0,1:T(8,128)S(1)} %pad_maximum_fusion), channel_id=1, source_target_pairs={{0,1},{1,2},{2,3},{3,4},{4,5},{5,6},{6,7},{7,0},{8,9},{9,10},{10,1... | collective-permute-start | bytes 835592 | tf_op jit(solution)/shard_map/ppermute | solution.py:527
  6.2 1.9 %shard_map.73 = (bf16[10,256,768]{2,1,0:T(8,128)(2,1)S(1)}, bf16[3,384,128]{2,1,0:T(8,128)(2,1)S(1)}) custom-call(f32[256,256]{1,0:T(8,128)S(1)} %copy-done, f32[128,128]{1,0:T(8,128)S(1)} %bitcast.62, f32[256,256]{1,0:T(8,128)S(1)} %copy-done.1, f32[128,128]{1,0:T(8,128)S(1)} %bitcast.64), custom_call_target="tpu_custom_call" | custom-call | flops 1000000000 | bytes 655360 | tf_op jit(solution)/shard_map/pallas_call | solution.py:24
  8.2 2.3 %collective-permute-done = f32[16,34,128]{2,0,1:T(8,128)S(1)} collective-permute-done((f32[16,34,128]{2,0,1:T(8,128)S(1)}, f32[16,34,128]{2,0,1:T(8,128)S(1)}, u32[]{:S(2)}, u32[]{:S(2)}) %collective-permute-start) | collective-permute-done | bytes 278560 | tf_op jit(solution)/shard_map/ppermute | solution.py:527
  10.5 3.5 %collective-permute-done.1 = f32[16,34,128]{2,0,1:T(8,128)S(1)} collective-permute-done((f32[16,34,128]{2,0,1:T(8,128)S(1)}, f32[16,34,128]{2,0,1:T(8,128)S(1)}, u32[]{:S(2)}, u32[]{:S(2)}) %collective-permute-start.1) | collective-permute-done | bytes 278560 | tf_op jit(solution)/shard_map/ppermute | solution.py:528
  14.0 1.3 shard_map.74
  15.3 29.8 %all_to_all.10.in_ref = f32[16,13,16,128]{3,2,1,0:T(8,128)S(1)} all-to-all(f32[16,13,16,128]{3,2,1,0:T(8,128)S(1)} %shard_map.74), channel_id=1, replica_groups=mesh['section'=2,'stream'=16,'slab'=8] {'stream'}, dimensions={0} | all-to-all | bytes 3407872 | tf_op jit(solution)/shard_map/all_to_all | solution.py:550
  45.0 2.6 %shard_map.75 = (f32[2,256,128]{2,1,0:T(8,128)S(1)}, f32[3,256,128]{2,1,0:T(8,128)S(1)}) custom-call(f32[16,13,16,128]{3,2,1,0:T(8,128)S(1)} %all_to_all.10.in_ref, bf16[10,256,768]{2,1,0:T(8,128)(2,1)S(1)} %get-tuple-element.17.left_ref, bf16[3,384,128]{2,1,0:T(8,128)(2,1)S(1)} %get-tuple-element.16.right_ref), custom_call_target="tpu_custom_call" | custom-call | flops 2000000000 | bytes 5931008 | tf_op jit(solution)/shard_map/pallas_call | solution.py:24
  50.1 3.9 %collective-permute-start.3 = (f32[3,256,128]{2,1,0:T(8,128)S(1)}, f32[3,256,128]{2,1,0:T(8,128)S(1)}, u32[]{:S(2)}, u32[]{:S(2)}) collective-permute-start(f32[3,256,128]{2,1,0:T(8,128)S(1)} %broadcast_select_fusion), channel_id=1, source_target_pairs={{0,71},{32,0},{8,32},{40,8},{16,40},{48,16},{24,48},{56,24},{120,5... | collective-permute-start | bytes 1179656 | tf_op jit(solution)/shard_map/ppermute | solution.py:556
  54.0 1.9 %shard_map.76 = (bf16[10,256,768]{2,1,0:T(8,128)(2,1)S(1)}, bf16[3,384,128]{2,1,0:T(8,128)(2,1)S(1)}) custom-call(f32[3,256,128]{2,1,0:T(8,128)S(1)} %collective-permute-done.2.after_ref, f32[256,256]{1,0:T(8,128)S(1)} %copy-done, f32[128,128]{1,0:T(8,128)S(1)} %bitcast.63, f32[256,256]{1,0:T(8,128)S(1)} %copy-done.1, f32[128,128]{1,0:T(8,128)S(1)} %bitcast.65), custom_call_target="tpu_custom_call" | custom-call | flops 1000000000 | bytes 8000000 | tf_op jit(solution)/shard_map/pallas_call | solution.py:558
  55.9 1.7 %shard_map.77 = (f32[3,5,256,128]{3,2,1,0:T(8,128)S(1)}, f32[3,256,128]{2,1,0:T(8,128)S(1)}) custom-call(f32[16,13,16,128]{3,2,1,0:T(8,128)S(1)} %all_to_all.10.in_ref, f32[3,256,128]{2,1,0:T(8,128)S(1)} %get-tuple-element.18.sums_ref, bf16[10,256,768]{2,1,0:T(8,128)(2,1)S(1)} %get-tuple-element.19.left_ref, bf16[3,384,128]{2,1,0:T(8,128)(2,1)S(1)} %get-tuple-element.20.right_ref), custom_call_target="tpu_custom_call" | custom-call | flops 1000000000 | bytes 6324224 | tf_op jit(solution)/shard_map/pallas_call | solution.py:24
  58.4 4.4 %collective-permute-done.4.down_ref = f32[3,256,128]{2,1,0:T(8,128)S(1)} collective-permute-done((f32[3,256,128]{2,1,0:T(8,128)S(1)}, f32[3,256,128]{2,1,0:T(8,128)S(1)}, u32[]{:S(2)}, u32[]{:S(2)}) %collective-permute-start.4) | collective-permute-done | bytes 393248 | tf_op jit(solution)/shard_map/ppermute | solution.py:556
  63.5 1.7 %collective-permute-done.6.far_ref = f32[3,256,128]{2,1,0:T(8,128)S(1)} collective-permute-done((f32[3,256,128]{2,1,0:T(8,128)S(1)}, f32[3,256,128]{2,1,0:T(8,128)S(1)}, u32[]{:S(2)}, u32[]{:S(2)}) %collective-permute-start.6) | collective-permute-done | bytes 393248 | tf_op jit(solution)/shard_map/ppermute | solution.py:580
  65.2 1.4 %shard_map.80.own_ref = f32[3,3,256,128]{3,2,1,0:T(8,128)S(1)} custom-call(f32[23]{0:T(128)S(1)} %pad_maximum_fusion.2.edge_ref.flag_ref, f32[3,5,256,128]{3,2,1,0:T(8,128)S(1)} %get-tuple-element.23.after_ref.held_ref, f32[3,256,128]{2,1,0:T(8,128)S(1)} %collective-permute-done.3.up_ref, f32[3,256,128]{2,1,0:T(8,128)S(1)} %collective-permute-done.4.down_ref, ...), custom_call_target="tpu_custom_call" | custom-call | tf_op jit(solution)/shard_map/pallas_call | solution.py:541
  67.1 2.7 %collective-permute-done.7.moved_ref = f32[3,3,256,128]{3,2,1,0:T(8,128)S(1)} collective-permute-done((f32[3,3,256,128]{3,2,1,0:T(8,128)S(1)}, f32[3,3,256,128]{3,2,1,0:T(8,128)S(1)}, u32[]{:S(2)}, u32[]{:S(2)}) %collective-permute-start.7) | collective-permute-done | bytes 1179680 | tf_op jit(solution)/shard_map/ppermute | solution.py:582
  69.9 2.7 %shard_map.81.driven_ref = f32[12,256,128]{2,1,0:T(8,128)S(1)} custom-call(f32[23]{0:T(128)S(1)} %pad_maximum_fusion.2.edge_ref.flag_ref, f32[2,256,128]{2,1,0:T(8,128)S(1)} %get-tuple-element.22.waves_ref, f32[3,256,128]{2,1,0:T(8,128)S(1)} %get-tuple-element.18.sums_ref, f32[3,256,128]{2,1,0:T(8,128)S(1)} %shard_map.78.own0_ref, ...), custom_call_target="tpu_custom_call" | custom-call | tf_op jit(solution)/shard_map/pallas_call | solution.py:541
  72.6 5.2 %shard_map.82.last_ref = f32[17,256,128]{2,1,0:T(8,128)S(1)} custom-call(f32[23]{0:T(128)S(1)} %pad_maximum_fusion.2.edge_ref.flag_ref, f32[3,256,128]{2,1,0:T(8,128)S(1)} %get-tuple-element.21.later_ref, f32[12,256,128]{2,1,0:T(8,128)S(1)} %shard_map.81.driven_ref, f32[3,3,256,128]{3,2,1,0:T(8,128)S(1)} %shard_map.80.own_ref, ...), custom_call_target="tpu_custom_call" | custom-call | tf_op jit(solution)/shard_map/pallas_call | solution.py:541
  77.8 3.4 %shard_map.83 = f32[16,19,16,128]{3,2,1,0:T(8,128)S(1)} custom-call(f32[23]{0:T(128)S(1)} %pad_maximum_fusion.2.edge_ref.flag_ref, f32[17,256,128]{2,1,0:T(8,128)S(1)} %shard_map.82.last_ref, bf16[10,256,768]{2,1,0:T(8,128)(2,1)S(1)} %get-tuple-element.19.left_ref, bf16[3,384,128]{2,1,0:T(8,128)(2,1)S(1)} %get-tuple-element.20.right_ref), custom_call_target="tpu_custom_call" | custom-call | tf_op jit(solution)/shard_map/pallas_call | solution.py:541
  81.2 38.3 %all_to_all.11.back_ref = f32[16,19,16,128]{3,2,1,0:T(8,128)S(1)} all-to-all(f32[16,19,16,128]{3,2,1,0:T(8,128)S(1)} %shard_map.83), channel_id=1, replica_groups=mesh['section'=2,'stream'=16,'slab'=8] {'stream'}, dimensions={0} | all-to-all | bytes 4980736 | tf_op jit(solution)/shard_map/all_to_all | solution.py:588
  119.4 1.1 shard_map.85
  120.9 1.5 %shard_map.84 = (f32[4,16,16,128]{3,2,1,0:T(8,128)S(1)}, f32[46,16,128]{2,1,0:T(8,128)S(1)}, f32[46,16,128]{2,1,0:T(8,128)S(1)}) custom-call(f32[23]{0:T(128)S(1)} %pad_maximum_fusion.2.edge_ref.flag_ref, f32[16,19,16,128]{3,2,1,0:T(8,128)S(1)} %all_to_all.11.back_ref), custom_call_target="tpu_custom_call" | custom-call | tf_op jit(solution)/shard_map/pallas_call | solution.py:541
  123.6 2.1 %collective-permute-start.10 = (f32[46,16,128]{2,1,0:T(8,128)S(1)}, f32[46,16,128]{2,1,0:T(8,128)S(1)}, u32[]{:S(2)}, u32[]{:S(2)}) collective-permute-start(f32[46,16,128]{2,1,0:T(8,128)S(1)} %fusion.2), channel_id=1, source_target_pairs={{1,0},{2,1},{3,2},{4,3},{5,4},{6,5},{7,6},{0,7},{9,8},{10,9},{11,1... | collective-permute-start | bytes 1130504 | tf_op jit(solution)/shard_map/ppermute | solution.py:608
  125.6 8.6 %collective-permute-done.9 = f32[46,16,128]{2,1,0:T(8,128)S(1)} collective-permute-done((f32[46,16,128]{2,1,0:T(8,128)S(1)}, f32[46,16,128]{2,1,0:T(8,128)S(1)}, u32[]{:S(2)}, u32[]{:S(2)}) %collective-permute-start.9) | collective-permute-done | bytes 376864 | tf_op jit(solution)/shard_map/ppermute | solution.py:607
  134.3 1.4 %collective-permute-done.10 = f32[46,16,128]{2,1,0:T(8,128)S(1)} collective-permute-done((f32[46,16,128]{2,1,0:T(8,128)S(1)}, f32[46,16,128]{2,1,0:T(8,128)S(1)}, u32[]{:S(2)}, u32[]{:S(2)}) %collective-permute-start.10) | collective-permute-done | bytes 376864 | tf_op jit(solution)/shard_map/ppermute | solution.py:608
  (56 shorter events, 7.5 us)
Async XLA Ops:
  0.0 4.7 %copy-start.7 = (s32[16]{0:T(128)S(1)}, s32[16]{0:T(128)}, u32[]{:S(2)}) copy-start(s32[16]{0:T(128)} %constant.37.clone) | copy-start | bytes 196
  0.0 6.0 %copy-start.2 = (f32[128,128]{1,0:T(8,128)S(1)}, f32[128,128]{1,0:T(8,128)}, u32[]{:S(2)}) copy-start(f32[128,128]{1,0:T(8,128)} %param.10) | copy-start | bytes 196612
  0.0 6.1 %copy-start.3 = (f32[128,128]{1,0:T(8,128)S(1)}, f32[128,128]{1,0:T(8,128)}, u32[]{:S(2)}) copy-start(f32[128,128]{1,0:T(8,128)} %param.12) | copy-start | bytes 196612
  0.0 6.2 %copy-start.1 = (f32[256,256]{1,0:T(8,128)S(1)}, f32[256,256]{1,0:T(8,128)}, u32[]{:S(2)}) copy-start(f32[256,256]{1,0:T(8,128)} %refs_2_.1) | copy-start | bytes 786436
  0.0 6.2 %copy-start = (f32[256,256]{1,0:T(8,128)S(1)}, f32[256,256]{1,0:T(8,128)}, u32[]{:S(2)}) copy-start(f32[256,256]{1,0:T(8,128)} %refs_0_.1) | copy-start | bytes 786436
  1.4 9.1 %collective-permute-start = (f32[16,34,128]{2,0,1:T(8,128)S(1)}, f32[16,34,128]{2,0,1:T(8,128)S(1)}, u32[]{:S(2)}, u32[]{:S(2)}) collective-permute-start(f32[16,34,128]{2,0,1:T(8,128)S(1)} %pad_maximum_fusion), channel_id=1, source_target_pairs={{0,1},{1,2},{2,3},{3,4},{4,5},{5,6},{6,7},{7,0},{8,9},{9,10},{10,1... | collective-permute-start | bytes 835592 | tf_op jit(solution)/shard_map/ppermute | solution.py:527
  4.6 9.4 %collective-permute-start.1 = (f32[16,34,128]{2,0,1:T(8,128)S(1)}, f32[16,34,128]{2,0,1:T(8,128)S(1)}, u32[]{:S(2)}, u32[]{:S(2)}) collective-permute-start(f32[16,34,128]{2,0,1:T(8,128)S(1)} %pad_maximum_fusion.1), channel_id=1, source_target_pairs={{1,0},{2,1},{3,2},{4,3},{5,4},{6,5},{7,6},{0,7},{9,8},{10,9},{11,1... | collective-permute-start | bytes 835592 | tf_op jit(solution)/shard_map/ppermute | solution.py:528
  6.0 2.1 %copy-start.6 = (s32[16,1]{0,1:T(1,128)S(1)}, s32[16,1]{0,1:T(1,128)}, u32[]{:S(2)}) copy-start(s32[16,1]{0,1:T(1,128)} %param.8) | copy-start | bytes 196
  47.6 1.8 %collective-permute-start.2 = (f32[3,256,128]{2,1,0:T(8,128)S(1)}, f32[3,256,128]{2,1,0:T(8,128)S(1)}, u32[]{:S(2)}, u32[]{:S(2)}) collective-permute-start(f32[3,256,128]{2,1,0:T(8,128)S(1)} %get-tuple-element.18.sums_ref), channel_id=1, source_target_pairs={{0,128},{128,0},{1,129},{129,1},{2,130},{130,2},{3,131},{131,3},{4... | collective-permute-start | bytes 1179656 | tf_op jit(solution)/shard_map/ppermute | solution.py:554
  49.5 13.3 %collective-permute-start.4 = (f32[3,256,128]{2,1,0:T(8,128)S(1)}, f32[3,256,128]{2,1,0:T(8,128)S(1)}, u32[]{:S(2)}, u32[]{:S(2)}) collective-permute-start(f32[3,256,128]{2,1,0:T(8,128)S(1)} %broadcast_select_fusion), channel_id=1, source_target_pairs={{0,32},{32,8},{8,40},{40,16},{16,48},{48,24},{24,56},{56,120},{120... | collective-permute-start | bytes 1179656 | tf_op jit(solution)/shard_map/ppermute | solution.py:556
  50.1 12.8 %collective-permute-start.3 = (f32[3,256,128]{2,1,0:T(8,128)S(1)}, f32[3,256,128]{2,1,0:T(8,128)S(1)}, u32[]{:S(2)}, u32[]{:S(2)}) collective-permute-start(f32[3,256,128]{2,1,0:T(8,128)S(1)} %broadcast_select_fusion), channel_id=1, source_target_pairs={{0,71},{32,0},{8,32},{40,8},{16,40},{48,16},{24,48},{56,24},{120,5... | collective-permute-start | bytes 1179656 | tf_op jit(solution)/shard_map/ppermute | solution.py:556
  58.3 4.5 %collective-permute-start.5 = (f32[3,256,128]{2,1,0:T(8,128)S(1)}, f32[3,256,128]{2,1,0:T(8,128)S(1)}, u32[]{:S(2)}, u32[]{:S(2)}) collective-permute-start(f32[3,256,128]{2,1,0:T(8,128)S(1)} %shard_map.78.own0_ref), channel_id=1, source_target_pairs={{0,128},{128,0},{1,129},{129,1},{2,130},{130,2},{3,131},{131,3},{4... | collective-permute-start | bytes 1179656 | tf_op jit(solution)/shard_map/ppermute | solution.py:573
  63.4 1.8 %collective-permute-start.6 = (f32[3,256,128]{2,1,0:T(8,128)S(1)}, f32[3,256,128]{2,1,0:T(8,128)S(1)}, u32[]{:S(2)}, u32[]{:S(2)}) collective-permute-start(f32[3,256,128]{2,1,0:T(8,128)S(1)} %shard_map.79), channel_id=1, source_target_pairs={{0,128},{128,0},{1,129},{129,1},{2,130},{130,2},{3,131},{131,3},{4... | collective-permute-start | bytes 1179656 | tf_op jit(solution)/shard_map/ppermute | solution.py:580
  66.7 3.2 %collective-permute-start.7 = (f32[3,3,256,128]{3,2,1,0:T(8,128)S(1)}, f32[3,3,256,128]{3,2,1,0:T(8,128)S(1)}, u32[]{:S(2)}, u32[]{:S(2)}) collective-permute-start(f32[3,3,256,128]{3,2,1,0:T(8,128)S(1)} %shard_map.80.own_ref), channel_id=1, source_target_pairs={{0,128},{128,0},{1,129},{129,1},{2,130},{130,2},{3,131},{131,3},{4... | collective-permute-start | bytes 3538952 | tf_op jit(solution)/shard_map/ppermute | solution.py:582
  120.6 2.9 %copy-start.5 = (pred[46]{0:T(512)(128)(4,1)S(1)}, pred[46]{0:T(512)(128)(4,1)}, u32[]{:S(2)}) copy-start(pred[46]{0:T(512)(128)(4,1)} %constant.36.clone.1) | copy-start | bytes 142
  120.6 2.7 %collective-permute-start.8 = (f32[100,16,128]{2,1,0:T(8,128)S(1)}, f32[100,16,128]{2,1,0:T(8,128)S(1)}, u32[]{:S(2)}, u32[]{:S(2)}) collective-permute-start(f32[100,16,128]{2,1,0:T(8,128)S(1)} %shard_map.85), channel_id=1, source_target_pairs={{0,128},{128,0},{1,129},{129,1},{2,130},{130,2},{3,131},{131,3},{4... | collective-permute-start | bytes 2457608 | tf_op jit(solution)/shard_map/ppermute | solution.py:592
  123.3 12.5 %copy-start.4 = (pred[16]{0:T(512)(128)(4,1)S(1)}, pred[16]{0:T(512)(128)(4,1)}, u32[]{:S(2)}) copy-start(pred[16]{0:T(512)(128)(4,1)} %constant.34.clone.1) | copy-start | bytes 52
  123.3 10.9 %collective-permute-start.9 = (f32[46,16,128]{2,1,0:T(8,128)S(1)}, f32[46,16,128]{2,1,0:T(8,128)S(1)}, u32[]{:S(2)}, u32[]{:S(2)}) collective-permute-start(f32[46,16,128]{2,1,0:T(8,128)S(1)} %add_add_fusion), channel_id=1, source_target_pairs={{0,1},{1,2},{2,3},{3,4},{4,5},{5,6},{6,7},{7,0},{8,9},{9,10},{10,1... | collective-permute-start | bytes 1130504 | tf_op jit(solution)/shard_map/ppermute | solution.py:607
  123.6 12.1 %collective-permute-start.10 = (f32[46,16,128]{2,1,0:T(8,128)S(1)}, f32[46,16,128]{2,1,0:T(8,128)S(1)}, u32[]{:S(2)}, u32[]{:S(2)}) collective-permute-start(f32[46,16,128]{2,1,0:T(8,128)S(1)} %fusion.2), channel_id=1, source_target_pairs={{1,0},{2,1},{3,2},{4,3},{5,4},{6,5},{7,6},{0,7},{9,8},{10,9},{11,1... | collective-permute-start | bytes 1130504 | tf_op jit(solution)/shard_map/ppermute | solution.py:608
